TPU v7x, 32 devices: a whole 2x2x4 slice. The times are simulated.
32 devices in a mesh: groups: 2 (over y), expert: 8 (over z, x), dp: 2 (over core).
Axes of the slice: x: 2, y: 2, z: 4, core: 2. Of those that a mesh axis runs over, the one named last changes fastest.
Arguments:
- tokens: bfloat16 [4096, 2048], P(('groups', 'expert', 'dp')), parts along dimension 0, may hold values from -6 to 6
- cotangent: bfloat16 [4096, 2048], P(('groups', 'expert', 'dp')), parts along dimension 0, may hold values from -6 to 6
- routes: int32 [4096, 4], P(('groups', 'expert', 'dp')), parts along dimension 0, may hold values from 0 to 15, as said below
- gates: float32 [4096, 4], P(('groups', 'expert', 'dp')), parts along dimension 0, may hold values from 0.05 to 0.6
- helper: int32 [32], P('groups'), parts along dimension 0, may hold values from 0 to 1
- w_gate: bfloat16 [16, 2048, 384], P(('expert', 'dp')), may hold values from -0.125 to 0.125
- w_up: bfloat16 [16, 2048, 384], P(('expert', 'dp')), may hold values from -0.125 to 0.125
- w_down: bfloat16 [16, 384, 2048], P(('expert', 'dp')), may hold values from -0.3125 to 0.3125
Outputs:
- grad_tokens: bfloat16 [4096, 2048], P(('groups', 'expert', 'dp')), parts along dimension 0
- grad_gate: bfloat16 [32, 2048, 384], P(('groups', 'expert', 'dp')), parts along dimension 0
- grad_up: bfloat16 [32, 2048, 384], P(('groups', 'expert', 'dp')), parts along dimension 0
- grad_down: bfloat16 [32, 384, 2048], P(('groups', 'expert', 'dp')), parts along dimension 0
There are 2 independent parts, one for each index of `groups`. A program takes and returns all parts, laid end to end along the dimension named above; an argument that names none is the same for every part. Nothing has to cross between parts.
Inputs may be any that keep to these rules, and one draw needn't show every extreme that they name: `routes`: each row names 4 different experts; the rows of one device name no expert more than 64 times, and some expert exactly 64 times in the rows of every device.
All inputs are finite; a program needn't handle non-finite values.
Results may differ from a plain program's by a relative error of at most 0.0065.
Values may be sent and summed in bfloat16 or wider, within the bound.
No kernel may reach another device: no remote copies, remote signals or barrier semaphores. Data moves between devices by JAX's collectives and lax.ppermute only.
A program may use at most 128 MiB of HBM per device.

v0:
```python
import jax
import jax.numpy as jnp
from jax import lax
from jax.sharding import PartitionSpec as P


def expert_pass(rows, scaled, gate_w, up_w, down_w):
    gate_pre = jnp.dot(rows, gate_w, preferred_element_type=jnp.float32)
    up_pre = jnp.dot(rows, up_w, preferred_element_type=jnp.float32)
    sigma = jax.nn.sigmoid(gate_pre)
    active = gate_pre * sigma
    hidden = (active * up_pre).astype(jnp.bfloat16)
    over_last = (((1,), (1,)), ((), ()))
    over_rows = (((0,), (0,)), ((), ()))
    back_hidden = lax.dot_general(scaled, down_w, over_last, preferred_element_type=jnp.float32)
    grad_gating = (back_hidden * up_pre * sigma * (1.0 + gate_pre * (1.0 - sigma))).astype(
        jnp.bfloat16
    )
    grad_upward = (back_hidden * active).astype(jnp.bfloat16)
    grad_down = lax.dot_general(hidden, scaled, over_rows, preferred_element_type=jnp.float32)
    grad_gate = lax.dot_general(rows, grad_gating, over_rows, preferred_element_type=jnp.float32)
    grad_up = lax.dot_general(rows, grad_upward, over_rows, preferred_element_type=jnp.float32)
    row_grads = lax.dot_general(grad_gating, gate_w, over_last, preferred_element_type=jnp.float32)
    row_grads = row_grads + lax.dot_general(
        grad_upward, up_w, over_last, preferred_element_type=jnp.float32
    )
    return (row_grads.astype(jnp.bfloat16), grad_gate, grad_up, grad_down)


def local(tokens, cotangent, routes, gates, helper, w_gate, w_up, w_down):
    tok_rows, width = tokens.shape
    top_count = routes.shape[1]
    devices = lax.axis_size(("expert", "dp"))
    route_cap = 2 * tok_rows * top_count // devices
    spill_cap = 3 * route_cap // 8
    home_cap = route_cap - spill_cap
    block_rows = tok_rows * top_count
    slots = devices * route_cap
    flat_ids = routes.reshape(block_rows)
    experts_row = jnp.arange(devices, dtype=jnp.int32)
    one_hot = (flat_ids[:, None] == experts_row[None, :]).astype(jnp.float32)
    positions = jnp.arange(block_rows, dtype=jnp.int32)
    lower = (positions[:, None] > positions[None, :]).astype(jnp.float32)
    before = jnp.dot(lower, one_hot, precision=lax.Precision.HIGHEST)
    route_rank = jnp.sum(before * one_hot, axis=1).astype(jnp.int32)
    partner_help = helper.reshape(devices // 2, 2)[:, ::-1].reshape(devices).astype(jnp.float32)
    helped = jnp.dot(one_hot, partner_help, precision=lax.Precision.HIGHEST) > 0.5
    spilled = route_rank >= home_cap
    kept = jnp.logical_not(spilled) | helped
    slot_index = jnp.where(kept, flat_ids * route_cap + route_rank, slots)
    source = jnp.full((slots + 1,), block_rows, jnp.int32).at[slot_index].set(positions)[:slots]
    token_of = jnp.where(source < block_rows, source // top_count, tok_rows)
    tokens_pad = jnp.concatenate([tokens, jnp.zeros((1, width), jnp.bfloat16)], axis=0)
    cot_pad = jnp.concatenate([cotangent, jnp.zeros((1, width), jnp.bfloat16)], axis=0)
    gate_pad = jnp.concatenate([gates.reshape(block_rows), jnp.zeros((1,), jnp.float32)], axis=0)
    send_rows = tokens_pad[token_of].reshape(devices, route_cap, width)
    send_scaled = (cot_pad[token_of].astype(jnp.float32) * gate_pad[source][:, None]).astype(
        jnp.bfloat16
    )
    send_scaled = send_scaled.reshape(devices, route_cap, width)
    recv_rows, recv_scaled = (
        lax.all_to_all(send_rows, ("expert", "dp"), split_axis=0, concat_axis=0, tiled=True),
        lax.all_to_all(send_scaled, ("expert", "dp"), split_axis=0, concat_axis=0, tiled=True),
    )
    gate_w = w_gate[0]
    up_w = w_up[0]
    down_w = w_down[0]
    whole_out = expert_pass(
        recv_rows.reshape(slots, width), recv_scaled.reshape(slots, width), gate_w, up_w, down_w
    )
    grad_gate = whole_out[1]
    grad_up = whole_out[2]
    grad_down = whole_out[3]
    row_grads = whole_out[0].reshape(devices, route_cap, width)
    back_rows = lax.all_to_all(row_grads, ("expert", "dp"), split_axis=0, concat_axis=0, tiled=True)
    back_pad = jnp.concatenate(
        [back_rows.reshape(slots, width), jnp.zeros((1, width), jnp.bfloat16)], axis=0
    )
    picked = back_pad[slot_index].reshape(tok_rows, top_count, width)
    grad_tokens = jnp.sum(picked.astype(jnp.float32), axis=1).astype(jnp.bfloat16)
    return (
        grad_tokens,
        grad_gate[None].astype(jnp.bfloat16),
        grad_up[None].astype(jnp.bfloat16),
        grad_down[None].astype(jnp.bfloat16),
    )


def solution(mesh):
    return jax.shard_map(
        local,
        mesh=mesh,
        in_specs=(
            P(("groups", "expert", "dp"), None),
            P(("groups", "expert", "dp"), None),
            P(("groups", "expert", "dp"), None),
            P(("groups", "expert", "dp"), None),
            P("groups"),
            P(("expert", "dp"), None, None),
            P(("expert", "dp"), None, None),
            P(("expert", "dp"), None, None),
        ),
        out_specs=(
            P(("groups", "expert", "dp"), None),
            P(("groups", "expert", "dp"), None, None),
            P(("groups", "expert", "dp"), None, None),
            P(("groups", "expert", "dp"), None, None),
        ),
        check_vma=False,
    )
```

profile of v0, /device:TPU:11, one launch (start us, length us, event | category | flops | bytes accessed | tf_op | source)
XLA Modules:
  0.0 341.6 jit_solution(10373236790888874912)
XLA Ops:
  0.6 0.0 copy-start
  0.6 0.8 reshape.49
  1.5 0.1 rev.3
  1.6 0.1 reshape.103
  1.7 0.8 copy.12
  2.5 0.1 eq.15
  2.6 0.3 fusion.14
  2.8 0.1 fusion.16
  3.0 2.5 scatter_custom_fusion
  5.5 1.1 concatenate.14
  6.6 6.1 %gather_fusion.2 = bf16[1024,2048]{1,0:T(8,128)(2,1)} fusion(bf16[129,2048]{1,0:T(8,128)(2,1)S(1)} %concatenate.14, s32[1024]{0:T(1024)S(1)} %get-tuple-element.7), kind=kCustom, calls=%fused_computation.2 | custom fusion | bytes 8392704 | tf_op jit(solution)/shard_map/gather | solution.py:56
  12.7 0.0 copy-start.7
  12.7 6.7 %all-to-all-start.1 = ((bf16[16,64,2048]{2,1,0:T(8,128)(2,1)}), bf16[16,64,2048]{2,1,0:T(8,128)(2,1)}, u32[]{:S(2)}, u32[]{:S(2)}) async-start(bf16[16,64,2048]{2,1,0:T(8,128)(2,1)} %bitcast.42), calls=%async_computation.1 | async-start | bytes 8388608 | tf_op jit(solution)/shard_map/all_to_all | solution.py:62
  19.4 0.0 copy-done.7
  19.4 0.1 copy.13
  19.5 0.1 reshape.50
  19.6 0.0 copy-start.6
  19.6 4.5 %gather_fusion.1 = f32[1024]{0:T(1024)S(1)} fusion(f32[513]{0:T(1024)S(1)} %pad_maximum_fusion, s32[1024]{0:T(1024)S(1)} %get-tuple-element.6), kind=kCustom, calls=%fused_computation.1 | custom fusion | bytes 12288 | tf_op jit(solution)/shard_map/gather | solution.py:57
  24.1 0.1 mul.44
  24.2 0.0 copy-done.6
  24.3 6.0 %gather_fusion = bf16[1024,2048]{1,0:T(8,128)(2,1)} fusion(bf16[129,2048]{1,0:T(8,128)(2,1)S(1)} %concatenate.12, s32[1024]{0:T(1024)S(1)} %get-tuple-element.7), kind=kCustom, calls=%fused_computation | custom fusion | bytes 8392704 | tf_op jit(solution)/shard_map/gather | solution.py:57
  30.3 4.9 %fusion = bf16[16,64,2048]{2,1,0:T(8,128)(2,1)} fusion(bf16[16,64,2048]{2,1,0:T(8,128)(2,1)} %bitcast.41, f32[16,64]{1,0:T(8,128)S(1)} %mul.44), kind=kLoop, calls=%fused_computation.6 | loop fusion | flops 6291456 | bytes 8392704 | tf_op jit(solution)/shard_map/convert_element_type | solution.py:57
  35.2 76.6 %all-to-all-done.1 = bf16[16,64,2048]{2,1,0:T(8,128)(2,1)} async-done(((bf16[16,64,2048]{2,1,0:T(8,128)(2,1)}), bf16[16,64,2048]{2,1,0:T(8,128)(2,1)}, u32[]{:S(2)}, u32[]{:S(2)}) %all-to-all-start.1) | async-done | bytes 4194336 | tf_op jit(solution)/shard_map/all_to_all | solution.py:62
  111.8 4.9 %all-to-all-start = ((bf16[16,64,2048]{2,1,0:T(8,128)(2,1)}), bf16[16,64,2048]{2,1,0:T(8,128)(2,1)}, u32[]{:S(2)}, u32[]{:S(2)}) async-start(bf16[16,64,2048]{2,1,0:T(8,128)(2,1)} %fusion), calls=%async_computation | async-start | bytes 8388608 | tf_op jit(solution)/shard_map/all_to_all | solution.py:63
  116.7 0.0 copy-done
  116.7 0.0 copy-start.1
  116.8 5.8 %fusion.6 = f32[1024,384]{1,0:T(8,128)} fusion(bf16[1024,2048]{1,0:T(8,128)(2,1)} %bitcast.5, bf16[1,2048,384]{2,1,0:T(8,128)(2,1)S(1)} %copy-done), kind=kOutput, calls=%fused_computation.16 | convolution fusion | flops 1610612736 | bytes 7340032 | tf_op jit(solution)/shard_map/dot_general | solution.py:8
  122.5 0.0 copy-done.1
  122.5 5.7 %fusion.9 = f32[1024,384]{1,0:T(8,128)} fusion(bf16[1024,2048]{1,0:T(8,128)(2,1)} %bitcast.5, bf16[1,2048,384]{2,1,0:T(8,128)(2,1)S(1)} %copy-done.1), kind=kOutput, calls=%fused_computation.19 | convolution fusion | flops 1610612736 | bytes 7340032 | tf_op jit(solution)/shard_map/dot_general | solution.py:9
  128.2 81.0 %all-to-all-done = bf16[16,64,2048]{2,1,0:T(8,128)(2,1)} async-done(((bf16[16,64,2048]{2,1,0:T(8,128)(2,1)}), bf16[16,64,2048]{2,1,0:T(8,128)(2,1)}, u32[]{:S(2)}, u32[]{:S(2)}) %all-to-all-start) | async-done | bytes 4194336 | tf_op jit(solution)/shard_map/all_to_all | solution.py:63
  209.2 6.4 %multiply_convert_fusion.1 = (bf16[1024,384]{1,0:T(8,128)(2,1)S(1)}, bf16[1024,384]{1,0:T(8,128)(2,1)S(1)}) fusion(f32[1024,384]{1,0:T(8,128)} %fusion.6, f32[1024,384]{1,0:T(8,128)} %fusion.9, bf16[1024,2048]{1,0:T(8,128)(2,1)} %bitcast.2, bf16[1,384,2048]{2,1,0:T(8,128)(2,1)} %param.15), kind=kOutput, calls=%fused_computation.24 | convolution fusion | flops 1615724544 | bytes 10485760 | tf_op jit(solution)/shard_map/dot_general | solution.py:15
  215.6 0.0 copy-start.2
  215.6 0.0 copy-start.4
  215.6 2.4 fusion.4
  218.0 0.0 copy-done.2
  218.0 0.0 copy-done.4
  218.0 4.3 %add_convert_fusion = bf16[1024,2048]{1,0:T(8,128)(2,1)} fusion(f32[1024,2048]{1,0:T(8,128)S(1)} %fusion.4, bf16[1024,384]{1,0:T(8,128)(2,1)S(1)} %get-tuple-element.4, bf16[1,2048,384]{2,1,0:T(8,128)(2,1)S(1)} %copy-done.1), kind=kOutput, calls=%fused_computation.7 | convolution fusion | flops 1614807040 | bytes 14942208 | tf_op jit(solution)/shard_map/dot_general | solution.py:24
  222.3 0.0 copy-start.5
  222.3 5.0 %all-to-all-start.2 = ((bf16[16,64,2048]{2,1,0:T(8,128)(2,1)}), bf16[16,64,2048]{2,1,0:T(8,128)(2,1)}, u32[]{:S(2)}, u32[]{:S(2)}) async-start(bf16[16,64,2048]{2,1,0:T(8,128)(2,1)} %bitcast.43), calls=%async_computation.2 | async-start | bytes 8388608 | tf_op jit(solution)/shard_map/all_to_all | solution.py:75
  227.4 0.0 copy-done.5
  227.4 0.0 copy-start.3
  227.4 5.8 %fusion.2 = bf16[1,2048,384]{2,1,0:T(8,128)(2,1)} fusion(bf16[1024,2048]{1,0:T(8,128)(2,1)} %bitcast.5, bf16[1024,384]{1,0:T(8,128)(2,1)S(1)} %copy-done.5), kind=kOutput, calls=%fused_computation.12 | convolution fusion | flops 1611399168 | bytes 6553600 | tf_op jit(solution)/shard_map/dot_general | solution.py:22
  233.2 0.0 copy-done.3
  233.2 0.0 copy-start.8
  233.2 0.0 copy-start.9
  233.2 5.9 %fusion.1 = bf16[1,2048,384]{2,1,0:T(8,128)(2,1)} fusion(bf16[1024,2048]{1,0:T(8,128)(2,1)} %bitcast.5, bf16[1024,384]{1,0:T(8,128)(2,1)S(1)} %copy-done.3), kind=kOutput, calls=%fused_computation.11 | convolution fusion | flops 1611399168 | bytes 6553600 | tf_op jit(solution)/shard_map/dot_general | solution.py:21
  239.1 0.0 copy-done.8
  239.1 0.0 copy-done.9
  239.1 5.3 %fusion.3 = bf16[1,384,2048]{2,1,0:T(8,128)(2,1)} fusion(bf16[1024,2048]{1,0:T(8,128)(2,1)} %bitcast.2, f32[1024,384]{1,0:T(8,128)S(1)} %copy-done.9, f32[1024,384]{1,0:T(8,128)S(1)} %copy-done.8), kind=kOutput, calls=%fused_computation.13 | convolution fusion | flops 1613758464 | bytes 8912896 | tf_op jit(solution)/shard_map/dot_general | solution.py:20
  244.4 75.5 %all-to-all-done.2 = bf16[16,64,2048]{2,1,0:T(8,128)(2,1)} async-done(((bf16[16,64,2048]{2,1,0:T(8,128)(2,1)}), bf16[16,64,2048]{2,1,0:T(8,128)(2,1)}, u32[]{:S(2)}, u32[]{:S(2)}) %all-to-all-start.2) | async-done | bytes 4194336 | tf_op jit(solution)/shard_map/all_to_all | solution.py:75
  319.8 4.7 %concatenate.15 = bf16[1025,2048]{1,0:T(8,128)(2,1)} pad(bf16[1024,2048]{1,0:T(8,128)(2,1)} %bitcast.9, bf16[]{:T(256)} %constant.18.clone.1), padding=0_1x0_0 | pad | bytes 8392706 | tf_op jit(solution)/shard_map/concatenate | solution.py:76
  324.6 8.0 %gather_fusion.3 = bf16[512,2048]{1,0:T(8,128)(2,1)} fusion(bf16[1025,2048]{1,0:T(8,128)(2,1)} %concatenate.15, s32[1024]{0:T(1024)S(1)} %pad_clamp_fusion), kind=kCustom, calls=%fused_computation.3 | custom fusion | bytes 4196352 | tf_op jit(solution)/shard_map/gather | solution.py:79
  332.5 4.1 %reshape.56 = bf16[128,4,2048]{2,1,0:T(4,128)(2,1)} reshape(bf16[512,2048]{1,0:T(8,128)(2,1)} %gather_fusion.3) | data formatting | bytes 4194304 | tf_op jit(solution)/shard_map/reshape | solution.py:79
  336.6 5.0 %reduce_sum.22 = bf16[128,2048]{1,0:T(8,128)(2,1)} reduce(bf16[128,4,2048]{2,1,0:T(4,128)(2,1)} %reshape.56, bf16[]{:T(256)} %constant.18.clone.1), dimensions={1}, to_apply=%region_2.3 | reduce | flops 786432 | bytes 2621442 | tf_op jit(solution)/shard_map/reduce_sum | solution.py:80
  (7 shorter events, 0.1 us)
Async XLA Ops:
  0.6 116.1 %copy-start = (bf16[1,2048,384]{2,1,0:T(8,128)(2,1)S(1)}, bf16[1,2048,384]{2,1,0:T(8,128)(2,1)}, u32[]{:S(2)}) copy-start(bf16[1,2048,384]{2,1,0:T(8,128)(2,1)} %param.13) | copy-start | bytes 4718596
  12.7 6.7 %copy-start.7 = (f32[128,4]{0,1:T(4,128)S(1)}, f32[128,4]{0,1:T(4,128)}, u32[]{:S(2)}) copy-start(f32[128,4]{0,1:T(4,128)} %param.11) | copy-start | bytes 6148
  12.7 99.2 %all-to-all-start.1 = ((bf16[16,64,2048]{2,1,0:T(8,128)(2,1)}), bf16[16,64,2048]{2,1,0:T(8,128)(2,1)}, u32[]{:S(2)}, u32[]{:S(2)}) async-start(bf16[16,64,2048]{2,1,0:T(8,128)(2,1)} %bitcast.42), calls=%async_computation.1 | async-start | bytes 8388608 | tf_op jit(solution)/shard_map/all_to_all | solution.py:62
  19.6 4.6 %copy-start.6 = (bf16[128,2048]{1,0:T(8,128)(2,1)S(1)}, bf16[128,2048]{1,0:T(8,128)(2,1)}, u32[]{:S(2)}) copy-start(bf16[128,2048]{1,0:T(8,128)(2,1)} %param.9) | copy-start | bytes 1572868
  111.8 97.4 %all-to-all-start = ((bf16[16,64,2048]{2,1,0:T(8,128)(2,1)}), bf16[16,64,2048]{2,1,0:T(8,128)(2,1)}, u32[]{:S(2)}, u32[]{:S(2)}) async-start(bf16[16,64,2048]{2,1,0:T(8,128)(2,1)} %fusion), calls=%async_computation | async-start | bytes 8388608 | tf_op jit(solution)/shard_map/all_to_all | solution.py:63
  116.7 5.8 %copy-start.1 = (bf16[1,2048,384]{2,1,0:T(8,128)(2,1)S(1)}, bf16[1,2048,384]{2,1,0:T(8,128)(2,1)}, u32[]{:S(2)}) copy-start(bf16[1,2048,384]{2,1,0:T(8,128)(2,1)} %param.14) | copy-start | bytes 4718596
  215.6 2.4 copy-start.2
  215.6 2.4 copy-start.4
  222.3 5.1 %copy-start.5 = (bf16[1024,384]{1,0:T(8,128)(2,1)S(1)}, bf16[1024,384]{1,0:T(8,128)(2,1)}, u32[]{:S(2)}) copy-start(bf16[1024,384]{1,0:T(8,128)(2,1)} %copy-done.4) | copy-start | bytes 2359300
  222.3 97.5 %all-to-all-start.2 = ((bf16[16,64,2048]{2,1,0:T(8,128)(2,1)}), bf16[16,64,2048]{2,1,0:T(8,128)(2,1)}, u32[]{:S(2)}, u32[]{:S(2)}) async-start(bf16[16,64,2048]{2,1,0:T(8,128)(2,1)} %bitcast.43), calls=%async_computation.2 | async-start | bytes 8388608 | tf_op jit(solution)/shard_map/all_to_all | solution.py:75
  227.4 5.8 %copy-start.3 = (bf16[1024,384]{1,0:T(8,128)(2,1)S(1)}, bf16[1024,384]{1,0:T(8,128)(2,1)}, u32[]{:S(2)}) copy-start(bf16[1024,384]{1,0:T(8,128)(2,1)} %copy-done.2) | copy-start | bytes 2359300
  233.2 5.9 %copy-start.8 = (f32[1024,384]{1,0:T(8,128)S(1)}, f32[1024,384]{1,0:T(8,128)}, u32[]{:S(2)}) copy-start(f32[1024,384]{1,0:T(8,128)} %fusion.6) | copy-start | bytes 4718596
  233.2 5.9 %copy-start.9 = (f32[1024,384]{1,0:T(8,128)S(1)}, f32[1024,384]{1,0:T(8,128)}, u32[]{:S(2)}) copy-start(f32[1024,384]{1,0:T(8,128)} %fusion.9) | copy-start | bytes 4718596
where the time goes:
time: 342 us
  waiting for transfers between devices  233 us (68%)
  matrix products  41.8 us (12%)
  local copies, waits for them, and re-layouts  39.3 us (11%)
  starting transfers between devices  16.6 us (5%)
  other arithmetic  9.91 us (3%)
    all_to_all x1, waiting for transfers between devices, local(): lax.all_to_all(send_scaled, ('expert', 'dp'), split_axis=0, concat_axis=0...  81 us
    all_to_all x1, waiting for transfers between devices, local(): lax.all_to_all(send_rows, ('expert', 'dp'), split_axis=0, concat_axis=0,...  76.6 us
    all_to_all x1, waiting for transfers between devices, local(): lax.all_to_all(row_grads, ('expert', 'dp'), split_axis=0, concat_axis=0,...  75.5 us
    gather x1, local copies, waits for them, and re-layouts, local(): picked = back_pad[slot_index].reshape(tok_rows, top_count, width)  7.98 us
  transfers between devices with their start and end apart: 3, of which 3 were waited for; matrix products, arithmetic and copies ran while one was open for 13% of the time, Pallas kernels for 0%

commit v1 on v0

--- a/solution.py
+++ b/solution.py
@@ -1,7 +1,346 @@
+import functools
+
 import jax
 import jax.numpy as jnp
 from jax import lax
+from jax.experimental import pallas as pl
+from jax.experimental.pallas import tpu as pltpu
 from jax.sharding import PartitionSpec as P
+
+OVER_LAST = (((1,), (1,)), ((), ()))
+OVER_ROWS = (((0,), (0,)), ((), ()))
+VMEM_LIMIT = 56 * 1024 * 1024
+
+
+def ring_of(mesh):
+    chips = list(mesh.devices[0, :, 0])
+    places = [getattr(chip, "coords", None) for chip in chips]
+    natural = list(range(len(chips)))
+    if any(place is None for place in places):
+        return natural
+    at = {(place[0], place[2]): i for i, place in enumerate(places)}
+    xs = sorted({x for x, _ in at})
+    zs = sorted({z for _, z in at})
+    if len(at) != len(chips) or len(xs) * len(zs) != len(chips):
+        return natural
+    if len(xs) == 2:
+        return [at[xs[0], z] for z in zs] + [at[xs[1], z] for z in reversed(zs)]
+    if len(zs) == 2:
+        return [at[x, zs[0]] for x in xs] + [at[x, zs[1]] for x in reversed(xs)]
+    return natural
+
+
+def pack_kernel(home_cap, lanes, routes_ref, gates_ref, helper_ref, tokens_ref, out_ref):
+    rows, width = tokens_ref.shape
+    experts = helper_ref.shape[1]
+    expert_of_row = lax.broadcasted_iota(jnp.int32, (experts, rows), 0)
+    named = jnp.zeros((experts, rows), jnp.float32)
+    gate = jnp.zeros((experts, rows), jnp.float32)
+    for k in range(routes_ref.shape[0]):
+        hit = routes_ref[k : k + 1, :] == expert_of_row
+        named = named + jnp.where(hit, 1.0, 0.0)
+        gate = gate + jnp.where(hit, gates_ref[k : k + 1, :], 0.0)
+    earlier = lax.broadcasted_iota(jnp.int32, (rows, rows), 0) < lax.broadcasted_iota(
+        jnp.int32, (rows, rows), 1
+    )
+    rank = jnp.dot(
+        named.astype(jnp.bfloat16),
+        jnp.where(earlier, 1.0, 0.0).astype(jnp.bfloat16),
+        preferred_element_type=jnp.float32,
+    )
+    partner = jnp.bitwise_xor(lax.broadcasted_iota(jnp.int32, (experts, experts), 0), 1)
+    column = lax.broadcasted_iota(jnp.int32, (experts, experts), 1)
+    flag = jnp.where(partner == column, helper_ref[...], 0)
+    helped = jnp.max(flag, axis=1, keepdims=True) == 1
+    gate = jnp.where((rank < home_cap) | helped, gate, 0.0)
+    terms = []
+    for _ in range(3):
+        term = gate.astype(jnp.bfloat16).astype(jnp.float32)
+        terms.append(term)
+        gate = gate - term
+    terms.append(jnp.zeros((lanes - 3 * experts, rows), jnp.float32))
+    out_ref[:, :width] = tokens_ref[...]
+    out_ref[:, width:] = jnp.concatenate(terms, axis=0).T.astype(jnp.bfloat16)
+
+
+def pack(tokens, routes, gates, helper, home_cap):
+    rows, width = tokens.shape
+    lanes = 128 * pl.cdiv(3 * helper.shape[0] + 1, 128)
+    return pl.pallas_call(
+        functools.partial(pack_kernel, home_cap, lanes),
+        out_shape=jax.ShapeDtypeStruct((rows, width + lanes), jnp.bfloat16),
+        name="pack",
+    )(routes.T, gates.T, helper[None, :], tokens)
+
+
+def expert_kernel(count, experts, *refs):
+    token_refs, cot_refs = refs[:count], refs[count : 2 * count]
+    sources = refs[2 * count : 2 * count + 6]
+    act_ref, grad_ref, held_tokens, held_cot = refs[2 * count + 6 : 2 * count + 10]
+    weights, arrived = refs[2 * count + 10 : 2 * count + 16], refs[2 * count + 16]
+    rows, width = cot_refs[0].shape
+    lanes = token_refs[0].shape[1] - width
+    hidden = weights[0].shape[1]
+    chip, core, cores = lax.axis_index("expert"), lax.axis_index("dp"), lax.axis_size("dp")
+    copies = [
+        pltpu.make_async_copy(sources[i], weights[i], arrived.at[i]) for i in range(len(sources))
+    ]
+    for copy in copies:
+        copy.start()
+    for i in range(count):
+        held_tokens[pl.ds(i * rows, rows), :] = token_refs[i][:, :width]
+        held_cot[pl.ds(i * rows, rows), :] = cot_refs[i][...]
+    lane = lax.broadcasted_iota(jnp.int32, (rows, lanes), 1)
+    grads = []
+    for which in range(2):
+        gate_w, up_w, down_w = weights[3 * which : 3 * which + 3]
+        expert = chip * cores + (core if which == 0 else 1 - core)
+        chosen = (lane == expert) | (lane == expert + experts) | (lane == expert + 2 * experts)
+        columns = [
+            jnp.sum(
+                jnp.where(chosen, ref[:, width:].astype(jnp.float32), 0.0), axis=1, keepdims=True
+            )
+            for ref in token_refs
+        ]
+        gate = columns[0] if count == 1 else jnp.concatenate(columns, axis=0)
+        copies[3 * which].wait()
+        gate_pre = jnp.dot(held_tokens[...], gate_w[...], preferred_element_type=jnp.float32)
+        copies[3 * which + 1].wait()
+        up_pre = jnp.dot(held_tokens[...], up_w[...], preferred_element_type=jnp.float32)
+        copies[3 * which + 2].wait()
+        back = lax.dot_general(held_cot[...], down_w[...], OVER_LAST, preferred_element_type=jnp.float32)
+        sigma = jax.nn.sigmoid(gate_pre)
+        active = gate_pre * sigma
+        back = back * gate
+        grad_up = (back * active).astype(jnp.bfloat16)
+        grad_gate = (back * up_pre * sigma * (1.0 + gate_pre * (1.0 - sigma))).astype(jnp.bfloat16)
+        scaled_hidden = (active * up_pre * gate).astype(jnp.bfloat16)
+        act_ref[:, pl.ds(3 * which * hidden, hidden)] = grad_gate
+        act_ref[:, pl.ds((3 * which + 1) * hidden, hidden)] = grad_up
+        act_ref[:, pl.ds((3 * which + 2) * hidden, hidden)] = scaled_hidden
+        grads += [(grad_gate, gate_w), (grad_up, up_w)]
+    step = 512
+    for start in range(0, width, step):
+        total = None
+        for value, weight in grads:
+            part = lax.dot_general(
+                value, weight[pl.ds(start, step), :], OVER_LAST, preferred_element_type=jnp.float32
+            )
+            total = part if total is None else total + part
+        grad_ref[:, pl.ds(start, step)] = total
+
+
+def expert_batch(blocks, weights, experts):
+    tokens, cots = zip(*blocks)
+    rows, width = cots[0].shape
+    hidden = weights[0].shape[1]
+    total = rows * len(blocks)
+    vmem = pl.BlockSpec(memory_space=pltpu.VMEM)
+    return pl.pallas_call(
+        functools.partial(expert_kernel, len(blocks), experts),
+        in_specs=[vmem] * (2 * len(blocks)) + [pl.BlockSpec(memory_space=pl.ANY)] * 6,
+        out_specs=[vmem, vmem],
+        out_shape=[
+            jax.ShapeDtypeStruct((total, 6 * hidden), jnp.bfloat16),
+            jax.ShapeDtypeStruct((total, width), jnp.float32),
+        ],
+        scratch_shapes=[pltpu.VMEM((total, width), jnp.bfloat16)] * 2
+        + [pltpu.VMEM(weight.shape, jnp.bfloat16) for weight in weights]
+        + [pltpu.SemaphoreType.DMA((6,))],
+        compiler_params=pltpu.CompilerParams(vmem_limit_bytes=VMEM_LIMIT),
+        cost_estimate=pl.CostEstimate(
+            flops=2 * 5 * total * 2 * hidden * width,
+            bytes_accessed=12 * hidden * width + total * (8 * width + 12 * hidden),
+            transcendentals=2 * total * hidden,
+        ),
+        name="expert_batch",
+    )(*tokens, *cots, *weights)
+
+
+def row_grads_kernel(counts, add, *refs):
+    blocks, batches = counts
+    token_refs, act_refs = refs[:blocks], refs[blocks : blocks + batches]
+    rest = refs[blocks + batches :]
+    terms, (gate_ref, up_ref, acts) = rest[: 2 * add], rest[2 * add :]
+    hidden = gate_ref.shape[1]
+
+    @pl.when(pl.program_id(0) == 0)
+    def _():
+        at = 0
+        for ref in act_refs:
+            acts[pl.ds(at, ref.shape[0]), :] = ref[:, : 2 * hidden]
+            at += ref.shape[0]
+
+    rows = jnp.concatenate([ref[...] for ref in token_refs], axis=0)
+    out = lax.dot_general(rows, acts[...], OVER_ROWS, preferred_element_type=jnp.float32)
+    for i, ref in enumerate((gate_ref, up_ref)):
+        value = out[:, i * hidden : (i + 1) * hidden]
+        if add:
+            value = value + terms[i][...].astype(jnp.float32)
+        ref[...] = value.astype(jnp.bfloat16)
+
+
+def row_grads(which, tokens, acts, width, terms=()):
+    rows = tokens[0].shape[0]
+    hidden = acts[0].shape[1] // 6
+    total = rows * len(tokens)
+    tile = 256
+    out_spec = pl.BlockSpec((tile, hidden), lambda j: (j, 0))
+    return pl.pallas_call(
+        functools.partial(row_grads_kernel, (len(tokens), len(acts)), len(terms) // 2),
+        grid=(width // tile,),
+        in_specs=[pl.BlockSpec((rows, tile), lambda j: (0, j))] * len(tokens)
+        + [pl.BlockSpec((act.shape[0], 3 * hidden), lambda j: (0, which)) for act in acts]
+        + [out_spec] * len(terms),
+        out_specs=[out_spec] * 2,
+        out_shape=[jax.ShapeDtypeStruct((width, hidden), jnp.bfloat16)] * 2,
+        scratch_shapes=[pltpu.VMEM((total, 2 * hidden), jnp.bfloat16)],
+        compiler_params=pltpu.CompilerParams(vmem_limit_bytes=VMEM_LIMIT),
+        cost_estimate=pl.CostEstimate(
+            flops=2 * total * width * 2 * hidden,
+            bytes_accessed=2 * total * (width + 2 * hidden) + 8 * width * hidden,
+            transcendentals=0,
+        ),
+        name="row_grads",
+    )(*tokens, *acts, *terms)
+
+
+def down_grads_kernel(counts, add, *refs):
+    blocks, batches = counts
+    cot_refs, act_refs = refs[:blocks], refs[blocks : blocks + batches]
+    rest = refs[blocks + batches :]
+    terms, (down_ref, acts) = rest[:add], rest[add:]
+    hidden = down_ref.shape[0]
+
+    @pl.when(pl.program_id(0) == 0)
+    def _():
+        at = 0
+        for ref in act_refs:
+            acts[:, pl.ds(at, ref.shape[0])] = ref[...].T
+            at += ref.shape[0]
+
+    rows = jnp.concatenate([ref[...] for ref in cot_refs], axis=0)
+    out = jnp.dot(acts[...], rows, preferred_element_type=jnp.float32)
+    for term in terms:
+        out = out + term[...].astype(jnp.float32)
+    down_ref[...] = out.astype(jnp.bfloat16)
+
+
+def down_grads(which, cots, acts, terms=()):
+    rows, width = cots[0].shape
+    hidden = acts[0].shape[1] // 6
+    total = rows * len(cots)
+    tile = 512
+    out_spec = pl.BlockSpec((hidden, tile), lambda j: (0, j))
+    return pl.pallas_call(
+        functools.partial(down_grads_kernel, (len(cots), len(acts)), len(terms)),
+        grid=(width // tile,),
+        in_specs=[pl.BlockSpec((rows, tile), lambda j: (0, j))] * len(cots)
+        + [pl.BlockSpec((act.shape[0], hidden), lambda j: (0, 3 * which + 2)) for act in acts]
+        + [out_spec] * len(terms),
+        out_specs=out_spec,
+        out_shape=jax.ShapeDtypeStruct((hidden, width), jnp.bfloat16),
+        scratch_shapes=[pltpu.VMEM((hidden, total), jnp.bfloat16)],
+        compiler_params=pltpu.CompilerParams(vmem_limit_bytes=VMEM_LIMIT),
+        cost_estimate=pl.CostEstimate(
+            flops=2 * total * width * hidden,
+            bytes_accessed=2 * total * (width + hidden) + 4 * width * hidden,
+            transcendentals=0,
+        ),
+        name="down_grads",
+    )(*cots, *acts, *terms)
+
+
+def ring_local(ring, tokens, cotangent, routes, gates, helper, w_gate, w_up, w_down):
+    rows, width = tokens.shape
+    experts = helper.shape[0]
+    chips, cores = lax.axis_size("expert"), lax.axis_size("dp")
+    route_cap = 2 * rows * routes.shape[1] // (chips * cores)
+    home_cap = route_cap - 3 * route_cap // 8
+    reach = chips // 2
+    up_pairs = [(ring[i], ring[(i + 1) % chips]) for i in range(chips)]
+    down_pairs = [(b, a) for a, b in up_pairs]
+    swap = [(0, 1), (1, 0)]
+    up = lambda value: lax.ppermute(value, "expert", up_pairs)
+    down = lambda value: lax.ppermute(value, "expert", down_pairs)
+    other = lambda value: lax.ppermute(value, "dp", swap)
+    tied = lax.optimization_barrier
+
+    packed = pack(tokens, routes, gates, helper, home_cap)
+    own = (w_gate[0], w_up[0], w_down[0])
+    weights = own + tuple(other(value) for value in own)
+    act, own_grad = expert_batch([(packed, cotangent)], weights, experts)
+    row_blocks, cot_blocks, acts = [packed], [cotangent], [act]
+    grads_below, grads_above = [], []
+    tok_b = tok_a = packed
+    cot_b = cot_a = cotangent
+    for s in range(1, reach):
+        cot_b, cot_a = up(cot_b), down(cot_a)
+        tok_b, tok_a = up(tok_b), down(tok_a)
+        tok_b, tok_a, acts[-1] = tied((tok_b, tok_a, acts[-1]))
+        act, grad = expert_batch(((tok_b, cot_b), (tok_a, cot_a)), weights, experts)
+        row_blocks += (tok_b, tok_a)
+        cot_blocks += (cot_b, cot_a)
+        acts.append(act)
+        grads_below.insert(0, grad[:rows])
+        grads_above.insert(0, grad[rows:])
+
+    cut = width // 2
+    low = lambda value: value[:, :cut]
+    high = lambda value: value[:, cut:]
+    half = lambda value: value.astype(jnp.bfloat16)
+    plus = lambda value, term: half(value.astype(jnp.float32) + term)
+
+    far_cot, far_tok = down(cot_a), up(tok_b)
+    high_down, low_up = down(half(high(grads_below[0]))), up(half(low(grads_above[0])))
+    far_tok, acts[-1] = tied((far_tok, acts[-1]))
+    act, far_grad = expert_batch([(far_tok, far_cot)], weights, experts)
+    row_blocks.append(far_tok)
+    cot_blocks.append(far_cot)
+    acts.append(act)
+    low_down, high_up = down(half(low(far_grad))), up(half(high(far_grad)))
+
+    sent, out = {}, {}
+
+    def far_rows():
+        parts = row_grads(1, row_blocks, acts, width)
+        sent["gate"], sent["up"] = (other(part) for part in parts)
+        return parts[0]
+
+    def far_down():
+        part = down_grads(1, cot_blocks, acts)
+        sent["down"] = other(part)
+        return part
+
+    def own_rows():
+        terms = (sent["gate"], sent["up"])
+        out["gate"], out["up"] = row_grads(0, row_blocks, acts, width, terms)
+        return out["gate"]
+
+    def own_down():
+        out["down"] = down_grads(0, cot_blocks, acts, (sent["down"],))
+        return out["down"]
+
+    chores = [far_rows, far_down, own_rows, own_down]
+    for s in range(reach - 1):
+        if chores:
+            high_down, low_up, _ = tied((high_down, low_up, chores.pop(0)()))
+        if s + 1 < reach - 1:
+            high_down = down(plus(high_down, high(grads_below[s + 1])))
+            low_up = up(plus(low_up, low(grads_above[s + 1])))
+        low_down = down(plus(low_down, low(grads_below[s])))
+        high_up = up(plus(high_up, high(grads_above[s])))
+    for chore in chores:
+        chore()
+
+    def three(mine, first, second):
+        return half(mine + first.astype(jnp.float32) + second.astype(jnp.float32))
+
+    low_down, high_up, out["down"] = tied((low_down, high_up, out["down"]))
+    grad_tokens = jnp.concatenate(
+        [three(low(own_grad), low_down, low_up), three(high(own_grad), high_down, high_up)], axis=1
+    )
+    return (grad_tokens, out["gate"][None], out["up"][None], out["down"][None])
 
 
 def expert_pass(rows, scaled, gate_w, up_w, down_w):
@@ -27,7 +366,7 @@
     return (row_grads.astype(jnp.bfloat16), grad_gate, grad_up, grad_down)
 
 
-def local(tokens, cotangent, routes, gates, helper, w_gate, w_up, w_down):
+def exchange_local(tokens, cotangent, routes, gates, helper, w_gate, w_up, w_down):
     tok_rows, width = tokens.shape
     top_count = routes.shape[1]
     devices = lax.axis_size(("expert", "dp"))
@@ -87,6 +426,15 @@
 
 
 def solution(mesh):
+    chips, cores = mesh.shape["expert"], mesh.shape["dp"]
+
+    def local(tokens, cotangent, routes, *rest):
+        slots = 2 * tokens.shape[0] * routes.shape[1]
+        whole = chips * cores * tokens.shape[0]
+        if cores == 2 and chips % 2 == 0 and chips > 2 and whole <= 2 * slots:
+            return ring_local(ring_of(mesh), tokens, cotangent, routes, *rest)
+        return exchange_local(tokens, cotangent, routes, *rest)
+
     return jax.shard_map(
         local,
         mesh=mesh,

time: 342 us -> 171 us (0.50)
  the two profiles are of different devices: /device:TPU:11 before, /device:TPU:0 now
where the time goes in v1:
time: 171 us; the launch traced here: 170 us
  Pallas kernels  84.7 us (50%)
  waiting for transfers between devices  38 us (22%)
  starting transfers between devices  34.7 us (20%)
  local copies, waits for them, and re-layouts  5.94 us (3%)
  other arithmetic  5.66 us (3%)
    pallas_call x5, Pallas kernels, expert_batch(): pl.pallas_call(functools.partial(expert_kernel, len(blocks), experts), in...  50.2 us
    ppermute x14, waiting for transfers between devices, ring_local(): down = lambda value: lax.ppermute(value, 'expert', down_pairs)  23.3 us
    pallas_call x2, Pallas kernels, row_grads(): pl.pallas_call(functools.partial(row_grads_kernel, (len(tokens), len(acts...  19.9 us
    ppermute x14, starting transfers between devices, ring_local(): down = lambda value: lax.ppermute(value, 'expert', down_pairs)  19.3 us
    ppermute x14, waiting for transfers between devices, ring_local(): up = lambda value: lax.ppermute(value, 'expert', up_pairs)  14.1 us
    ppermute x14, starting transfers between devices, ring_local(): up = lambda value: lax.ppermute(value, 'expert', up_pairs)  13.8 us
    pallas_call x2, Pallas kernels, down_grads(): pl.pallas_call(functools.partial(down_grads_kernel, (len(cots), len(acts)...  12.4 us
    unnamed x46, local copies, waits for them, and re-layouts  5.87 us
  transfers between devices with their start and end apart: 34, of which 11 were waited for; matrix products, arithmetic and copies ran while one was open for 2% of the time, Pallas kernels for 45%

profile of v1, /device:TPU:0, one launch (start us, length us, event | category | flops | bytes accessed | tf_op | source)
XLA Modules:
  0.0 169.9 jit_solution(12387365754990987522)
XLA Ops:
  0.6 0.5 collective-permute-start
  1.2 0.4 collective-permute-start.2
  1.7 2.2 %pack.1.refs_0_ = bf16[128,2176]{1,0:T(8,128)(2,1)} custom-call(s32[4,128]{1,0:T(4,128)} %bitcast.28, f32[4,128]{1,0:T(4,128)} %bitcast.29, s32[1,16]{1,0:T(1,128)} %bitcast.30, bf16[128,2048]{1,0:T(8,128)(2,1)} %tokens_ref.1), custom_call_target="tpu_custom_call" | custom-call | tf_op jit(solution)/shard_map/pack/pallas_call | solution.py:69
  3.8 2.6 %collective-permute-start.4 = (bf16[128,2176]{1,0:T(8,128)(2,1)}, bf16[128,2176]{1,0:T(8,128)(2,1)S(1)}, u32[]{:S(2)}, u32[]{:S(2)}) collective-permute-start(bf16[128,2176]{1,0:T(8,128)(2,1)} %pack.1.refs_0_), channel_id=1, source_target_pairs={{4,0},{8,4},{12,8},{14,12},{10,14},{6,10},{2,6},{0,2},{5,1},{9,5},... | collective-permute-start | bytes 1671176 | tf_op jit(solution)/shard_map/ppermute | solution.py:265
  6.5 1.9 %collective-permute-start.8 = (bf16[128,2048]{1,0:T(8,128)(2,1)}, bf16[128,2048]{1,0:T(8,128)(2,1)S(1)}, u32[]{:S(2)}, u32[]{:S(2)}) collective-permute-start(bf16[128,2048]{1,0:T(8,128)(2,1)} %refs_0_.3), channel_id=1, source_target_pairs={{4,0},{8,4},{12,8},{14,12},{10,14},{6,10},{2,6},{0,2},{5,1},{9,5},... | collective-permute-start | bytes 1572872 | tf_op jit(solution)/shard_map/ppermute | solution.py:265
  8.4 0.5 collective-permute-done.1.refs_6_.refs_8_
  8.9 2.9 %collective-permute-start.7 = (bf16[128,2048]{1,0:T(8,128)(2,1)}, bf16[128,2048]{1,0:T(8,128)(2,1)S(1)}, u32[]{:S(2)}, u32[]{:S(2)}) collective-permute-start(bf16[128,2048]{1,0:T(8,128)(2,1)} %refs_0_.3), channel_id=1, source_target_pairs={{0,4},{4,8},{8,12},{12,14},{14,10},{10,6},{6,2},{2,0},{1,5},{5,9},... | collective-permute-start | bytes 1572872 | tf_op jit(solution)/shard_map/ppermute | solution.py:264
  11.9 8.7 %expert_batch.5 = (bf16[128,2304]{1,0:T(8,128)(2,1)}, f32[128,2048]{1,0:T(8,128)}) custom-call(bf16[128,2176]{1,0:T(8,128)(2,1)} %pack.1.refs_0_, bf16[128,2048]{1,0:T(8,128)(2,1)} %refs_0_.3, bf16[2048,384]{1,0:T(8,128)(2,1)} %bitcast.10, bf16[2048,384]{1,0:T(8,128)(2,1)} %bitcast.16, bf16[384,2048]{1,0:T(8,128)(2,1)} %bitcast.22, ...), custom_call_target="tpu_custom_call" | custom-call | flops 2013265920 | bytes 12124160 | tf_op jit(solution)/shard_map/expert_batch/pallas_call | solution.py:139
  20.6 1.5 collective-permute-done.3.refs_0_.refs_1_
  22.1 0.2 collective-permute-start.5
  22.2 1.9 %collective-permute-start.6 = (bf16[128,2176]{1,0:T(8,128)(2,1)S(1)}, bf16[128,2176]{1,0:T(8,128)(2,1)S(1)}, u32[]{:S(2)}, u32[]{:S(2)}) collective-permute-start(bf16[128,2176]{1,0:T(8,128)(2,1)S(1)} %collective-permute-done.4.refs_1_.refs_2_), channel_id=1, source_target_pairs={{4,0},{8,4},{12,8},{14,12},{10,14},{6,10},{2,6},{0,2},{5,1},{9,5},... | collective-permute-start | bytes 1671176 | tf_op jit(solution)/shard_map/ppermute | solution.py:265
  24.1 7.3 %collective-permute-done.8.refs_3_.refs_2_ = bf16[128,2048]{1,0:T(8,128)(2,1)S(1)} collective-permute-done((bf16[128,2048]{1,0:T(8,128)(2,1)}, bf16[128,2048]{1,0:T(8,128)(2,1)S(1)}, u32[]{:S(2)}, u32[]{:S(2)}) %collective-permute-start.8) | collective-permute-done | bytes 524320 | tf_op jit(solution)/shard_map/ppermute | solution.py:265
  31.4 1.9 %collective-permute-start.12 = (bf16[128,2048]{1,0:T(8,128)(2,1)S(1)}, bf16[128,2048]{1,0:T(8,128)(2,1)S(1)}, u32[]{:S(2)}, u32[]{:S(2)}) collective-permute-start(bf16[128,2048]{1,0:T(8,128)(2,1)S(1)} %collective-permute-done.8.refs_3_.refs_2_), channel_id=1, source_target_pairs={{4,0},{8,4},{12,8},{14,12},{10,14},{6,10},{2,6},{0,2},{5,1},{9,5},... | collective-permute-start | bytes 1572872 | tf_op jit(solution)/shard_map/ppermute | solution.py:265
  33.4 0.7 copy-done.6
  34.1 11.0 %expert_batch.6 = (bf16[256,2304]{1,0:T(8,128)(2,1)}, f32[256,2048]{1,0:T(8,128)}) custom-call(bf16[128,2176]{1,0:T(8,128)(2,1)} %copy-done.18, bf16[128,2176]{1,0:T(8,128)(2,1)} %copy-done.17, bf16[128,2048]{1,0:T(8,128)(2,1)} %copy-done.6, bf16[128,2048]{1,0:T(8,128)(2,1)} %copy-done.5, bf16[2048,384]{1,0:T(8,128)(2,1)} %bitcast.11, ...), custom_call_target="tpu_custom_call" | custom-call | flops 4026531840 | bytes 14811136 | tf_op jit(solution)/shard_map/expert_batch/pallas_call | solution.py:139
  45.1 0.2 collective-permute-done.5.refs_0_.refs_3_
  45.3 1.3 collective-permute-start.9
  46.5 0.8 collective-permute-start.10
  47.3 7.2 %collective-permute-done.12.refs_3_.refs_4_ = bf16[128,2048]{1,0:T(8,128)(2,1)S(1)} collective-permute-done((bf16[128,2048]{1,0:T(8,128)(2,1)S(1)}, bf16[128,2048]{1,0:T(8,128)(2,1)S(1)}, u32[]{:S(2)}, u32[]{:S(2)}) %collective-permute-start.12) | collective-permute-done | bytes 524320 | tf_op jit(solution)/shard_map/ppermute | solution.py:265
  54.6 1.9 %collective-permute-start.15 = (bf16[128,2048]{1,0:T(8,128)(2,1)S(1)}, bf16[128,2048]{1,0:T(8,128)(2,1)S(1)}, u32[]{:S(2)}, u32[]{:S(2)}) collective-permute-start(bf16[128,2048]{1,0:T(8,128)(2,1)S(1)} %collective-permute-done.12.refs_3_.refs_4_), channel_id=1, source_target_pairs={{4,0},{8,4},{12,8},{14,12},{10,14},{6,10},{2,6},{0,2},{5,1},{9,5},... | collective-permute-start | bytes 1572872 | tf_op jit(solution)/shard_map/ppermute | solution.py:265
  56.5 0.3 collective-permute-start.14
  56.8 0.5 copy-done.8
  57.3 11.0 %expert_batch.7 = (bf16[256,2304]{1,0:T(8,128)(2,1)}, f32[256,2048]{1,0:T(8,128)}) custom-call(bf16[128,2176]{1,0:T(8,128)(2,1)} %copy-done.19, bf16[128,2176]{1,0:T(8,128)(2,1)} %copy-done.20, bf16[128,2048]{1,0:T(8,128)(2,1)} %copy-done.8, bf16[128,2048]{1,0:T(8,128)(2,1)} %copy-done.7, bf16[2048,384]{1,0:T(8,128)(2,1)} %bitcast.12, ...), custom_call_target="tpu_custom_call" | custom-call | flops 4026531840 | bytes 14811136 | tf_op jit(solution)/shard_map/expert_batch/pallas_call | solution.py:139
  68.2 0.2 collective-permute-done.9.refs_0_.refs_5_
  68.4 1.3 collective-permute-start.13
  69.7 7.8 %collective-permute-done.15.refs_3_.refs_6_ = bf16[128,2048]{1,0:T(8,128)(2,1)S(1)} collective-permute-done((bf16[128,2048]{1,0:T(8,128)(2,1)S(1)}, bf16[128,2048]{1,0:T(8,128)(2,1)S(1)}, u32[]{:S(2)}, u32[]{:S(2)}) %collective-permute-start.15) | collective-permute-done | bytes 524320 | tf_op jit(solution)/shard_map/ppermute | solution.py:265
  77.5 1.7 collective-permute-start.16
  79.2 0.5 collective-permute-done.14.refs_2_.refs_5_
  79.7 0.8 copy-done.10
  80.5 11.0 %expert_batch.8 = (bf16[256,2304]{1,0:T(8,128)(2,1)}, f32[256,2048]{1,0:T(8,128)}) custom-call(bf16[128,2176]{1,0:T(8,128)(2,1)} %copy-done.21, bf16[128,2176]{1,0:T(8,128)(2,1)} %copy-done.22, bf16[128,2048]{1,0:T(8,128)(2,1)} %copy-done.10, bf16[128,2048]{1,0:T(8,128)(2,1)} %copy-done.9, bf16[2048,384]{1,0:T(8,128)(2,1)} %bitcast.13, ...), custom_call_target="tpu_custom_call" | custom-call | flops 4026531840 | bytes 14811136 | tf_op jit(solution)/shard_map/expert_batch/pallas_call | solution.py:139
  91.4 1.7 %convert.9 = bf16[256,2048]{1,0:T(8,128)(2,1)S(1)} convert(f32[256,2048]{1,0:T(8,128)} %get-tuple-element.51) | non-fusion elementwise | flops 524288 | bytes 3145728 | tf_op jit(solution)/shard_map/convert.1
  93.2 0.8 copy-done.4
  94.0 0.8 copy-done.2
  94.8 8.6 %expert_batch.9 = (bf16[128,2304]{1,0:T(8,128)(2,1)}, f32[128,2048]{1,0:T(8,128)}) custom-call(bf16[128,2176]{1,0:T(8,128)(2,1)} %copy-done.4, bf16[128,2048]{1,0:T(8,128)(2,1)} %copy-done.2, bf16[2048,384]{1,0:T(8,128)(2,1)} %bitcast.14, bf16[2048,384]{1,0:T(8,128)(2,1)} %bitcast.20, bf16[384,2048]{1,0:T(8,128)(2,1)} %bitcast.26, ...), custom_call_target="tpu_custom_call" | custom-call | flops 2013265920 | bytes 12124160 | tf_op jit(solution)/shard_map/expert_batch/pallas_call | solution.py:139
  103.4 1.3 convert.8
  104.8 0.4 collective-permute-start.21
  105.2 1.6 collective-permute-start.17
  106.9 0.4 collective-permute-start.27
  107.3 1.6 collective-permute-start.26
  109.0 6.0 %down_grads.2 = bf16[384,2048]{1,0:T(8,128)(2,1)} custom-call(bf16[128,2048]{1,0:T(8,128)(2,1)} %refs_0_.3, bf16[128,2048]{1,0:T(8,128)(2,1)} %copy-done.6, bf16[128,2048]{1,0:T(8,128)(2,1)} %copy-done.5, bf16[128,2048]{1,0:T(8,128)(2,1)} %copy-done.8, bf16[128,2048]{1,0:T(8,128)(2,1)} %copy-done.7, bf16[128,2048]{1,0:T(8,128)(2,1)} %copy-done.10, ...), custom_call_target="tpu_custom_call" | custom-call | flops 1610612736 | bytes 8126464 | tf_op jit(solution)/shard_map/down_grads/pallas_call | solution.py:235
  115.1 0.8 add_convert_fusion.8
  115.9 1.1 collective-permute-start.22
  117.0 0.9 collective-permute-start.18
  117.9 9.6 %row_grads.2 = (bf16[2048,384]{1,0:T(8,128)(2,1)}, bf16[2048,384]{1,0:T(8,128)(2,1)}) custom-call(bf16[128,2176]{1,0:T(8,128)(2,1)} %pack.1.refs_0_, bf16[128,2176]{1,0:T(8,128)(2,1)} %copy-done.18, bf16[128,2176]{1,0:T(8,128)(2,1)} %copy-done.17, bf16[128,2176]{1,0:T(8,128)(2,1)} %copy-done.19, bf16[128,2176]{1,0:T(8,128)(2,1)} %copy-done.20, ...), custom_call_target="tpu_custom_call" | custom-call | flops 3221225472 | bytes 12058624 | tf_op jit(solution)/shard_map/row_grads/pallas_call | solution.py:189
  127.6 0.5 collective-permute-start.32
  128.2 0.3 add_convert_fusion.4
  128.5 1.3 collective-permute-start.29
  129.8 0.8 collective-permute-start.28
  130.6 6.3 %collective-permute-done.29 = bf16[128,1024]{1,0:T(8,128)(2,1)S(1)} collective-permute-done((bf16[128,1024]{1,0:T(8,128)(2,1)S(1)}, bf16[128,1024]{1,0:T(8,128)(2,1)S(1)}, u32[]{:S(2)}, u32[]{:S(2)}) %collective-permute-start.29) | collective-permute-done | bytes 262176 | tf_op jit(solution)/shard_map/ppermute | solution.py:264
  136.9 1.2 collective-permute-start.23
  138.1 0.8 collective-permute-start.19
  138.9 5.4 %collective-permute-done.23 = bf16[128,1024]{1,0:T(8,128)(2,1)S(1)} collective-permute-done((bf16[128,1024]{1,0:T(8,128)(2,1)S(1)}, bf16[128,1024]{1,0:T(8,128)(2,1)S(1)}, u32[]{:S(2)}, u32[]{:S(2)}) %collective-permute-start.23) | collective-permute-done | bytes 262176 | tf_op jit(solution)/shard_map/ppermute | solution.py:264
  144.3 1.0 collective-permute-done.19
  145.3 0.4 add_convert_fusion.2
  145.7 1.6 collective-permute-start.24
  147.3 0.5 collective-permute-start.20
  147.8 1.6 collective-permute-start.31
  149.3 6.3 %down_grads.3 = bf16[384,2048]{1,0:T(8,128)(2,1)} custom-call(bf16[128,2048]{1,0:T(8,128)(2,1)} %refs_0_.3, bf16[128,2048]{1,0:T(8,128)(2,1)} %copy-done.6, bf16[128,2048]{1,0:T(8,128)(2,1)} %copy-done.5, bf16[128,2048]{1,0:T(8,128)(2,1)} %copy-done.8, bf16[128,2048]{1,0:T(8,128)(2,1)} %copy-done.7, bf16[128,2048]{1,0:T(8,128)(2,1)} %copy-done.10, ...), custom_call_target="tpu_custom_call" | custom-call | flops 1610612736 | bytes 8126464 | tf_op jit(solution)/shard_map/down_grads/pallas_call | solution.py:235
  155.7 0.5 collective-permute-start.30
  156.2 1.1 copy-done.13
  157.3 1.2 copy-done.14
  158.5 10.3 %row_grads.3 = (bf16[2048,384]{1,0:T(8,128)(2,1)}, bf16[2048,384]{1,0:T(8,128)(2,1)}) custom-call(bf16[128,2176]{1,0:T(8,128)(2,1)} %pack.1.refs_0_, bf16[128,2176]{1,0:T(8,128)(2,1)} %copy-done.18, bf16[128,2176]{1,0:T(8,128)(2,1)} %copy-done.17, bf16[128,2176]{1,0:T(8,128)(2,1)} %copy-done.19, bf16[128,2176]{1,0:T(8,128)(2,1)} %copy-done.20, ...), custom_call_target="tpu_custom_call" | custom-call | flops 3221225472 | bytes 12058624 | tf_op jit(solution)/shard_map/row_grads/pallas_call | solution.py:189
  168.8 0.2 add_convert_fusion.1
  169.1 0.8 pad_maximum_fusion
  (69 shorter events, 0.6 us)
Async XLA Ops:
  0.6 5.9 %collective-permute-start = (bf16[2048,384]{1,0:T(8,128)(2,1)}, bf16[2048,384]{1,0:T(8,128)(2,1)S(1)}, u32[]{:S(2)}, u32[]{:S(2)}) collective-permute-start(bf16[2048,384]{1,0:T(8,128)(2,1)} %bitcast.9), channel_id=1, source_target_pairs={{0,1},{1,0},{2,3},{3,2},{4,5},{5,4},{6,7},{7,6},{8,9},{9,8},{10,11... | collective-permute-start | bytes 4718600 | tf_op jit(solution)/shard_map/ppermute | solution.py:266
  1.1 7.7 %collective-permute-start.1 = (bf16[2048,384]{1,0:T(8,128)(2,1)}, bf16[2048,384]{1,0:T(8,128)(2,1)S(1)}, u32[]{:S(2)}, u32[]{:S(2)}) collective-permute-start(bf16[2048,384]{1,0:T(8,128)(2,1)} %bitcast.15), channel_id=1, source_target_pairs={{0,1},{1,0},{2,3},{3,2},{4,5},{5,4},{6,7},{7,6},{8,9},{9,8},{10,11... | collective-permute-start | bytes 4718600 | tf_op jit(solution)/shard_map/ppermute | solution.py:266
  1.2 10.6 %collective-permute-start.2 = (bf16[384,2048]{1,0:T(8,128)(2,1)}, bf16[384,2048]{1,0:T(8,128)(2,1)}, u32[]{:S(2)}, u32[]{:S(2)}) collective-permute-start(bf16[384,2048]{1,0:T(8,128)(2,1)} %bitcast.21), channel_id=1, source_target_pairs={{0,1},{1,0},{2,3},{3,2},{4,5},{5,4},{6,7},{7,6},{8,9},{9,8},{10,11... | collective-permute-start | bytes 4718600 | tf_op jit(solution)/shard_map/ppermute | solution.py:266
  3.8 16.7 %collective-permute-start.4 = (bf16[128,2176]{1,0:T(8,128)(2,1)}, bf16[128,2176]{1,0:T(8,128)(2,1)S(1)}, u32[]{:S(2)}, u32[]{:S(2)}) collective-permute-start(bf16[128,2176]{1,0:T(8,128)(2,1)} %pack.1.refs_0_), channel_id=1, source_target_pairs={{4,0},{8,4},{12,8},{14,12},{10,14},{6,10},{2,6},{0,2},{5,1},{9,5},... | collective-permute-start | bytes 1671176 | tf_op jit(solution)/shard_map/ppermute | solution.py:265
  6.4 15.7 %collective-permute-start.3 = (bf16[128,2176]{1,0:T(8,128)(2,1)}, bf16[128,2176]{1,0:T(8,128)(2,1)S(1)}, u32[]{:S(2)}, u32[]{:S(2)}) collective-permute-start(bf16[128,2176]{1,0:T(8,128)(2,1)} %pack.1.refs_0_), channel_id=1, source_target_pairs={{0,4},{4,8},{8,12},{12,14},{14,10},{10,6},{6,2},{2,0},{1,5},{5,9},... | collective-permute-start | bytes 1671176 | tf_op jit(solution)/shard_map/ppermute | solution.py:264
  6.5 5.4 %copy-start = (bf16[2048,384]{1,0:T(8,128)(2,1)}, bf16[2048,384]{1,0:T(8,128)(2,1)S(1)}, u32[]{:S(2)}) copy-start(bf16[2048,384]{1,0:T(8,128)(2,1)S(1)} %collective-permute-done.refs_5_.refs_7_) | copy-start | bytes 4718596
  6.5 24.9 %collective-permute-start.8 = (bf16[128,2048]{1,0:T(8,128)(2,1)}, bf16[128,2048]{1,0:T(8,128)(2,1)S(1)}, u32[]{:S(2)}, u32[]{:S(2)}) collective-permute-start(bf16[128,2048]{1,0:T(8,128)(2,1)} %refs_0_.3), channel_id=1, source_target_pairs={{4,0},{8,4},{12,8},{14,12},{10,14},{6,10},{2,6},{0,2},{5,1},{9,5},... | collective-permute-start | bytes 1572872 | tf_op jit(solution)/shard_map/ppermute | solution.py:265
  8.9 3.0 %copy-start.1 = (bf16[2048,384]{1,0:T(8,128)(2,1)}, bf16[2048,384]{1,0:T(8,128)(2,1)S(1)}, u32[]{:S(2)}) copy-start(bf16[2048,384]{1,0:T(8,128)(2,1)S(1)} %collective-permute-done.1.refs_6_.refs_8_) | copy-start | bytes 4718596
  8.9 24.4 %collective-permute-start.7 = (bf16[128,2048]{1,0:T(8,128)(2,1)}, bf16[128,2048]{1,0:T(8,128)(2,1)S(1)}, u32[]{:S(2)}, u32[]{:S(2)}) collective-permute-start(bf16[128,2048]{1,0:T(8,128)(2,1)} %refs_0_.3), channel_id=1, source_target_pairs={{0,4},{4,8},{8,12},{12,14},{14,10},{10,6},{6,2},{2,0},{1,5},{5,9},... | collective-permute-start | bytes 1572872 | tf_op jit(solution)/shard_map/ppermute | solution.py:264
  20.6 12.9 %copy-start.17 = (bf16[128,2176]{1,0:T(8,128)(2,1)}, bf16[128,2176]{1,0:T(8,128)(2,1)S(1)}, u32[]{:S(2)}) copy-start(bf16[128,2176]{1,0:T(8,128)(2,1)S(1)} %collective-permute-done.4.refs_1_.refs_2_) | copy-start | bytes 1671172
  22.1 11.4 %copy-start.18 = (bf16[128,2176]{1,0:T(8,128)(2,1)}, bf16[128,2176]{1,0:T(8,128)(2,1)S(1)}, u32[]{:S(2)}) copy-start(bf16[128,2176]{1,0:T(8,128)(2,1)S(1)} %collective-permute-done.3.refs_0_.refs_1_) | copy-start | bytes 1671172
  22.1 23.2 %collective-permute-start.5 = (bf16[128,2176]{1,0:T(8,128)(2,1)S(1)}, bf16[128,2176]{1,0:T(8,128)(2,1)S(1)}, u32[]{:S(2)}, u32[]{:S(2)}) collective-permute-start(bf16[128,2176]{1,0:T(8,128)(2,1)S(1)} %collective-permute-done.3.refs_0_.refs_1_), channel_id=1, source_target_pairs={{0,4},{4,8},{8,12},{12,14},{14,10},{10,6},{6,2},{2,0},{1,5},{5,9},... | collective-permute-start | bytes 1671176 | tf_op jit(solution)/shard_map/ppermute | solution.py:264
  22.2 23.0 %collective-permute-start.6 = (bf16[128,2176]{1,0:T(8,128)(2,1)S(1)}, bf16[128,2176]{1,0:T(8,128)(2,1)S(1)}, u32[]{:S(2)}, u32[]{:S(2)}) collective-permute-start(bf16[128,2176]{1,0:T(8,128)(2,1)S(1)} %collective-permute-done.4.refs_1_.refs_2_), channel_id=1, source_target_pairs={{4,0},{8,4},{12,8},{14,12},{10,14},{6,10},{2,6},{0,2},{5,1},{9,5},... | collective-permute-start | bytes 1671176 | tf_op jit(solution)/shard_map/ppermute | solution.py:265
  31.4 2.0 %copy-start.5 = (bf16[128,2048]{1,0:T(8,128)(2,1)}, bf16[128,2048]{1,0:T(8,128)(2,1)S(1)}, u32[]{:S(2)}) copy-start(bf16[128,2048]{1,0:T(8,128)(2,1)S(1)} %collective-permute-done.8.refs_3_.refs_2_) | copy-start | bytes 1572868
  31.4 23.2 %collective-permute-start.12 = (bf16[128,2048]{1,0:T(8,128)(2,1)S(1)}, bf16[128,2048]{1,0:T(8,128)(2,1)S(1)}, u32[]{:S(2)}, u32[]{:S(2)}) collective-permute-start(bf16[128,2048]{1,0:T(8,128)(2,1)S(1)} %collective-permute-done.8.refs_3_.refs_2_), channel_id=1, source_target_pairs={{4,0},{8,4},{12,8},{14,12},{10,14},{6,10},{2,6},{0,2},{5,1},{9,5},... | collective-permute-start | bytes 1572872 | tf_op jit(solution)/shard_map/ppermute | solution.py:265
  33.3 0.8 copy-start.6
  33.3 23.2 %collective-permute-start.11 = (bf16[128,2048]{1,0:T(8,128)(2,1)S(1)}, bf16[128,2048]{1,0:T(8,128)(2,1)S(1)}, u32[]{:S(2)}, u32[]{:S(2)}) collective-permute-start(bf16[128,2048]{1,0:T(8,128)(2,1)S(1)} %collective-permute-done.7.refs_2_.refs_1_), channel_id=1, source_target_pairs={{0,4},{4,8},{8,12},{12,14},{14,10},{10,6},{6,2},{2,0},{1,5},{5,9},... | collective-permute-start | bytes 1572872 | tf_op jit(solution)/shard_map/ppermute | solution.py:264
  45.2 11.5 %copy-start.19 = (bf16[128,2176]{1,0:T(8,128)(2,1)}, bf16[128,2176]{1,0:T(8,128)(2,1)S(1)}, u32[]{:S(2)}) copy-start(bf16[128,2176]{1,0:T(8,128)(2,1)S(1)} %collective-permute-done.5.refs_0_.refs_3_) | copy-start | bytes 1671172
  45.3 11.5 %copy-start.20 = (bf16[128,2176]{1,0:T(8,128)(2,1)}, bf16[128,2176]{1,0:T(8,128)(2,1)S(1)}, u32[]{:S(2)}) copy-start(bf16[128,2176]{1,0:T(8,128)(2,1)S(1)} %collective-permute-done.6.refs_1_.refs_4_) | copy-start | bytes 1671172
  45.3 23.2 %collective-permute-start.9 = (bf16[128,2176]{1,0:T(8,128)(2,1)S(1)}, bf16[128,2176]{1,0:T(8,128)(2,1)S(1)}, u32[]{:S(2)}, u32[]{:S(2)}) collective-permute-start(bf16[128,2176]{1,0:T(8,128)(2,1)S(1)} %collective-permute-done.5.refs_0_.refs_3_), channel_id=1, source_target_pairs={{0,4},{4,8},{8,12},{12,14},{14,10},{10,6},{6,2},{2,0},{1,5},{5,9},... | collective-permute-start | bytes 1671176 | tf_op jit(solution)/shard_map/ppermute | solution.py:264
  46.5 21.9 %collective-permute-start.10 = (bf16[128,2176]{1,0:T(8,128)(2,1)S(1)}, bf16[128,2176]{1,0:T(8,128)(2,1)S(1)}, u32[]{:S(2)}, u32[]{:S(2)}) collective-permute-start(bf16[128,2176]{1,0:T(8,128)(2,1)S(1)} %collective-permute-done.6.refs_1_.refs_4_), channel_id=1, source_target_pairs={{4,0},{8,4},{12,8},{14,12},{10,14},{6,10},{2,6},{0,2},{5,1},{9,5},... | collective-permute-start | bytes 1671176 | tf_op jit(solution)/shard_map/ppermute | solution.py:265
  54.6 2.2 %copy-start.7 = (bf16[128,2048]{1,0:T(8,128)(2,1)}, bf16[128,2048]{1,0:T(8,128)(2,1)S(1)}, u32[]{:S(2)}) copy-start(bf16[128,2048]{1,0:T(8,128)(2,1)S(1)} %collective-permute-done.12.refs_3_.refs_4_) | copy-start | bytes 1572868
  54.6 22.9 %collective-permute-start.15 = (bf16[128,2048]{1,0:T(8,128)(2,1)S(1)}, bf16[128,2048]{1,0:T(8,128)(2,1)S(1)}, u32[]{:S(2)}, u32[]{:S(2)}) collective-permute-start(bf16[128,2048]{1,0:T(8,128)(2,1)S(1)} %collective-permute-done.12.refs_3_.refs_4_), channel_id=1, source_target_pairs={{4,0},{8,4},{12,8},{14,12},{10,14},{6,10},{2,6},{0,2},{5,1},{9,5},... | collective-permute-start | bytes 1572872 | tf_op jit(solution)/shard_map/ppermute | solution.py:265
  56.5 0.8 copy-start.8
  56.5 23.2 %collective-permute-start.14 = (bf16[128,2048]{1,0:T(8,128)(2,1)S(1)}, bf16[128,2048]{1,0:T(8,128)(2,1)S(1)}, u32[]{:S(2)}, u32[]{:S(2)}) collective-permute-start(bf16[128,2048]{1,0:T(8,128)(2,1)S(1)} %collective-permute-done.11.refs_2_.refs_3_), channel_id=1, source_target_pairs={{0,4},{4,8},{8,12},{12,14},{14,10},{10,6},{6,2},{2,0},{1,5},{5,9},... | collective-permute-start | bytes 1572872 | tf_op jit(solution)/shard_map/ppermute | solution.py:264
  68.4 11.2 %copy-start.21 = (bf16[128,2176]{1,0:T(8,128)(2,1)}, bf16[128,2176]{1,0:T(8,128)(2,1)S(1)}, u32[]{:S(2)}) copy-start(bf16[128,2176]{1,0:T(8,128)(2,1)S(1)} %collective-permute-done.9.refs_0_.refs_5_) | copy-start | bytes 1671172
  68.4 11.2 %copy-start.22 = (bf16[128,2176]{1,0:T(8,128)(2,1)}, bf16[128,2176]{1,0:T(8,128)(2,1)S(1)}, u32[]{:S(2)}) copy-start(bf16[128,2176]{1,0:T(8,128)(2,1)S(1)} %collective-permute-done.10.refs_1_.refs_6_) | copy-start | bytes 1671172
  68.4 24.8 %collective-permute-start.13 = (bf16[128,2176]{1,0:T(8,128)(2,1)S(1)}, bf16[128,2176]{1,0:T(8,128)(2,1)S(1)}, u32[]{:S(2)}, u32[]{:S(2)}) collective-permute-start(bf16[128,2176]{1,0:T(8,128)(2,1)S(1)} %collective-permute-done.9.refs_0_.refs_5_), channel_id=1, source_target_pairs={{0,4},{4,8},{8,12},{12,14},{14,10},{10,6},{6,2},{2,0},{1,5},{5,9},... | collective-permute-start | bytes 1671176 | tf_op jit(solution)/shard_map/ppermute | solution.py:264
  77.5 2.2 %copy-start.9 = (bf16[128,2048]{1,0:T(8,128)(2,1)}, bf16[128,2048]{1,0:T(8,128)(2,1)S(1)}, u32[]{:S(2)}) copy-start(bf16[128,2048]{1,0:T(8,128)(2,1)S(1)} %collective-permute-done.15.refs_3_.refs_6_) | copy-start | bytes 1572868
  77.5 15.7 %collective-permute-start.16 = (bf16[128,2048]{1,0:T(8,128)(2,1)S(1)}, bf16[128,2048]{1,0:T(8,128)(2,1)S(1)}, u32[]{:S(2)}, u32[]{:S(2)}) collective-permute-start(bf16[128,2048]{1,0:T(8,128)(2,1)S(1)} %collective-permute-done.15.refs_3_.refs_6_), channel_id=1, source_target_pairs={{4,0},{8,4},{12,8},{14,12},{10,14},{6,10},{2,6},{0,2},{5,1},{9,5},... | collective-permute-start | bytes 1572872 | tf_op jit(solution)/shard_map/ppermute | solution.py:265
  79.7 0.8 copy-start.10
  93.2 0.8 copy-start.4
  94.0 0.8 copy-start.2
  104.8 10.3 %collective-permute-start.21 = (bf16[128,1024]{1,0:T(8,128)(2,1)S(1)}, bf16[128,1024]{1,0:T(8,128)(2,1)S(1)}, u32[]{:S(2)}, u32[]{:S(2)}) collective-permute-start(bf16[128,1024]{1,0:T(8,128)(2,1)S(1)} %get-tuple-element.86), channel_id=1, source_target_pairs={{0,4},{4,8},{8,12},{12,14},{14,10},{10,6},{6,2},{2,0},{1,5},{5,9},... | collective-permute-start | bytes 786440 | tf_op jit(solution)/shard_map/ppermute | solution.py:264
  105.2 9.8 %collective-permute-start.17 = (bf16[128,1024]{1,0:T(8,128)(2,1)S(1)}, bf16[128,1024]{1,0:T(8,128)(2,1)S(1)}, u32[]{:S(2)}, u32[]{:S(2)}) collective-permute-start(bf16[128,1024]{1,0:T(8,128)(2,1)S(1)} %get-tuple-element.87), channel_id=1, source_target_pairs={{4,0},{8,4},{12,8},{14,12},{10,14},{6,10},{2,6},{0,2},{5,1},{9,5},... | collective-permute-start | bytes 786440 | tf_op jit(solution)/shard_map/ppermute | solution.py:265
  106.9 20.7 %collective-permute-start.27 = (bf16[128,1024]{1,0:T(8,128)(2,1)S(1)}, bf16[128,1024]{1,0:T(8,128)(2,1)S(1)}, u32[]{:S(2)}, u32[]{:S(2)}) collective-permute-start(bf16[128,1024]{1,0:T(8,128)(2,1)S(1)} %get-tuple-element.84), channel_id=1, source_target_pairs={{0,4},{4,8},{8,12},{12,14},{14,10},{10,6},{6,2},{2,0},{1,5},{5,9},... | collective-permute-start | bytes 786440 | tf_op jit(solution)/shard_map/ppermute | solution.py:264
  107.3 20.3 %collective-permute-start.26 = (bf16[128,1024]{1,0:T(8,128)(2,1)S(1)}, bf16[128,1024]{1,0:T(8,128)(2,1)S(1)}, u32[]{:S(2)}, u32[]{:S(2)}) collective-permute-start(bf16[128,1024]{1,0:T(8,128)(2,1)S(1)} %get-tuple-element.85), channel_id=1, source_target_pairs={{4,0},{8,4},{12,8},{14,12},{10,14},{6,10},{2,6},{0,2},{5,1},{9,5},... | collective-permute-start | bytes 786440 | tf_op jit(solution)/shard_map/ppermute | solution.py:265
  109.0 6.1 %copy-start.3 = (f32[256,2048]{1,0:T(8,128)S(1)}, f32[256,2048]{1,0:T(8,128)}, u32[]{:S(2)}) copy-start(f32[256,2048]{1,0:T(8,128)} %get-tuple-element.51) | copy-start | bytes 6291460
  115.0 32.7 %collective-permute-start.25 = (bf16[384,2048]{1,0:T(8,128)(2,1)}, bf16[384,2048]{1,0:T(8,128)(2,1)S(1)}, u32[]{:S(2)}, u32[]{:S(2)}) collective-permute-start(bf16[384,2048]{1,0:T(8,128)(2,1)} %down_grads.2), channel_id=1, source_target_pairs={{0,1},{1,0},{2,3},{3,2},{4,5},{5,4},{6,7},{7,6},{8,9},{9,8},{10,11... | collective-permute-start | bytes 4718600 | tf_op jit(solution)/shard_map/ppermute | solution.py:266
  115.9 12.2 %collective-permute-start.22 = (bf16[128,1024]{1,0:T(8,128)(2,1)}, bf16[128,1024]{1,0:T(8,128)(2,1)S(1)}, u32[]{:S(2)}, u32[]{:S(2)}) collective-permute-start(bf16[128,1024]{1,0:T(8,128)(2,1)} %get-tuple-element.80), channel_id=1, source_target_pairs={{0,4},{4,8},{8,12},{12,14},{14,10},{10,6},{6,2},{2,0},{1,5},{5,9},... | collective-permute-start | bytes 786440 | tf_op jit(solution)/shard_map/ppermute | solution.py:264
  117.0 11.1 %copy-start.12 = (f32[256,2048]{1,0:T(8,128)S(1)}, f32[256,2048]{1,0:T(8,128)}, u32[]{:S(2)}) copy-start(f32[256,2048]{1,0:T(8,128)} %get-tuple-element.52) | copy-start | bytes 6291460
  117.0 11.1 %collective-permute-start.18 = (bf16[128,1024]{1,0:T(8,128)(2,1)S(1)}, bf16[128,1024]{1,0:T(8,128)(2,1)S(1)}, u32[]{:S(2)}, u32[]{:S(2)}) collective-permute-start(bf16[128,1024]{1,0:T(8,128)(2,1)S(1)} %get-tuple-element.81), channel_id=1, source_target_pairs={{4,0},{8,4},{12,8},{14,12},{10,14},{6,10},{2,6},{0,2},{5,1},{9,5},... | collective-permute-start | bytes 786440 | tf_op jit(solution)/shard_map/ppermute | solution.py:265
  127.6 28.6 %collective-permute-start.33 = (bf16[2048,384]{1,0:T(8,128)(2,1)}, bf16[2048,384]{1,0:T(8,128)(2,1)S(1)}, u32[]{:S(2)}, u32[]{:S(2)}) collective-permute-start(bf16[2048,384]{1,0:T(8,128)(2,1)} %get-tuple-element.65), channel_id=1, source_target_pairs={{0,1},{1,0},{2,3},{3,2},{4,5},{5,4},{6,7},{7,6},{8,9},{9,8},{10,11... | collective-permute-start | bytes 4718600 | tf_op jit(solution)/shard_map/ppermute | solution.py:266
  127.6 28.5 %collective-permute-start.32 = (bf16[2048,384]{1,0:T(8,128)(2,1)}, bf16[2048,384]{1,0:T(8,128)(2,1)S(1)}, u32[]{:S(2)}, u32[]{:S(2)}) collective-permute-start(bf16[2048,384]{1,0:T(8,128)(2,1)} %get-tuple-element.60), channel_id=1, source_target_pairs={{0,1},{1,0},{2,3},{3,2},{4,5},{5,4},{6,7},{7,6},{8,9},{9,8},{10,11... | collective-permute-start | bytes 4718600 | tf_op jit(solution)/shard_map/ppermute | solution.py:266
  128.1 17.1 %copy-start.11 = (f32[256,2048]{1,0:T(8,128)S(1)}, f32[256,2048]{1,0:T(8,128)}, u32[]{:S(2)}) copy-start(f32[256,2048]{1,0:T(8,128)} %get-tuple-element.53) | copy-start | bytes 6291460
  128.5 8.3 %collective-permute-start.29 = (bf16[128,1024]{1,0:T(8,128)(2,1)S(1)}, bf16[128,1024]{1,0:T(8,128)(2,1)S(1)}, u32[]{:S(2)}, u32[]{:S(2)}) collective-permute-start(bf16[128,1024]{1,0:T(8,128)(2,1)S(1)} %get-tuple-element.76), channel_id=1, source_target_pairs={{0,4},{4,8},{8,12},{12,14},{14,10},{10,6},{6,2},{2,0},{1,5},{5,9},... | collective-permute-start | bytes 786440 | tf_op jit(solution)/shard_map/ppermute | solution.py:264
  129.8 8.3 %collective-permute-start.28 = (bf16[128,1024]{1,0:T(8,128)(2,1)S(1)}, bf16[128,1024]{1,0:T(8,128)(2,1)S(1)}, u32[]{:S(2)}, u32[]{:S(2)}) collective-permute-start(bf16[128,1024]{1,0:T(8,128)(2,1)S(1)} %get-tuple-element.77), channel_id=1, source_target_pairs={{4,0},{8,4},{12,8},{14,12},{10,14},{6,10},{2,6},{0,2},{5,1},{9,5},... | collective-permute-start | bytes 786440 | tf_op jit(solution)/shard_map/ppermute | solution.py:265
  136.9 7.5 %collective-permute-start.23 = (bf16[128,1024]{1,0:T(8,128)(2,1)S(1)}, bf16[128,1024]{1,0:T(8,128)(2,1)S(1)}, u32[]{:S(2)}, u32[]{:S(2)}) collective-permute-start(bf16[128,1024]{1,0:T(8,128)(2,1)S(1)} %get-tuple-element.78), channel_id=1, source_target_pairs={{0,4},{4,8},{8,12},{12,14},{14,10},{10,6},{6,2},{2,0},{1,5},{5,9},... | collective-permute-start | bytes 786440 | tf_op jit(solution)/shard_map/ppermute | solution.py:264
  138.1 7.2 %collective-permute-start.19 = (bf16[128,1024]{1,0:T(8,128)(2,1)S(1)}, bf16[128,1024]{1,0:T(8,128)(2,1)S(1)}, u32[]{:S(2)}, u32[]{:S(2)}) collective-permute-start(bf16[128,1024]{1,0:T(8,128)(2,1)S(1)} %get-tuple-element.79), channel_id=1, source_target_pairs={{4,0},{8,4},{12,8},{14,12},{10,14},{6,10},{2,6},{0,2},{5,1},{9,5},... | collective-permute-start | bytes 786440 | tf_op jit(solution)/shard_map/ppermute | solution.py:265
  145.7 10.0 %collective-permute-start.24 = (bf16[128,1024]{1,0:T(8,128)(2,1)S(1)}, bf16[128,1024]{1,0:T(8,128)(2,1)S(1)}, u32[]{:S(2)}, u32[]{:S(2)}) collective-permute-start(bf16[128,1024]{1,0:T(8,128)(2,1)S(1)} %get-tuple-element.74), channel_id=1, source_target_pairs={{0,4},{4,8},{8,12},{12,14},{14,10},{10,6},{6,2},{2,0},{1,5},{5,9},... | collective-permute-start | bytes 786440 | tf_op jit(solution)/shard_map/ppermute | solution.py:264
  147.3 8.9 %collective-permute-start.20 = (bf16[128,1024]{1,0:T(8,128)(2,1)S(1)}, bf16[128,1024]{1,0:T(8,128)(2,1)S(1)}, u32[]{:S(2)}, u32[]{:S(2)}) collective-permute-start(bf16[128,1024]{1,0:T(8,128)(2,1)S(1)} %get-tuple-element.75), channel_id=1, source_target_pairs={{4,0},{8,4},{12,8},{14,12},{10,14},{6,10},{2,6},{0,2},{5,1},{9,5},... | collective-permute-start | bytes 786440 | tf_op jit(solution)/shard_map/ppermute | solution.py:265
  147.8 1.6 copy-start.15
  147.8 21.0 %collective-permute-start.31 = (bf16[128,1024]{1,0:T(8,128)(2,1)S(1)}, bf16[128,1024]{1,0:T(8,128)(2,1)S(1)}, u32[]{:S(2)}, u32[]{:S(2)}) collective-permute-start(bf16[128,1024]{1,0:T(8,128)(2,1)S(1)} %get-tuple-element.72), channel_id=1, source_target_pairs={{0,4},{4,8},{8,12},{12,14},{14,10},{10,6},{6,2},{2,0},{1,5},{5,9},... | collective-permute-start | bytes 786440 | tf_op jit(solution)/shard_map/ppermute | solution.py:264
  155.6 13.2 %copy-start.16 = (f32[128,2048]{1,0:T(8,128)S(1)}, f32[128,2048]{1,0:T(8,128)}, u32[]{:S(2)}) copy-start(f32[128,2048]{1,0:T(8,128)} %get-tuple-element.38) | copy-start | bytes 3145732
  155.7 13.2 %collective-permute-start.30 = (bf16[128,1024]{1,0:T(8,128)(2,1)S(1)}, bf16[128,1024]{1,0:T(8,128)(2,1)S(1)}, u32[]{:S(2)}, u32[]{:S(2)}) collective-permute-start(bf16[128,1024]{1,0:T(8,128)(2,1)S(1)} %get-tuple-element.73), channel_id=1, source_target_pairs={{4,0},{8,4},{12,8},{14,12},{10,14},{6,10},{2,6},{0,2},{5,1},{9,5},... | collective-permute-start | bytes 786440 | tf_op jit(solution)/shard_map/ppermute | solution.py:265
  156.2 1.1 copy-start.13
  157.3 1.2 copy-start.14

commit v2 on v1

--- a/solution.py
+++ b/solution.py
@@ -8,8 +8,9 @@
 from jax.sharding import PartitionSpec as P
 
 OVER_LAST = (((1,), (1,)), ((), ()))
-OVER_ROWS = (((0,), (0,)), ((), ()))
-VMEM_LIMIT = 56 * 1024 * 1024
+EXPERT_VMEM = 28 * 1024 * 1024
+GRADS_VMEM = 24 * 1024 * 1024
+CHEAP = pl.CostEstimate(flops=1024, bytes_accessed=1024, transcendentals=0)
 
 
 def ring_of(mesh):
@@ -74,40 +75,54 @@
 
 
 def expert_kernel(count, experts, *refs):
-    token_refs, cot_refs = refs[:count], refs[count : 2 * count]
-    sources = refs[2 * count : 2 * count + 6]
-    act_ref, grad_ref, held_tokens, held_cot = refs[2 * count + 6 : 2 * count + 10]
-    weights, arrived = refs[2 * count + 10 : 2 * count + 16], refs[2 * count + 16]
+    token_refs, cot_refs, sources = refs[:count], refs[count : 2 * count], refs[2 * count : 2 * count + 6]
+    rest = refs[2 * count + 6 :]
+    outs, rest = rest[: 5 + 2 * count], rest[5 + 2 * count :]
+    held_tokens, held_cot, *weights = rest[:8]
+    results, (arrived, left) = rest[8:-2], rest[-2:]
+    turned, act_refs, hidden_refs, grad_refs = results[0], results[1:3], results[3:5], results[5:]
     rows, width = cot_refs[0].shape
     lanes = token_refs[0].shape[1] - width
     hidden = weights[0].shape[1]
+    total = rows * count
     chip, core, cores = lax.axis_index("expert"), lax.axis_index("dp"), lax.axis_size("dp")
-    copies = [
-        pltpu.make_async_copy(sources[i], weights[i], arrived.at[i]) for i in range(len(sources))
-    ]
-    for copy in copies:
+    ins = []
+    for i in range(count):
+        ins.append((token_refs[i], held_tokens.at[pl.ds(i * rows, rows)]))
+    ins.append((sources[0], weights[0]))
+    ins.append((sources[1], weights[1]))
+    for i in range(count):
+        ins.append((cot_refs[i], held_cot.at[pl.ds(i * rows, rows)]))
+    ins += [(sources[i], weights[i]) for i in range(2, 6)]
+    copies = [pltpu.make_async_copy(src, dst, arrived.at[i]) for i, (src, dst) in enumerate(ins)]
+    soon = count + 2
+    for copy in copies[:soon]:
         copy.start()
-    for i in range(count):
-        held_tokens[pl.ds(i * rows, rows), :] = token_refs[i][:, :width]
-        held_cot[pl.ds(i * rows, rows), :] = cot_refs[i][...]
-    lane = lax.broadcasted_iota(jnp.int32, (rows, lanes), 1)
+    pending = iter(copies)
+
+    def wait(number):
+        for _ in range(number):
+            next(pending).wait()
+
+    sends = [pltpu.make_async_copy(results[i], outs[i], left.at[i]) for i in range(len(outs))]
+    lane = lax.broadcasted_iota(jnp.int32, (total, lanes), 1)
+    wait(count)
+    gate_terms = held_tokens[:, width:].astype(jnp.float32)
     grads = []
     for which in range(2):
         gate_w, up_w, down_w = weights[3 * which : 3 * which + 3]
         expert = chip * cores + (core if which == 0 else 1 - core)
         chosen = (lane == expert) | (lane == expert + experts) | (lane == expert + 2 * experts)
-        columns = [
-            jnp.sum(
-                jnp.where(chosen, ref[:, width:].astype(jnp.float32), 0.0), axis=1, keepdims=True
-            )
-            for ref in token_refs
-        ]
-        gate = columns[0] if count == 1 else jnp.concatenate(columns, axis=0)
-        copies[3 * which].wait()
-        gate_pre = jnp.dot(held_tokens[...], gate_w[...], preferred_element_type=jnp.float32)
-        copies[3 * which + 1].wait()
-        up_pre = jnp.dot(held_tokens[...], up_w[...], preferred_element_type=jnp.float32)
-        copies[3 * which + 2].wait()
+        gate = jnp.sum(jnp.where(chosen, gate_terms, 0.0), axis=1, keepdims=True)
+        rows_in = held_tokens[:, :width]
+        wait(1)
+        if which == 0:
+            for copy in copies[soon:]:
+                copy.start()
+        gate_pre = jnp.dot(rows_in, gate_w[...], preferred_element_type=jnp.float32)
+        wait(1)
+        up_pre = jnp.dot(rows_in, up_w[...], preferred_element_type=jnp.float32)
+        wait(1 + count if which == 0 else 1)
         back = lax.dot_general(held_cot[...], down_w[...], OVER_LAST, preferred_element_type=jnp.float32)
         sigma = jax.nn.sigmoid(gate_pre)
         active = gate_pre * sigma
@@ -115,147 +130,150 @@
         grad_up = (back * active).astype(jnp.bfloat16)
         grad_gate = (back * up_pre * sigma * (1.0 + gate_pre * (1.0 - sigma))).astype(jnp.bfloat16)
         scaled_hidden = (active * up_pre * gate).astype(jnp.bfloat16)
-        act_ref[:, pl.ds(3 * which * hidden, hidden)] = grad_gate
-        act_ref[:, pl.ds((3 * which + 1) * hidden, hidden)] = grad_up
-        act_ref[:, pl.ds((3 * which + 2) * hidden, hidden)] = scaled_hidden
+        act_refs[which][:, :hidden] = grad_gate
+        act_refs[which][:, hidden:] = grad_up
+        hidden_refs[which][...] = scaled_hidden.T
+        sends[1 + which].start()
+        sends[3 + which].start()
         grads += [(grad_gate, gate_w), (grad_up, up_w)]
     step = 512
-    for start in range(0, width, step):
-        total = None
-        for value, weight in grads:
-            part = lax.dot_general(
-                value, weight[pl.ds(start, step), :], OVER_LAST, preferred_element_type=jnp.float32
-            )
-            total = part if total is None else total + part
-        grad_ref[:, pl.ds(start, step)] = total
-
-
-def expert_batch(blocks, weights, experts):
+    cut = width // 2
+    for part in range(2):
+        for start in range(part * cut, part * cut + cut, step):
+            sums = None
+            for value, weight in grads:
+                term = lax.dot_general(
+                    value, weight[pl.ds(start, step), :], OVER_LAST, preferred_element_type=jnp.float32
+                )
+                sums = term if sums is None else sums + term
+            turned[pl.ds(start, step), :] = held_tokens[:, pl.ds(start, step)].T
+            for i in range(count):
+                ref = grad_refs[2 * i + part]
+                ref[:, pl.ds(start - part * cut, step)] = sums[i * rows : (i + 1) * rows].astype(ref.dtype)
+        for i in range(count):
+            sends[5 + 2 * i + part].start()
+    sends[0].start()
+    for send in sends:
+        send.wait()
+
+
+def expert_batch(blocks, weights, experts, grad_types):
     tokens, cots = zip(*blocks)
     rows, width = cots[0].shape
     hidden = weights[0].shape[1]
     total = rows * len(blocks)
-    vmem = pl.BlockSpec(memory_space=pltpu.VMEM)
-    return pl.pallas_call(
+    anywhere = pl.BlockSpec(memory_space=pl.ANY)
+    half = jnp.bfloat16
+    results = [((width, total), half)] + [((total, 2 * hidden), half)] * 2 + [((hidden, total), half)] * 2
+    results += [((rows, width // 2), kind) for kind in grad_types]
+    outs = pl.pallas_call(
         functools.partial(expert_kernel, len(blocks), experts),
-        in_specs=[vmem] * (2 * len(blocks)) + [pl.BlockSpec(memory_space=pl.ANY)] * 6,
-        out_specs=[vmem, vmem],
-        out_shape=[
-            jax.ShapeDtypeStruct((total, 6 * hidden), jnp.bfloat16),
-            jax.ShapeDtypeStruct((total, width), jnp.float32),
+        in_specs=[anywhere] * (2 * len(blocks) + 6),
+        out_specs=[anywhere] * len(results),
+        out_shape=[jax.ShapeDtypeStruct(shape, kind) for shape, kind in results],
+        scratch_shapes=[
+            pltpu.VMEM((total, tokens[0].shape[1]), half),
+            pltpu.VMEM((total, width), half),
+        ]
+        + [pltpu.VMEM(weight.shape, half) for weight in weights]
+        + [pltpu.VMEM(shape, kind) for shape, kind in results]
+        + [
+            pltpu.SemaphoreType.DMA((2 * len(blocks) + 6,)),
+            pltpu.SemaphoreType.DMA((len(results),)),
         ],
-        scratch_shapes=[pltpu.VMEM((total, width), jnp.bfloat16)] * 2
-        + [pltpu.VMEM(weight.shape, jnp.bfloat16) for weight in weights]
-        + [pltpu.SemaphoreType.DMA((6,))],
-        compiler_params=pltpu.CompilerParams(vmem_limit_bytes=VMEM_LIMIT),
-        cost_estimate=pl.CostEstimate(
-            flops=2 * 5 * total * 2 * hidden * width,
-            bytes_accessed=12 * hidden * width + total * (8 * width + 12 * hidden),
-            transcendentals=2 * total * hidden,
-        ),
+        compiler_params=pltpu.CompilerParams(vmem_limit_bytes=EXPERT_VMEM),
+        cost_estimate=CHEAP,
         name="expert_batch",
     )(*tokens, *cots, *weights)
-
-
-def row_grads_kernel(counts, add, *refs):
-    blocks, batches = counts
-    token_refs, act_refs = refs[:blocks], refs[blocks : blocks + batches]
-    rest = refs[blocks + batches :]
-    terms, (gate_ref, up_ref, acts) = rest[: 2 * add], rest[2 * add :]
-    hidden = gate_ref.shape[1]
+    return outs[0], outs[1:3], outs[3:5], outs[5:]
+
+
+def row_kernel(count, add, *refs):
+    turned_refs, act_refs, rest = refs[:count], refs[count : 2 * count], refs[2 * count :]
+    terms, outs, held = rest[:add], rest[add:-1], rest[-1]
 
     @pl.when(pl.program_id(0) == 0)
     def _():
         at = 0
         for ref in act_refs:
-            acts[pl.ds(at, ref.shape[0]), :] = ref[:, : 2 * hidden]
+            held[pl.ds(at, ref.shape[0]), :] = ref[...]
             at += ref.shape[0]
 
-    rows = jnp.concatenate([ref[...] for ref in token_refs], axis=0)
-    out = lax.dot_general(rows, acts[...], OVER_ROWS, preferred_element_type=jnp.float32)
-    for i, ref in enumerate((gate_ref, up_ref)):
-        value = out[:, i * hidden : (i + 1) * hidden]
+    tile = jnp.concatenate([ref[...] for ref in turned_refs], axis=1)
+    sums = jnp.dot(tile, held[...], preferred_element_type=jnp.float32)
+    at = 0
+    for i, ref in enumerate(outs):
+        value = sums[:, at : at + ref.shape[1]]
+        at += ref.shape[1]
         if add:
             value = value + terms[i][...].astype(jnp.float32)
         ref[...] = value.astype(jnp.bfloat16)
 
 
-def row_grads(which, tokens, acts, width, terms=()):
-    rows = tokens[0].shape[0]
-    hidden = acts[0].shape[1] // 6
-    total = rows * len(tokens)
-    tile = 256
+def row_grads(turned, acts, terms=()):
+    width = turned[0].shape[0]
+    hidden = acts[0].shape[1] // 2
+    total = sum(act.shape[0] for act in acts)
+    tile = 512
     out_spec = pl.BlockSpec((tile, hidden), lambda j: (j, 0))
     return pl.pallas_call(
-        functools.partial(row_grads_kernel, (len(tokens), len(acts)), len(terms) // 2),
+        functools.partial(row_kernel, len(acts), len(terms)),
         grid=(width // tile,),
-        in_specs=[pl.BlockSpec((rows, tile), lambda j: (0, j))] * len(tokens)
-        + [pl.BlockSpec((act.shape[0], 3 * hidden), lambda j: (0, which)) for act in acts]
+        in_specs=[pl.BlockSpec((tile, part.shape[1]), lambda j: (j, 0)) for part in turned]
+        + [pl.BlockSpec(act.shape, lambda j: (0, 0)) for act in acts]
         + [out_spec] * len(terms),
         out_specs=[out_spec] * 2,
         out_shape=[jax.ShapeDtypeStruct((width, hidden), jnp.bfloat16)] * 2,
         scratch_shapes=[pltpu.VMEM((total, 2 * hidden), jnp.bfloat16)],
-        compiler_params=pltpu.CompilerParams(vmem_limit_bytes=VMEM_LIMIT),
-        cost_estimate=pl.CostEstimate(
-            flops=2 * total * width * 2 * hidden,
-            bytes_accessed=2 * total * (width + 2 * hidden) + 8 * width * hidden,
-            transcendentals=0,
-        ),
+        compiler_params=pltpu.CompilerParams(vmem_limit_bytes=GRADS_VMEM),
+        cost_estimate=CHEAP,
         name="row_grads",
-    )(*tokens, *acts, *terms)
-
-
-def down_grads_kernel(counts, add, *refs):
-    blocks, batches = counts
-    cot_refs, act_refs = refs[:blocks], refs[blocks : blocks + batches]
-    rest = refs[blocks + batches :]
-    terms, (down_ref, acts) = rest[:add], rest[add:]
-    hidden = down_ref.shape[0]
+    )(*turned, *acts, *terms)
+
+
+def down_kernel(count, blocks, add, *refs):
+    hidden_refs, cot_refs, rest = refs[:count], refs[count : count + blocks], refs[count + blocks :]
+    terms, down_ref, held = rest[:add], rest[add], rest[-1]
 
     @pl.when(pl.program_id(0) == 0)
     def _():
         at = 0
-        for ref in act_refs:
-            acts[:, pl.ds(at, ref.shape[0])] = ref[...].T
-            at += ref.shape[0]
-
-    rows = jnp.concatenate([ref[...] for ref in cot_refs], axis=0)
-    out = jnp.dot(acts[...], rows, preferred_element_type=jnp.float32)
+        for ref in hidden_refs:
+            held[:, pl.ds(at, ref.shape[1])] = ref[...]
+            at += ref.shape[1]
+
+    tile = jnp.concatenate([ref[...] for ref in cot_refs], axis=0)
+    sums = jnp.dot(held[...], tile, preferred_element_type=jnp.float32)
     for term in terms:
-        out = out + term[...].astype(jnp.float32)
-    down_ref[...] = out.astype(jnp.bfloat16)
-
-
-def down_grads(which, cots, acts, terms=()):
+        sums = sums + term[...].astype(jnp.float32)
+    down_ref[...] = sums.astype(jnp.bfloat16)
+
+
+def down_grads(hiddens, cots, terms=()):
     rows, width = cots[0].shape
-    hidden = acts[0].shape[1] // 6
+    hidden = hiddens[0].shape[0]
     total = rows * len(cots)
     tile = 512
     out_spec = pl.BlockSpec((hidden, tile), lambda j: (0, j))
     return pl.pallas_call(
-        functools.partial(down_grads_kernel, (len(cots), len(acts)), len(terms)),
+        functools.partial(down_kernel, len(hiddens), len(cots), len(terms)),
         grid=(width // tile,),
-        in_specs=[pl.BlockSpec((rows, tile), lambda j: (0, j))] * len(cots)
-        + [pl.BlockSpec((act.shape[0], hidden), lambda j: (0, 3 * which + 2)) for act in acts]
+        in_specs=[pl.BlockSpec(part.shape, lambda j: (0, 0)) for part in hiddens]
+        + [pl.BlockSpec((rows, tile), lambda j: (0, j))] * len(cots)
         + [out_spec] * len(terms),
         out_specs=out_spec,
         out_shape=jax.ShapeDtypeStruct((hidden, width), jnp.bfloat16),
         scratch_shapes=[pltpu.VMEM((hidden, total), jnp.bfloat16)],
-        compiler_params=pltpu.CompilerParams(vmem_limit_bytes=VMEM_LIMIT),
-        cost_estimate=pl.CostEstimate(
-            flops=2 * total * width * hidden,
-            bytes_accessed=2 * total * (width + hidden) + 4 * width * hidden,
-            transcendentals=0,
-        ),
+        compiler_params=pltpu.CompilerParams(vmem_limit_bytes=GRADS_VMEM),
+        cost_estimate=CHEAP,
         name="down_grads",
-    )(*cots, *acts, *terms)
+    )(*hiddens, *cots, *terms)
 
 
 def ring_local(ring, tokens, cotangent, routes, gates, helper, w_gate, w_up, w_down):
-    rows, width = tokens.shape
     experts = helper.shape[0]
     chips, cores = lax.axis_size("expert"), lax.axis_size("dp")
-    route_cap = 2 * rows * routes.shape[1] // (chips * cores)
+    route_cap = 2 * tokens.shape[0] * routes.shape[1] // (chips * cores)
     home_cap = route_cap - 3 * route_cap // 8
     reach = chips // 2
     up_pairs = [(ring[i], ring[(i + 1) % chips]) for i in range(chips)]
@@ -265,81 +283,90 @@
     down = lambda value: lax.ppermute(value, "expert", down_pairs)
     other = lambda value: lax.ppermute(value, "dp", swap)
     tied = lax.optimization_barrier
+    wide, half = jnp.float32, jnp.bfloat16
 
     packed = pack(tokens, routes, gates, helper, home_cap)
-    own = (w_gate[0], w_up[0], w_down[0])
+    packed, own = tied((packed, (w_gate[0], w_up[0], w_down[0])))
     weights = own + tuple(other(value) for value in own)
-    act, own_grad = expert_batch([(packed, cotangent)], weights, experts)
-    row_blocks, cot_blocks, acts = [packed], [cotangent], [act]
-    grads_below, grads_above = [], []
+    turned, acts, hiddens, cots = [], [], [], []
+
+    def batch(blocks, grad_types):
+        turn, act, hid, grads = expert_batch(blocks, weights, experts, grad_types)
+        turned.append(turn)
+        acts.append(act)
+        hiddens.append(hid)
+        cots.extend(cot for _, cot in blocks)
+        return grads
+
+    own_low, own_high = batch([(packed, cotangent)], (wide, wide))
+    below_low, below_high, above_low, above_high = [], [], [], []
     tok_b = tok_a = packed
     cot_b = cot_a = cotangent
     for s in range(1, reach):
         cot_b, cot_a = up(cot_b), down(cot_a)
         tok_b, tok_a = up(tok_b), down(tok_a)
-        tok_b, tok_a, acts[-1] = tied((tok_b, tok_a, acts[-1]))
-        act, grad = expert_batch(((tok_b, cot_b), (tok_a, cot_a)), weights, experts)
-        row_blocks += (tok_b, tok_a)
-        cot_blocks += (cot_b, cot_a)
-        acts.append(act)
-        grads_below.insert(0, grad[:rows])
-        grads_above.insert(0, grad[rows:])
-
-    cut = width // 2
-    low = lambda value: value[:, :cut]
-    high = lambda value: value[:, cut:]
-    half = lambda value: value.astype(jnp.bfloat16)
-    plus = lambda value, term: half(value.astype(jnp.float32) + term)
-
+        tok_b, tok_a, turned[-1] = tied((tok_b, tok_a, turned[-1]))
+        last = half if s == reach - 1 else wide
+        parts = batch([(tok_b, cot_b), (tok_a, cot_a)], (wide, last, last, wide))
+        for store, part in zip((below_low, below_high, above_low, above_high), parts):
+            store.insert(0, part)
+
+    plus = lambda value, term: (value.astype(wide) + term).astype(half)
     far_cot, far_tok = down(cot_a), up(tok_b)
-    high_down, low_up = down(half(high(grads_below[0]))), up(half(low(grads_above[0])))
-    far_tok, acts[-1] = tied((far_tok, acts[-1]))
-    act, far_grad = expert_batch([(far_tok, far_cot)], weights, experts)
-    row_blocks.append(far_tok)
-    cot_blocks.append(far_cot)
-    acts.append(act)
-    low_down, high_up = down(half(low(far_grad))), up(half(high(far_grad)))
+    high_down, low_up = down(below_high[0]), up(above_low[0])
+    far_tok, turned[-1] = tied((far_tok, turned[-1]))
+    far_low, far_high = batch([(far_tok, far_cot)], (half, half))
+    low_down, high_up = down(far_low), up(far_high)
 
     sent, out = {}, {}
 
     def far_rows():
-        parts = row_grads(1, row_blocks, acts, width)
+        parts = row_grads(turned, [act[1] for act in acts])
         sent["gate"], sent["up"] = (other(part) for part in parts)
         return parts[0]
 
     def far_down():
-        part = down_grads(1, cot_blocks, acts)
+        part = down_grads([hid[1] for hid in hiddens], cots)
         sent["down"] = other(part)
         return part
 
     def own_rows():
         terms = (sent["gate"], sent["up"])
-        out["gate"], out["up"] = row_grads(0, row_blocks, acts, width, terms)
+        out["gate"], out["up"] = row_grads(turned, [act[0] for act in acts], terms)
         return out["gate"]
 
     def own_down():
-        out["down"] = down_grads(0, cot_blocks, acts, (sent["down"],))
+        out["down"] = down_grads([hid[0] for hid in hiddens], cots, (sent["down"],))
         return out["down"]
 
     chores = [far_rows, far_down, own_rows, own_down]
+
+    def before_chore(first, second):
+        first, second, turned[-1], cots[-1] = tied((first, second, turned[-1], cots[-1]))
+        return first, second
+
+    def after_chore(first, second):
+        first, second, _ = tied((first, second, chores.pop(0)()))
+        return first, second
+
     for s in range(reach - 1):
-        if chores:
-            high_down, low_up, _ = tied((high_down, low_up, chores.pop(0)()))
         if s + 1 < reach - 1:
-            high_down = down(plus(high_down, high(grads_below[s + 1])))
-            low_up = up(plus(low_up, low(grads_above[s + 1])))
-        low_down = down(plus(low_down, low(grads_below[s])))
-        high_up = up(plus(high_up, high(grads_above[s])))
-    for chore in chores:
-        chore()
-
-    def three(mine, first, second):
-        return half(mine + first.astype(jnp.float32) + second.astype(jnp.float32))
-
-    low_down, high_up, out["down"] = tied((low_down, high_up, out["down"]))
-    grad_tokens = jnp.concatenate(
-        [three(low(own_grad), low_down, low_up), three(high(own_grad), high_down, high_up)], axis=1
-    )
+            high_down, low_up = plus(high_down, below_high[s + 1]), plus(low_up, above_low[s + 1])
+            high_down, low_up = before_chore(high_down, low_up)
+            high_down, low_up = down(high_down), up(low_up)
+        if s != 1 and chores:
+            low_down, high_up = after_chore(low_down, high_up)
+        low_down, high_up = plus(low_down, below_low[s]), plus(high_up, above_high[s])
+        low_down, high_up = before_chore(low_down, high_up)
+        low_down, high_up = down(low_down), up(high_up)
+        if s == 0 and chores:
+            high_down, low_up = after_chore(high_down, low_up)
+    while chores:
+        low_down, high_up = after_chore(low_down, high_up)
+
+    grad_low = (own_low + low_down.astype(wide) + low_up.astype(wide)).astype(half)
+    grad_high = (own_high + high_down.astype(wide) + high_up.astype(wide)).astype(half)
+    grad_tokens = jnp.concatenate([grad_low, grad_high], axis=1)
     return (grad_tokens, out["gate"][None], out["up"][None], out["down"][None])
 
 

time: 171 us -> 145 us (0.85)
  Pallas kernels: 84.7 us -> 61.3 us
  other arithmetic: 5.66 us -> 1.58 us
  waiting for transfers between devices: 38 us -> 41.4 us
    pallas_call x4, Pallas kernels: 32.3 us -> 15.9 us  [the longest x2 9.11 us: row_grads(): pl.pallas_call(functools.partial(row_kernel, len(acts), len(terms)), grid...]
    ppermute x14, starting transfers between devices: 19.3 us -> 8.92 us  [ring_local(): down = lambda value: lax.ppermute(value, 'expert', down_pairs)]
    ppermute x14, starting transfers between devices: 13.8 us -> 23.6 us  [ring_local(): up = lambda value: lax.ppermute(value, 'expert', up_pairs)]
    pallas_call x5, Pallas kernels: 50.2 us -> 43.2 us  [expert_batch(): pl.pallas_call(functools.partial(expert_kernel, len(blocks), experts), in...]
    ppermute x14, waiting for transfers between devices: 23.3 us -> 29.2 us  [ring_local(): down = lambda value: lax.ppermute(value, 'expert', down_pairs)]
    another operation x2 -> x0, other arithmetic: 3.02 us -> none
    ppermute x14, waiting for transfers between devices: 14.1 us -> 12.1 us  [ring_local(): up = lambda value: lax.ppermute(value, 'expert', up_pairs)]
    unnamed x46 -> x18, local copies, waits for them, and re-layouts: 5.87 us -> 6.34 us
  transfers between devices with their start and end apart: 34 -> 34, of which waited for: 11 -> 16; matrix products, arithmetic and copies ran while one was open for 2% -> 0% of each run, Pallas kernels for 45% -> 41%
where the time goes in v2:
time: 145 us
  Pallas kernels  61.3 us (42%)
  waiting for transfers between devices  41.4 us (29%)
  starting transfers between devices  33.6 us (23%)
  local copies, waits for them, and re-layouts  6.34 us (4%)
  other arithmetic  1.58 us (1%)
    pallas_call x5, Pallas kernels, expert_batch(): pl.pallas_call(functools.partial(expert_kernel, len(blocks), experts), in...  43.2 us
    ppermute x14, waiting for transfers between devices, ring_local(): down = lambda value: lax.ppermute(value, 'expert', down_pairs)  29.2 us
    ppermute x14, starting transfers between devices, ring_local(): up = lambda value: lax.ppermute(value, 'expert', up_pairs)  23.6 us
    ppermute x14, waiting for transfers between devices, ring_local(): up = lambda value: lax.ppermute(value, 'expert', up_pairs)  12.1 us
    pallas_call x2, Pallas kernels, row_grads(): pl.pallas_call(functools.partial(row_kernel, len(acts), len(terms)), grid...  9.11 us
    ppermute x14, starting transfers between devices, ring_local(): down = lambda value: lax.ppermute(value, 'expert', down_pairs)  8.92 us
    pallas_call x2, Pallas kernels, down_grads(): pl.pallas_call(functools.partial(down_kernel, len(hiddens), len(cots), le...  6.8 us
    unnamed x18, local copies, waits for them, and re-layouts  6.34 us
  transfers between devices with their start and end apart: 34, of which 16 were waited for; matrix products, arithmetic and copies ran while one was open for 0% of the time, Pallas kernels for 41%

profile of v2, /device:TPU:0, one launch (start us, length us, event | category | flops | bytes accessed | tf_op | source)
XLA Modules:
  0.0 145.2 jit_solution(13010406120887655581)
XLA Ops:
  0.6 2.2 %pack.1.refs_0_ = bf16[128,2176]{1,0:T(8,128)(2,1)} custom-call(s32[4,128]{1,0:T(4,128)} %bitcast.28, f32[4,128]{1,0:T(4,128)} %bitcast.29, s32[1,16]{1,0:T(1,128)} %bitcast.30, bf16[128,2048]{1,0:T(8,128)(2,1)} %tokens_ref.1), custom_call_target="tpu_custom_call" | custom-call | tf_op jit(solution)/shard_map/pack/pallas_call | solution.py:70
  2.8 0.5 collective-permute-start
  3.2 0.1 collective-permute-start.1
  3.3 0.5 collective-permute-start.2
  3.8 2.6 %collective-permute-start.3 = (bf16[128,2176]{1,0:T(8,128)(2,1)}, bf16[128,2176]{1,0:T(8,128)(2,1)S(1)}, u32[]{:S(2)}, u32[]{:S(2)}) collective-permute-start(bf16[128,2176]{1,0:T(8,128)(2,1)} %pack.1.refs_0_), channel_id=1, source_target_pairs={{0,4},{4,8},{8,12},{12,14},{14,10},{10,6},{6,2},{2,0},{1,5},{5,9},... | collective-permute-start | bytes 1671176 | tf_op jit(solution)/shard_map/ppermute | solution.py:282
  6.3 0.2 collective-permute-done.refs_5_.refs_7_
  6.5 2.9 %collective-permute-start.8 = (bf16[128,2048]{1,0:T(8,128)(2,1)}, bf16[128,2048]{1,0:T(8,128)(2,1)S(1)}, u32[]{:S(2)}, u32[]{:S(2)}) collective-permute-start(bf16[128,2048]{1,0:T(8,128)(2,1)} %refs_5_.3), channel_id=1, source_target_pairs={{4,0},{8,4},{12,8},{14,12},{10,14},{6,10},{2,6},{0,2},{5,1},{9,5},... | collective-permute-start | bytes 1572872 | tf_op jit(solution)/shard_map/ppermute | solution.py:283
  9.4 2.3 %collective-permute-start.7 = (bf16[128,2048]{1,0:T(8,128)(2,1)}, bf16[128,2048]{1,0:T(8,128)(2,1)S(1)}, u32[]{:S(2)}, u32[]{:S(2)}) collective-permute-start(bf16[128,2048]{1,0:T(8,128)(2,1)} %refs_5_.3), channel_id=1, source_target_pairs={{0,4},{4,8},{8,12},{12,14},{14,10},{10,6},{6,2},{2,0},{1,5},{5,9},... | collective-permute-start | bytes 1572872 | tf_op jit(solution)/shard_map/ppermute | solution.py:282
  11.7 1.4 copy-done
  13.1 1.4 copy-done.2
  14.5 1.4 copy-done.4
  15.9 1.0 copy-done.6
  17.0 1.1 copy-done.8
  18.0 7.4 %expert_batch.5 = (bf16[2048,128]{1,0:T(8,128)(2,1)S(1)}, bf16[128,768]{1,0:T(8,128)(2,1)S(1)}, bf16[128,768]{1,0:T(8,128)(2,1)S(1)}, bf16[384,128]{1,0:T(8,128)...) custom-call(bf16[128,2176]{1,0:T(8,128)(2,1)S(1)} %copy-done.8, ...), custom_call_target="tpu_custom_call" | custom-call | flops 1024 | bytes 1024 | tf_op jit(solution)/shard_map/expert_batch/pallas_call | solution.py:169
  25.5 2.3 %collective-permute-start.5 = (bf16[128,2176]{1,0:T(8,128)(2,1)S(1)}, bf16[128,2176]{1,0:T(8,128)(2,1)S(1)}, u32[]{:S(2)}, u32[]{:S(2)}) collective-permute-start(bf16[128,2176]{1,0:T(8,128)(2,1)S(1)} %collective-permute-done.3.refs_0_), channel_id=1, source_target_pairs={{0,4},{4,8},{8,12},{12,14},{14,10},{10,6},{6,2},{2,0},{1,5},{5,9},... | collective-permute-start | bytes 1671176 | tf_op jit(solution)/shard_map/ppermute | solution.py:282
  27.8 5.5 %collective-permute-done.8.refs_3_.refs_7_ = bf16[128,2048]{1,0:T(8,128)(2,1)S(1)} collective-permute-done((bf16[128,2048]{1,0:T(8,128)(2,1)}, bf16[128,2048]{1,0:T(8,128)(2,1)S(1)}, u32[]{:S(2)}, u32[]{:S(2)}) %collective-permute-start.8) | collective-permute-done | bytes 524320 | tf_op jit(solution)/shard_map/ppermute | solution.py:283
  33.2 2.0 %collective-permute-start.11 = (bf16[128,2048]{1,0:T(8,128)(2,1)S(1)}, bf16[128,2048]{1,0:T(8,128)(2,1)S(1)}, u32[]{:S(2)}, u32[]{:S(2)}) collective-permute-start(bf16[128,2048]{1,0:T(8,128)(2,1)S(1)} %collective-permute-done.7.refs_2_.refs_6_), channel_id=1, source_target_pairs={{0,4},{4,8},{8,12},{12,14},{14,10},{10,6},{6,2},{2,0},{1,5},{5,9},... | collective-permute-start | bytes 1572872 | tf_op jit(solution)/shard_map/ppermute | solution.py:282
  35.3 9.5 %expert_batch.6 = (bf16[2048,256]{1,0:T(8,128)(2,1)S(1)}, bf16[256,768]{1,0:T(8,128)(2,1)S(1)}, bf16[256,768]{1,0:T(8,128)(2,1)S(1)}, bf16[384,256]{1,0:T(8,128)...) custom-call(bf16[128,2176]{1,0:T(8,128)(2,1)S(1)} %collective-permut, ...), custom_call_target="tpu_custom_call" | custom-call | flops 1024 | bytes 1024 | tf_op jit(solution)/shard_map/expert_batch/pallas_call | solution.py:169
  44.8 0.4 collective-permute-done.6.refs_1_
  45.2 2.0 %collective-permute-start.9 = (bf16[128,2176]{1,0:T(8,128)(2,1)S(1)}, bf16[128,2176]{1,0:T(8,128)(2,1)S(1)}, u32[]{:S(2)}, u32[]{:S(2)}) collective-permute-start(bf16[128,2176]{1,0:T(8,128)(2,1)S(1)} %collective-permute-done.5.refs_0_), channel_id=1, source_target_pairs={{0,4},{4,8},{8,12},{12,14},{14,10},{10,6},{6,2},{2,0},{1,5},{5,9},... | collective-permute-start | bytes 1671176 | tf_op jit(solution)/shard_map/ppermute | solution.py:282
  47.2 9.2 %collective-permute-done.12.refs_3_.refs_9_ = bf16[128,2048]{1,0:T(8,128)(2,1)S(1)} collective-permute-done((bf16[128,2048]{1,0:T(8,128)(2,1)S(1)}, bf16[128,2048]{1,0:T(8,128)(2,1)S(1)}, u32[]{:S(2)}, u32[]{:S(2)}) %collective-permute-start.12) | collective-permute-done | bytes 524320 | tf_op jit(solution)/shard_map/ppermute | solution.py:283
  56.4 2.0 %collective-permute-start.14 = (bf16[128,2048]{1,0:T(8,128)(2,1)S(1)}, bf16[128,2048]{1,0:T(8,128)(2,1)S(1)}, u32[]{:S(2)}, u32[]{:S(2)}) collective-permute-start(bf16[128,2048]{1,0:T(8,128)(2,1)S(1)} %collective-permute-done.11.refs_2_.refs_8_), channel_id=1, source_target_pairs={{0,4},{4,8},{8,12},{12,14},{14,10},{10,6},{6,2},{2,0},{1,5},{5,9},... | collective-permute-start | bytes 1572872 | tf_op jit(solution)/shard_map/ppermute | solution.py:282
  58.4 9.5 %expert_batch.7 = (bf16[2048,256]{1,0:T(8,128)(2,1)S(1)}, bf16[256,768]{1,0:T(8,128)(2,1)S(1)}, bf16[256,768]{1,0:T(8,128)(2,1)S(1)}, bf16[384,256]{1,0:T(8,128)...) custom-call(bf16[128,2176]{1,0:T(8,128)(2,1)S(1)} %collective-permut, ...), custom_call_target="tpu_custom_call" | custom-call | flops 1024 | bytes 1024 | tf_op jit(solution)/shard_map/expert_batch/pallas_call | solution.py:169
  67.9 0.4 collective-permute-done.10.refs_1_
  68.4 1.6 %collective-permute-start.13 = (bf16[128,2176]{1,0:T(8,128)(2,1)S(1)}, bf16[128,2176]{1,0:T(8,128)(2,1)S(1)}, u32[]{:S(2)}, u32[]{:S(2)}) collective-permute-start(bf16[128,2176]{1,0:T(8,128)(2,1)S(1)} %collective-permute-done.9.refs_0_), channel_id=1, source_target_pairs={{0,4},{4,8},{8,12},{12,14},{14,10},{10,6},{6,2},{2,0},{1,5},{5,9},... | collective-permute-start | bytes 1671176 | tf_op jit(solution)/shard_map/ppermute | solution.py:282
  69.9 9.0 %collective-permute-done.15.refs_3_.refs_11_ = bf16[128,2048]{1,0:T(8,128)(2,1)S(1)} collective-permute-done((bf16[128,2048]{1,0:T(8,128)(2,1)S(1)}, bf16[128,2048]{1,0:T(8,128)(2,1)S(1)}, u32[]{:S(2)}, u32[]{:S(2)}) %collective-permute-start.15) | collective-permute-done | bytes 524320 | tf_op jit(solution)/shard_map/ppermute | solution.py:283
  78.9 0.3 collective-permute-start.16
  79.2 9.4 %expert_batch.8 = (bf16[2048,256]{1,0:T(8,128)(2,1)S(1)}, bf16[256,768]{1,0:T(8,128)(2,1)S(1)}, bf16[256,768]{1,0:T(8,128)(2,1)S(1)}, bf16[384,256]{1,0:T(8,128)...) custom-call(bf16[128,2176]{1,0:T(8,128)(2,1)S(1)} %collective-permut, ...), custom_call_target="tpu_custom_call" | custom-call | flops 1024 | bytes 1024 | tf_op jit(solution)/shard_map/expert_batch/pallas_call | solution.py:169
  88.7 1.8 %collective-permute-start.20 = (bf16[128,1024]{1,0:T(8,128)(2,1)S(1)}, bf16[128,1024]{1,0:T(8,128)(2,1)S(1)}, u32[]{:S(2)}, u32[]{:S(2)}) collective-permute-start(bf16[128,1024]{1,0:T(8,128)(2,1)S(1)} %get-tuple-element.115), channel_id=1, source_target_pairs={{0,4},{4,8},{8,12},{12,14},{14,10},{10,6},{6,2},{2,0},{1,5},{5,9},... | collective-permute-start | bytes 786440 | tf_op jit(solution)/shard_map/ppermute | solution.py:282
  90.4 0.3 collective-permute-start.19
  90.7 1.6 %collective-permute-done.16.refs_1_.refs_12_ = bf16[128,2048]{1,0:T(8,128)(2,1)S(1)} collective-permute-done((bf16[128,2048]{1,0:T(8,128)(2,1)S(1)}, bf16[128,2048]{1,0:T(8,128)(2,1)S(1)}, u32[]{:S(2)}, u32[]{:S(2)}) %collective-permute-start.16) | collective-permute-done | bytes 524320 | tf_op jit(solution)/shard_map/ppermute | solution.py:283
  92.3 7.4 %expert_batch.9 = (bf16[2048,128]{1,0:T(8,128)(2,1)S(1)}, bf16[128,768]{1,0:T(8,128)(2,1)S(1)}, bf16[128,768]{1,0:T(8,128)(2,1)S(1)}, bf16[384,128]{1,0:T(8,128)...) custom-call(bf16[128,2176]{1,0:T(8,128)(2,1)S(1)} %collective-permute-done.13., ...), custom_call_target="tpu_custom_call" | custom-call | flops 1024 | bytes 1024 | tf_op jit(solution)/shard_map/expert_batch/pallas_call | solution.py:169
  99.7 0.7 collective-permute-start.17
  100.4 1.4 collective-permute-start.18
  101.9 0.7 collective-permute-start.23
  102.6 1.4 collective-permute-start.24
  104.0 4.1 %row_grads.2 = (bf16[2048,384]{1,0:T(8,128)(2,1)S(1)}, bf16[2048,384]{1,0:T(8,128)(2,1)S(1)}) custom-call(bf16[2048,128]{1,0:T(8,128)(2,1)S(1)} %get-tuple-element.109.refs_0_, bf16[2048,256]{1,0:T(8,128)(2,1)S(1)} %get-tuple-element.110.refs_1_, bf16[2048,256]{1,0:T(8,128)(2,1)S(1)} %get-tuple-element.111.refs_2_, ...), custom_call_target="tpu_custom_call" | custom-call | flops 1024 | bytes 1024 | tf_op jit(solution)/shard_map/row_grads/pallas_call | solution.py:219
  108.1 0.1 collective-permute-start.27
  108.2 0.8 collective-permute-done.17
  109.0 0.6 collective-permute-done.18
  109.7 0.1 add_convert_fusion.9
  109.8 3.0 %down_grads.2 = bf16[384,2048]{1,0:T(8,128)(2,1)S(1)} custom-call(bf16[384,128]{1,0:T(8,128)(2,1)S(1)} %get-tuple-element.136.refs_0_, bf16[384,256]{1,0:T(8,128)(2,1)S(1)} %get-tuple-element.137.refs_1_, bf16[384,256]{1,0:T(8,128)(2,1)S(1)} %get-tuple-element.138.refs_2_, bf16[384,256]{1,0:T(8,128)(2,1)S(1)} %get-tuple-element.139.refs_3_, ...), custom_call_target="tpu_custom_call" | custom-call | flops 1024 | bytes 1024 | tf_op jit(solution)/shard_map/down_grads/pallas_call | solution.py:258
  112.8 0.1 collective-permute-start.31
  112.9 1.4 collective-permute-start.22
  114.3 0.6 collective-permute-start.21
  115.1 6.5 %collective-permute-done.22 = bf16[128,1024]{1,0:T(8,128)(2,1)S(1)} collective-permute-done((bf16[128,1024]{1,0:T(8,128)(2,1)S(1)}, bf16[128,1024]{1,0:T(8,128)(2,1)S(1)}, u32[]{:S(2)}, u32[]{:S(2)}) %collective-permute-start.22) | collective-permute-done | bytes 262176 | tf_op jit(solution)/shard_map/ppermute | solution.py:282
  121.6 0.8 collective-permute-done.21
  122.5 0.9 collective-permute-start.25
  123.4 1.2 collective-permute-start.26
  124.6 5.0 %row_grads.3 = (bf16[2048,384]{1,0:T(8,128)(2,1)}, bf16[2048,384]{1,0:T(8,128)(2,1)}) custom-call(bf16[2048,128]{1,0:T(8,128)(2,1)S(1)} %get-tuple-element.109.refs_0_, bf16[2048,256]{1,0:T(8,128)(2,1)S(1)} %get-tuple-element.110.refs_1_, bf16[2048,256]{1,0:T(8,128)(2,1)S(1)} %get-tuple-element.111.refs_2_, ...), custom_call_target="tpu_custom_call" | custom-call | flops 1024 | bytes 1024 | tf_op jit(solution)/shard_map/row_grads/pallas_call | solution.py:219
  129.6 0.2 collective-permute-done.25
  129.9 0.8 collective-permute-done.26
  130.7 0.1 add_convert_fusion.2
  130.8 1.4 collective-permute-start.29
  132.2 0.7 collective-permute-start.30
  132.9 0.9 collective-permute-start.32
  133.8 1.1 collective-permute-start.33
  135.0 3.8 %down_grads.3 = bf16[384,2048]{1,0:T(8,128)(2,1)} custom-call(bf16[384,128]{1,0:T(8,128)(2,1)S(1)} %get-tuple-element.166.refs_0_, bf16[384,256]{1,0:T(8,128)(2,1)S(1)} %get-tuple-element.167.refs_1_, bf16[384,256]{1,0:T(8,128)(2,1)S(1)} %get-tuple-element.168.refs_2_, bf16[384,256]{1,0:T(8,128)(2,1)S(1)} %get-tuple-element.169.refs_3_, ...), custom_call_target="tpu_custom_call" | custom-call | flops 1024 | bytes 1024 | tf_op jit(solution)/shard_map/down_grads/pallas_call | solution.py:258
  138.8 1.3 collective-permute-done.29
  140.1 1.3 collective-permute-done.30
  141.3 2.8 %collective-permute-done.32 = bf16[128,1024]{1,0:T(8,128)(2,1)S(1)} collective-permute-done((bf16[128,1024]{1,0:T(8,128)(2,1)S(1)}, bf16[128,1024]{1,0:T(8,128)(2,1)S(1)}, u32[]{:S(2)}, u32[]{:S(2)}) %collective-permute-start.32) | collective-permute-done | bytes 262176 | tf_op jit(solution)/shard_map/ppermute | solution.py:282
  144.1 0.1 add_convert_fusion.1
  144.2 0.1 add_convert_fusion
  144.3 0.8 pad_maximum_fusion
  (44 shorter events, 0.5 us)
Async XLA Ops:
  2.8 3.7 %collective-permute-start = (bf16[2048,384]{1,0:T(8,128)(2,1)}, bf16[2048,384]{1,0:T(8,128)(2,1)S(1)}, u32[]{:S(2)}, u32[]{:S(2)}) collective-permute-start(bf16[2048,384]{1,0:T(8,128)(2,1)} %bitcast.9), channel_id=1, source_target_pairs={{0,1},{1,0},{2,3},{3,2},{4,5},{5,4},{6,7},{7,6},{8,9},{9,8},{10,11... | collective-permute-start | bytes 4718600 | tf_op jit(solution)/shard_map/ppermute | solution.py:284
  3.2 6.1 %collective-permute-start.1 = (bf16[2048,384]{1,0:T(8,128)(2,1)}, bf16[2048,384]{1,0:T(8,128)(2,1)S(1)}, u32[]{:S(2)}, u32[]{:S(2)}) collective-permute-start(bf16[2048,384]{1,0:T(8,128)(2,1)} %bitcast.15), channel_id=1, source_target_pairs={{0,1},{1,0},{2,3},{3,2},{4,5},{5,4},{6,7},{7,6},{8,9},{9,8},{10,11... | collective-permute-start | bytes 4718600 | tf_op jit(solution)/shard_map/ppermute | solution.py:284
  3.3 8.4 %collective-permute-start.2 = (bf16[384,2048]{1,0:T(8,128)(2,1)}, bf16[384,2048]{1,0:T(8,128)(2,1)S(1)}, u32[]{:S(2)}, u32[]{:S(2)}) collective-permute-start(bf16[384,2048]{1,0:T(8,128)(2,1)} %bitcast.21), channel_id=1, source_target_pairs={{0,1},{1,0},{2,3},{3,2},{4,5},{5,4},{6,7},{7,6},{8,9},{9,8},{10,11... | collective-permute-start | bytes 4718600 | tf_op jit(solution)/shard_map/ppermute | solution.py:284
  3.8 21.7 %collective-permute-start.3 = (bf16[128,2176]{1,0:T(8,128)(2,1)}, bf16[128,2176]{1,0:T(8,128)(2,1)S(1)}, u32[]{:S(2)}, u32[]{:S(2)}) collective-permute-start(bf16[128,2176]{1,0:T(8,128)(2,1)} %pack.1.refs_0_), channel_id=1, source_target_pairs={{0,4},{4,8},{8,12},{12,14},{14,10},{10,6},{6,2},{2,0},{1,5},{5,9},... | collective-permute-start | bytes 1671176 | tf_op jit(solution)/shard_map/ppermute | solution.py:282
  6.3 19.1 %collective-permute-start.4 = (bf16[128,2176]{1,0:T(8,128)(2,1)}, bf16[128,2176]{1,0:T(8,128)(2,1)S(1)}, u32[]{:S(2)}, u32[]{:S(2)}) collective-permute-start(bf16[128,2176]{1,0:T(8,128)(2,1)} %pack.1.refs_0_), channel_id=1, source_target_pairs={{4,0},{8,4},{12,8},{14,12},{10,14},{6,10},{2,6},{0,2},{5,1},{9,5},... | collective-permute-start | bytes 1671176 | tf_op jit(solution)/shard_map/ppermute | solution.py:283
  6.5 26.7 %collective-permute-start.8 = (bf16[128,2048]{1,0:T(8,128)(2,1)}, bf16[128,2048]{1,0:T(8,128)(2,1)S(1)}, u32[]{:S(2)}, u32[]{:S(2)}) collective-permute-start(bf16[128,2048]{1,0:T(8,128)(2,1)} %refs_5_.3), channel_id=1, source_target_pairs={{4,0},{8,4},{12,8},{14,12},{10,14},{6,10},{2,6},{0,2},{5,1},{9,5},... | collective-permute-start | bytes 1572872 | tf_op jit(solution)/shard_map/ppermute | solution.py:283
  9.4 23.9 %collective-permute-start.7 = (bf16[128,2048]{1,0:T(8,128)(2,1)}, bf16[128,2048]{1,0:T(8,128)(2,1)S(1)}, u32[]{:S(2)}, u32[]{:S(2)}) collective-permute-start(bf16[128,2048]{1,0:T(8,128)(2,1)} %refs_5_.3), channel_id=1, source_target_pairs={{0,4},{4,8},{8,12},{12,14},{14,10},{10,6},{6,2},{2,0},{1,5},{5,9},... | collective-permute-start | bytes 1572872 | tf_op jit(solution)/shard_map/ppermute | solution.py:282
  11.7 1.4 copy-start
  13.1 1.4 copy-start.2
  14.5 1.4 copy-start.4
  15.9 1.0 copy-start.6
  17.0 1.1 copy-start.8
  18.0 17.3 %copy-start.1 = (bf16[1,2048,384]{2,1,0:T(8,128)(2,1)S(1)}, bf16[1,2048,384]{2,1,0:T(8,128)(2,1)}, u32[]{:S(2)}) copy-start(bf16[1,2048,384]{2,1,0:T(8,128)(2,1)} %param.13) | copy-start | bytes 4718596
  18.0 17.3 %copy-start.3 = (bf16[1,2048,384]{2,1,0:T(8,128)(2,1)S(1)}, bf16[1,2048,384]{2,1,0:T(8,128)(2,1)}, u32[]{:S(2)}) copy-start(bf16[1,2048,384]{2,1,0:T(8,128)(2,1)} %param.14) | copy-start | bytes 4718596
  25.5 33.0 %copy-start.5 = (bf16[1,384,2048]{2,1,0:T(8,128)(2,1)S(1)}, bf16[1,384,2048]{2,1,0:T(8,128)(2,1)}, u32[]{:S(2)}) copy-start(bf16[1,384,2048]{2,1,0:T(8,128)(2,1)} %param.15) | copy-start | bytes 4718596
  25.5 19.3 %collective-permute-start.5 = (bf16[128,2176]{1,0:T(8,128)(2,1)S(1)}, bf16[128,2176]{1,0:T(8,128)(2,1)S(1)}, u32[]{:S(2)}, u32[]{:S(2)}) collective-permute-start(bf16[128,2176]{1,0:T(8,128)(2,1)S(1)} %collective-permute-done.3.refs_0_), channel_id=1, source_target_pairs={{0,4},{4,8},{8,12},{12,14},{14,10},{10,6},{6,2},{2,0},{1,5},{5,9},... | collective-permute-start | bytes 1671176 | tf_op jit(solution)/shard_map/ppermute | solution.py:282
  27.8 17.4 %collective-permute-start.6 = (bf16[128,2176]{1,0:T(8,128)(2,1)S(1)}, bf16[128,2176]{1,0:T(8,128)(2,1)S(1)}, u32[]{:S(2)}, u32[]{:S(2)}) collective-permute-start(bf16[128,2176]{1,0:T(8,128)(2,1)S(1)} %collective-permute-done.4.refs_1_), channel_id=1, source_target_pairs={{4,0},{8,4},{12,8},{14,12},{10,14},{6,10},{2,6},{0,2},{5,1},{9,5},... | collective-permute-start | bytes 1671176 | tf_op jit(solution)/shard_map/ppermute | solution.py:283
  33.2 23.2 %collective-permute-start.12 = (bf16[128,2048]{1,0:T(8,128)(2,1)S(1)}, bf16[128,2048]{1,0:T(8,128)(2,1)S(1)}, u32[]{:S(2)}, u32[]{:S(2)}) collective-permute-start(bf16[128,2048]{1,0:T(8,128)(2,1)S(1)} %collective-permute-done.8.refs_3_.refs_7_), channel_id=1, source_target_pairs={{4,0},{8,4},{12,8},{14,12},{10,14},{6,10},{2,6},{0,2},{5,1},{9,5},... | collective-permute-start | bytes 1572872 | tf_op jit(solution)/shard_map/ppermute | solution.py:283
  33.2 23.2 %collective-permute-start.11 = (bf16[128,2048]{1,0:T(8,128)(2,1)S(1)}, bf16[128,2048]{1,0:T(8,128)(2,1)S(1)}, u32[]{:S(2)}, u32[]{:S(2)}) collective-permute-start(bf16[128,2048]{1,0:T(8,128)(2,1)S(1)} %collective-permute-done.7.refs_2_.refs_6_), channel_id=1, source_target_pairs={{0,4},{4,8},{8,12},{12,14},{14,10},{10,6},{6,2},{2,0},{1,5},{5,9},... | collective-permute-start | bytes 1572872 | tf_op jit(solution)/shard_map/ppermute | solution.py:282
  45.2 23.2 %collective-permute-start.10 = (bf16[128,2176]{1,0:T(8,128)(2,1)S(1)}, bf16[128,2176]{1,0:T(8,128)(2,1)S(1)}, u32[]{:S(2)}, u32[]{:S(2)}) collective-permute-start(bf16[128,2176]{1,0:T(8,128)(2,1)S(1)} %collective-permute-done.6.refs_1_), channel_id=1, source_target_pairs={{4,0},{8,4},{12,8},{14,12},{10,14},{6,10},{2,6},{0,2},{5,1},{9,5},... | collective-permute-start | bytes 1671176 | tf_op jit(solution)/shard_map/ppermute | solution.py:283
  45.2 23.2 %collective-permute-start.9 = (bf16[128,2176]{1,0:T(8,128)(2,1)S(1)}, bf16[128,2176]{1,0:T(8,128)(2,1)S(1)}, u32[]{:S(2)}, u32[]{:S(2)}) collective-permute-start(bf16[128,2176]{1,0:T(8,128)(2,1)S(1)} %collective-permute-done.5.refs_0_), channel_id=1, source_target_pairs={{0,4},{4,8},{8,12},{12,14},{14,10},{10,6},{6,2},{2,0},{1,5},{5,9},... | collective-permute-start | bytes 1671176 | tf_op jit(solution)/shard_map/ppermute | solution.py:282
  56.4 22.5 %collective-permute-start.15 = (bf16[128,2048]{1,0:T(8,128)(2,1)S(1)}, bf16[128,2048]{1,0:T(8,128)(2,1)S(1)}, u32[]{:S(2)}, u32[]{:S(2)}) collective-permute-start(bf16[128,2048]{1,0:T(8,128)(2,1)S(1)} %collective-permute-done.12.refs_3_.refs_9_), channel_id=1, source_target_pairs={{4,0},{8,4},{12,8},{14,12},{10,14},{6,10},{2,6},{0,2},{5,1},{9,5},... | collective-permute-start | bytes 1572872 | tf_op jit(solution)/shard_map/ppermute | solution.py:283
  56.4 22.8 %collective-permute-start.14 = (bf16[128,2048]{1,0:T(8,128)(2,1)S(1)}, bf16[128,2048]{1,0:T(8,128)(2,1)S(1)}, u32[]{:S(2)}, u32[]{:S(2)}) collective-permute-start(bf16[128,2048]{1,0:T(8,128)(2,1)S(1)} %collective-permute-done.11.refs_2_.refs_8_), channel_id=1, source_target_pairs={{0,4},{4,8},{8,12},{12,14},{14,10},{10,6},{6,2},{2,0},{1,5},{5,9},... | collective-permute-start | bytes 1572872 | tf_op jit(solution)/shard_map/ppermute | solution.py:282
  68.4 22.4 %collective-permute-start.13 = (bf16[128,2176]{1,0:T(8,128)(2,1)S(1)}, bf16[128,2176]{1,0:T(8,128)(2,1)S(1)}, u32[]{:S(2)}, u32[]{:S(2)}) collective-permute-start(bf16[128,2176]{1,0:T(8,128)(2,1)S(1)} %collective-permute-done.9.refs_0_), channel_id=1, source_target_pairs={{0,4},{4,8},{8,12},{12,14},{14,10},{10,6},{6,2},{2,0},{1,5},{5,9},... | collective-permute-start | bytes 1671176 | tf_op jit(solution)/shard_map/ppermute | solution.py:282
  78.9 13.4 %collective-permute-start.16 = (bf16[128,2048]{1,0:T(8,128)(2,1)S(1)}, bf16[128,2048]{1,0:T(8,128)(2,1)S(1)}, u32[]{:S(2)}, u32[]{:S(2)}) collective-permute-start(bf16[128,2048]{1,0:T(8,128)(2,1)S(1)} %collective-permute-done.15.refs_3_.refs_11_), channel_id=1, source_target_pairs={{4,0},{8,4},{12,8},{14,12},{10,14},{6,10},{2,6},{0,2},{5,1},{9,5},... | collective-permute-start | bytes 1572872 | tf_op jit(solution)/shard_map/ppermute | solution.py:283
  88.7 13.1 %collective-permute-start.20 = (bf16[128,1024]{1,0:T(8,128)(2,1)S(1)}, bf16[128,1024]{1,0:T(8,128)(2,1)S(1)}, u32[]{:S(2)}, u32[]{:S(2)}) collective-permute-start(bf16[128,1024]{1,0:T(8,128)(2,1)S(1)} %get-tuple-element.115), channel_id=1, source_target_pairs={{0,4},{4,8},{8,12},{12,14},{14,10},{10,6},{6,2},{2,0},{1,5},{5,9},... | collective-permute-start | bytes 786440 | tf_op jit(solution)/shard_map/ppermute | solution.py:282
  90.4 11.4 %collective-permute-start.19 = (bf16[128,1024]{1,0:T(8,128)(2,1)S(1)}, bf16[128,1024]{1,0:T(8,128)(2,1)S(1)}, u32[]{:S(2)}, u32[]{:S(2)}) collective-permute-start(bf16[128,1024]{1,0:T(8,128)(2,1)S(1)} %get-tuple-element.113), channel_id=1, source_target_pairs={{4,0},{8,4},{12,8},{14,12},{10,14},{6,10},{2,6},{0,2},{5,1},{9,5},... | collective-permute-start | bytes 786440 | tf_op jit(solution)/shard_map/ppermute | solution.py:283
  99.7 9.3 %collective-permute-start.17 = (bf16[128,1024]{1,0:T(8,128)(2,1)S(1)}, bf16[128,1024]{1,0:T(8,128)(2,1)S(1)}, u32[]{:S(2)}, u32[]{:S(2)}) collective-permute-start(bf16[128,1024]{1,0:T(8,128)(2,1)S(1)} %get-tuple-element.107), channel_id=1, source_target_pairs={{4,0},{8,4},{12,8},{14,12},{10,14},{6,10},{2,6},{0,2},{5,1},{9,5},... | collective-permute-start | bytes 786440 | tf_op jit(solution)/shard_map/ppermute | solution.py:283
  100.4 9.2 %collective-permute-start.18 = (bf16[128,1024]{1,0:T(8,128)(2,1)S(1)}, bf16[128,1024]{1,0:T(8,128)(2,1)S(1)}, u32[]{:S(2)}, u32[]{:S(2)}) collective-permute-start(bf16[128,1024]{1,0:T(8,128)(2,1)S(1)} %get-tuple-element.108), channel_id=1, source_target_pairs={{0,4},{4,8},{8,12},{12,14},{14,10},{10,6},{6,2},{2,0},{1,5},{5,9},... | collective-permute-start | bytes 786440 | tf_op jit(solution)/shard_map/ppermute | solution.py:282
  101.9 10.9 %collective-permute-start.23 = (bf16[128,1024]{1,0:T(8,128)(2,1)S(1)}, bf16[128,1024]{1,0:T(8,128)(2,1)S(1)}, u32[]{:S(2)}, u32[]{:S(2)}) collective-permute-start(bf16[128,1024]{1,0:T(8,128)(2,1)S(1)} %add_convert_fusion.11), channel_id=1, source_target_pairs={{4,0},{8,4},{12,8},{14,12},{10,14},{6,10},{2,6},{0,2},{5,1},{9,5},... | collective-permute-start | bytes 786440 | tf_op jit(solution)/shard_map/ppermute | solution.py:283
  102.6 10.3 %collective-permute-start.24 = (bf16[128,1024]{1,0:T(8,128)(2,1)S(1)}, bf16[128,1024]{1,0:T(8,128)(2,1)S(1)}, u32[]{:S(2)}, u32[]{:S(2)}) collective-permute-start(bf16[128,1024]{1,0:T(8,128)(2,1)S(1)} %add_convert_fusion.10), channel_id=1, source_target_pairs={{0,4},{4,8},{8,12},{12,14},{14,10},{10,6},{6,2},{2,0},{1,5},{5,9},... | collective-permute-start | bytes 786440 | tf_op jit(solution)/shard_map/ppermute | solution.py:282
  108.1 1.7 %copy-start.7 = (bf16[128,2048]{1,0:T(8,128)(2,1)S(1)}, bf16[128,2048]{1,0:T(8,128)(2,1)}, u32[]{:S(2)}) copy-start(bf16[128,2048]{1,0:T(8,128)(2,1)} %refs_5_.3) | copy-start | bytes 1572868
  108.1 16.5 %collective-permute-start.27 = (bf16[2048,384]{1,0:T(8,128)(2,1)S(1)}, bf16[2048,384]{1,0:T(8,128)(2,1)S(1)}, u32[]{:S(2)}, u32[]{:S(2)}) collective-permute-start(bf16[2048,384]{1,0:T(8,128)(2,1)S(1)} %get-tuple-element.124), channel_id=1, source_target_pairs={{0,1},{1,0},{2,3},{3,2},{4,5},{5,4},{6,7},{7,6},{8,9},{9,8},{10,11... | collective-permute-start | bytes 4718600 | tf_op jit(solution)/shard_map/ppermute | solution.py:284
  109.0 15.6 %collective-permute-start.28 = (bf16[2048,384]{1,0:T(8,128)(2,1)S(1)}, bf16[2048,384]{1,0:T(8,128)(2,1)S(1)}, u32[]{:S(2)}, u32[]{:S(2)}) collective-permute-start(bf16[2048,384]{1,0:T(8,128)(2,1)S(1)} %get-tuple-element.157), channel_id=1, source_target_pairs={{0,1},{1,0},{2,3},{3,2},{4,5},{5,4},{6,7},{7,6},{8,9},{9,8},{10,11... | collective-permute-start | bytes 4718600 | tf_op jit(solution)/shard_map/ppermute | solution.py:284
  112.8 22.2 %collective-permute-start.31 = (bf16[384,2048]{1,0:T(8,128)(2,1)S(1)}, bf16[384,2048]{1,0:T(8,128)(2,1)S(1)}, u32[]{:S(2)}, u32[]{:S(2)}) collective-permute-start(bf16[384,2048]{1,0:T(8,128)(2,1)S(1)} %down_grads.2), channel_id=1, source_target_pairs={{0,1},{1,0},{2,3},{3,2},{4,5},{5,4},{6,7},{7,6},{8,9},{9,8},{10,11... | collective-permute-start | bytes 4718600 | tf_op jit(solution)/shard_map/ppermute | solution.py:284
  112.9 8.7 %collective-permute-start.22 = (bf16[128,1024]{1,0:T(8,128)(2,1)S(1)}, bf16[128,1024]{1,0:T(8,128)(2,1)S(1)}, u32[]{:S(2)}, u32[]{:S(2)}) collective-permute-start(bf16[128,1024]{1,0:T(8,128)(2,1)S(1)} %add_convert_fusion.8), channel_id=1, source_target_pairs={{0,4},{4,8},{8,12},{12,14},{14,10},{10,6},{6,2},{2,0},{1,5},{5,9},... | collective-permute-start | bytes 786440 | tf_op jit(solution)/shard_map/ppermute | solution.py:282
  114.3 8.2 %collective-permute-start.21 = (bf16[128,1024]{1,0:T(8,128)(2,1)S(1)}, bf16[128,1024]{1,0:T(8,128)(2,1)S(1)}, u32[]{:S(2)}, u32[]{:S(2)}) collective-permute-start(bf16[128,1024]{1,0:T(8,128)(2,1)S(1)} %add_convert_fusion.9), channel_id=1, source_target_pairs={{4,0},{8,4},{12,8},{14,12},{10,14},{6,10},{2,6},{0,2},{5,1},{9,5},... | collective-permute-start | bytes 786440 | tf_op jit(solution)/shard_map/ppermute | solution.py:283
  122.5 7.4 %collective-permute-start.25 = (bf16[128,1024]{1,0:T(8,128)(2,1)S(1)}, bf16[128,1024]{1,0:T(8,128)(2,1)S(1)}, u32[]{:S(2)}, u32[]{:S(2)}) collective-permute-start(bf16[128,1024]{1,0:T(8,128)(2,1)S(1)} %add_convert_fusion.7), channel_id=1, source_target_pairs={{4,0},{8,4},{12,8},{14,12},{10,14},{6,10},{2,6},{0,2},{5,1},{9,5},... | collective-permute-start | bytes 786440 | tf_op jit(solution)/shard_map/ppermute | solution.py:283
  123.4 7.3 %collective-permute-start.26 = (bf16[128,1024]{1,0:T(8,128)(2,1)S(1)}, bf16[128,1024]{1,0:T(8,128)(2,1)S(1)}, u32[]{:S(2)}, u32[]{:S(2)}) collective-permute-start(bf16[128,1024]{1,0:T(8,128)(2,1)S(1)} %add_convert_fusion.6), channel_id=1, source_target_pairs={{0,4},{4,8},{8,12},{12,14},{14,10},{10,6},{6,2},{2,0},{1,5},{5,9},... | collective-permute-start | bytes 786440 | tf_op jit(solution)/shard_map/ppermute | solution.py:282
  130.8 9.2 %collective-permute-start.29 = (bf16[128,1024]{1,0:T(8,128)(2,1)S(1)}, bf16[128,1024]{1,0:T(8,128)(2,1)S(1)}, u32[]{:S(2)}, u32[]{:S(2)}) collective-permute-start(bf16[128,1024]{1,0:T(8,128)(2,1)S(1)} %get-tuple-element.164), channel_id=1, source_target_pairs={{4,0},{8,4},{12,8},{14,12},{10,14},{6,10},{2,6},{0,2},{5,1},{9,5},... | collective-permute-start | bytes 786440 | tf_op jit(solution)/shard_map/ppermute | solution.py:283
  132.2 9.1 %collective-permute-start.30 = (bf16[128,1024]{1,0:T(8,128)(2,1)S(1)}, bf16[128,1024]{1,0:T(8,128)(2,1)S(1)}, u32[]{:S(2)}, u32[]{:S(2)}) collective-permute-start(bf16[128,1024]{1,0:T(8,128)(2,1)S(1)} %get-tuple-element.165), channel_id=1, source_target_pairs={{0,4},{4,8},{8,12},{12,14},{14,10},{10,6},{6,2},{2,0},{1,5},{5,9},... | collective-permute-start | bytes 786440 | tf_op jit(solution)/shard_map/ppermute | solution.py:282
  132.9 11.2 %collective-permute-start.32 = (bf16[128,1024]{1,0:T(8,128)(2,1)S(1)}, bf16[128,1024]{1,0:T(8,128)(2,1)S(1)}, u32[]{:S(2)}, u32[]{:S(2)}) collective-permute-start(bf16[128,1024]{1,0:T(8,128)(2,1)S(1)} %add_convert_fusion.4), channel_id=1, source_target_pairs={{0,4},{4,8},{8,12},{12,14},{14,10},{10,6},{6,2},{2,0},{1,5},{5,9},... | collective-permute-start | bytes 786440 | tf_op jit(solution)/shard_map/ppermute | solution.py:282
  133.8 10.4 %collective-permute-start.33 = (bf16[128,1024]{1,0:T(8,128)(2,1)S(1)}, bf16[128,1024]{1,0:T(8,128)(2,1)S(1)}, u32[]{:S(2)}, u32[]{:S(2)}) collective-permute-start(bf16[128,1024]{1,0:T(8,128)(2,1)S(1)} %add_convert_fusion.5), channel_id=1, source_target_pairs={{4,0},{8,4},{12,8},{14,12},{10,14},{6,10},{2,6},{0,2},{5,1},{9,5},... | collective-permute-start | bytes 786440 | tf_op jit(solution)/shard_map/ppermute | solution.py:283

commit v3 on v2

--- a/solution.py
+++ b/solution.py
@@ -350,17 +350,19 @@
         return first, second
 
     for s in range(reach - 1):
-        if s + 1 < reach - 1:
+        more = s + 1 < reach - 1
+        if more:
             high_down, low_up = plus(high_down, below_high[s + 1]), plus(low_up, above_low[s + 1])
             high_down, low_up = before_chore(high_down, low_up)
             high_down, low_up = down(high_down), up(low_up)
-        if s != 1 and chores:
+        if s > 0 and more and chores:
+            high_down, low_up = after_chore(high_down, low_up)
+            low_down, high_up, high_down, low_up = tied((low_down, high_up, high_down, low_up))
+        elif chores:
             low_down, high_up = after_chore(low_down, high_up)
         low_down, high_up = plus(low_down, below_low[s]), plus(high_up, above_high[s])
         low_down, high_up = before_chore(low_down, high_up)
         low_down, high_up = down(low_down), up(high_up)
-        if s == 0 and chores:
-            high_down, low_up = after_chore(high_down, low_up)
     while chores:
         low_down, high_up = after_chore(low_down, high_up)
 

time: 145 us -> 144 us (level)
    ppermute x14, waiting for transfers between devices: 12.1 us -> 7.22 us  [ring_local(): up = lambda value: lax.ppermute(value, 'expert', up_pairs)]
    ppermute x14, waiting for transfers between devices: 29.2 us -> 32.8 us  [ring_local(): down = lambda value: lax.ppermute(value, 'expert', down_pairs)]
  transfers between devices with their start and end apart: 34 -> 34, of which waited for: 16 -> 15; matrix products, arithmetic and copies ran while one was open for 0% -> 0% of each run, Pallas kernels for 41% -> 41%
where the time goes in v3:
time: 144 us
  Pallas kernels  61.3 us (43%)
  waiting for transfers between devices  40.2 us (28%)
  starting transfers between devices  33.7 us (23%)
  local copies, waits for them, and re-layouts  6.34 us (4%)
  other arithmetic  1.6 us (1%)
    pallas_call x5, Pallas kernels, expert_batch(): pl.pallas_call(functools.partial(expert_kernel, len(blocks), experts), in...  43.2 us
    ppermute x14, waiting for transfers between devices, ring_local(): down = lambda value: lax.ppermute(value, 'expert', down_pairs)  32.8 us
    ppermute x14, starting transfers between devices, ring_local(): up = lambda value: lax.ppermute(value, 'expert', up_pairs)  23.9 us
    pallas_call x2, Pallas kernels, row_grads(): pl.pallas_call(functools.partial(row_kernel, len(acts), len(terms)), grid...  9.11 us
    ppermute x14, starting transfers between devices, ring_local(): down = lambda value: lax.ppermute(value, 'expert', down_pairs)  8.7 us
    ppermute x14, waiting for transfers between devices, ring_local(): up = lambda value: lax.ppermute(value, 'expert', up_pairs)  7.22 us
    pallas_call x2, Pallas kernels, down_grads(): pl.pallas_call(functools.partial(down_kernel, len(hiddens), len(cots), le...  6.78 us
    unnamed x18, local copies, waits for them, and re-layouts  6.34 us
  transfers between devices with their start and end apart: 34, of which 15 were waited for; matrix products, arithmetic and copies ran while one was open for 0% of the time, Pallas kernels for 41%

profile of v3, /device:TPU:0, one launch (start us, length us, event | category | flops | bytes accessed | tf_op | source)
XLA Modules:
  0.0 144.0 jit_solution(6724187715167208691)
XLA Ops:
  0.6 2.2 %pack.1.refs_0_ = bf16[128,2176]{1,0:T(8,128)(2,1)} custom-call(s32[4,128]{1,0:T(4,128)} %bitcast.28, f32[4,128]{1,0:T(4,128)} %bitcast.29, s32[1,16]{1,0:T(1,128)} %bitcast.30, bf16[128,2048]{1,0:T(8,128)(2,1)} %tokens_ref.1), custom_call_target="tpu_custom_call" | custom-call | tf_op jit(solution)/shard_map/pack/pallas_call | solution.py:70
  2.8 0.5 collective-permute-start
  3.2 0.1 collective-permute-start.1
  3.3 0.5 collective-permute-start.2
  3.8 2.6 %collective-permute-start.3 = (bf16[128,2176]{1,0:T(8,128)(2,1)}, bf16[128,2176]{1,0:T(8,128)(2,1)S(1)}, u32[]{:S(2)}, u32[]{:S(2)}) collective-permute-start(bf16[128,2176]{1,0:T(8,128)(2,1)} %pack.1.refs_0_), channel_id=1, source_target_pairs={{0,4},{4,8},{8,12},{12,14},{14,10},{10,6},{6,2},{2,0},{1,5},{5,9},... | collective-permute-start | bytes 1671176 | tf_op jit(solution)/shard_map/ppermute | solution.py:282
  6.3 0.2 collective-permute-done.refs_5_.refs_7_
  6.5 2.9 %collective-permute-start.8 = (bf16[128,2048]{1,0:T(8,128)(2,1)}, bf16[128,2048]{1,0:T(8,128)(2,1)S(1)}, u32[]{:S(2)}, u32[]{:S(2)}) collective-permute-start(bf16[128,2048]{1,0:T(8,128)(2,1)} %refs_5_.3), channel_id=1, source_target_pairs={{4,0},{8,4},{12,8},{14,12},{10,14},{6,10},{2,6},{0,2},{5,1},{9,5},... | collective-permute-start | bytes 1572872 | tf_op jit(solution)/shard_map/ppermute | solution.py:283
  9.4 2.3 %collective-permute-start.7 = (bf16[128,2048]{1,0:T(8,128)(2,1)}, bf16[128,2048]{1,0:T(8,128)(2,1)S(1)}, u32[]{:S(2)}, u32[]{:S(2)}) collective-permute-start(bf16[128,2048]{1,0:T(8,128)(2,1)} %refs_5_.3), channel_id=1, source_target_pairs={{0,4},{4,8},{8,12},{12,14},{14,10},{10,6},{6,2},{2,0},{1,5},{5,9},... | collective-permute-start | bytes 1572872 | tf_op jit(solution)/shard_map/ppermute | solution.py:282
  11.7 1.4 copy-done
  13.1 1.4 copy-done.2
  14.5 1.4 copy-done.4
  15.9 1.0 copy-done.6
  17.0 1.1 copy-done.8
  18.0 7.4 %expert_batch.5 = (bf16[2048,128]{1,0:T(8,128)(2,1)S(1)}, bf16[128,768]{1,0:T(8,128)(2,1)S(1)}, bf16[128,768]{1,0:T(8,128)(2,1)S(1)}, bf16[384,128]{1,0:T(8,128)...) custom-call(bf16[128,2176]{1,0:T(8,128)(2,1)S(1)} %copy-done.8, ...), custom_call_target="tpu_custom_call" | custom-call | flops 1024 | bytes 1024 | tf_op jit(solution)/shard_map/expert_batch/pallas_call | solution.py:169
  25.5 2.3 %collective-permute-start.5 = (bf16[128,2176]{1,0:T(8,128)(2,1)S(1)}, bf16[128,2176]{1,0:T(8,128)(2,1)S(1)}, u32[]{:S(2)}, u32[]{:S(2)}) collective-permute-start(bf16[128,2176]{1,0:T(8,128)(2,1)S(1)} %collective-permute-done.3.refs_0_), channel_id=1, source_target_pairs={{0,4},{4,8},{8,12},{12,14},{14,10},{10,6},{6,2},{2,0},{1,5},{5,9},... | collective-permute-start | bytes 1671176 | tf_op jit(solution)/shard_map/ppermute | solution.py:282
  27.8 5.5 %collective-permute-done.8.refs_3_.refs_7_ = bf16[128,2048]{1,0:T(8,128)(2,1)S(1)} collective-permute-done((bf16[128,2048]{1,0:T(8,128)(2,1)}, bf16[128,2048]{1,0:T(8,128)(2,1)S(1)}, u32[]{:S(2)}, u32[]{:S(2)}) %collective-permute-start.8) | collective-permute-done | bytes 524320 | tf_op jit(solution)/shard_map/ppermute | solution.py:283
  33.2 2.0 %collective-permute-start.11 = (bf16[128,2048]{1,0:T(8,128)(2,1)S(1)}, bf16[128,2048]{1,0:T(8,128)(2,1)S(1)}, u32[]{:S(2)}, u32[]{:S(2)}) collective-permute-start(bf16[128,2048]{1,0:T(8,128)(2,1)S(1)} %collective-permute-done.7.refs_2_.refs_6_), channel_id=1, source_target_pairs={{0,4},{4,8},{8,12},{12,14},{14,10},{10,6},{6,2},{2,0},{1,5},{5,9},... | collective-permute-start | bytes 1572872 | tf_op jit(solution)/shard_map/ppermute | solution.py:282
  35.3 9.5 %expert_batch.6 = (bf16[2048,256]{1,0:T(8,128)(2,1)S(1)}, bf16[256,768]{1,0:T(8,128)(2,1)S(1)}, bf16[256,768]{1,0:T(8,128)(2,1)S(1)}, bf16[384,256]{1,0:T(8,128)...) custom-call(bf16[128,2176]{1,0:T(8,128)(2,1)S(1)} %collective-permut, ...), custom_call_target="tpu_custom_call" | custom-call | flops 1024 | bytes 1024 | tf_op jit(solution)/shard_map/expert_batch/pallas_call | solution.py:169
  44.8 0.4 collective-permute-done.6.refs_1_
  45.2 2.0 %collective-permute-start.9 = (bf16[128,2176]{1,0:T(8,128)(2,1)S(1)}, bf16[128,2176]{1,0:T(8,128)(2,1)S(1)}, u32[]{:S(2)}, u32[]{:S(2)}) collective-permute-start(bf16[128,2176]{1,0:T(8,128)(2,1)S(1)} %collective-permute-done.5.refs_0_), channel_id=1, source_target_pairs={{0,4},{4,8},{8,12},{12,14},{14,10},{10,6},{6,2},{2,0},{1,5},{5,9},... | collective-permute-start | bytes 1671176 | tf_op jit(solution)/shard_map/ppermute | solution.py:282
  47.2 9.2 %collective-permute-done.12.refs_3_.refs_9_ = bf16[128,2048]{1,0:T(8,128)(2,1)S(1)} collective-permute-done((bf16[128,2048]{1,0:T(8,128)(2,1)S(1)}, bf16[128,2048]{1,0:T(8,128)(2,1)S(1)}, u32[]{:S(2)}, u32[]{:S(2)}) %collective-permute-start.12) | collective-permute-done | bytes 524320 | tf_op jit(solution)/shard_map/ppermute | solution.py:283
  56.4 2.0 %collective-permute-start.14 = (bf16[128,2048]{1,0:T(8,128)(2,1)S(1)}, bf16[128,2048]{1,0:T(8,128)(2,1)S(1)}, u32[]{:S(2)}, u32[]{:S(2)}) collective-permute-start(bf16[128,2048]{1,0:T(8,128)(2,1)S(1)} %collective-permute-done.11.refs_2_.refs_8_), channel_id=1, source_target_pairs={{0,4},{4,8},{8,12},{12,14},{14,10},{10,6},{6,2},{2,0},{1,5},{5,9},... | collective-permute-start | bytes 1572872 | tf_op jit(solution)/shard_map/ppermute | solution.py:282
  58.4 9.5 %expert_batch.7 = (bf16[2048,256]{1,0:T(8,128)(2,1)S(1)}, bf16[256,768]{1,0:T(8,128)(2,1)S(1)}, bf16[256,768]{1,0:T(8,128)(2,1)S(1)}, bf16[384,256]{1,0:T(8,128)...) custom-call(bf16[128,2176]{1,0:T(8,128)(2,1)S(1)} %collective-permut, ...), custom_call_target="tpu_custom_call" | custom-call | flops 1024 | bytes 1024 | tf_op jit(solution)/shard_map/expert_batch/pallas_call | solution.py:169
  67.9 0.4 collective-permute-done.10.refs_1_
  68.4 1.6 %collective-permute-start.13 = (bf16[128,2176]{1,0:T(8,128)(2,1)S(1)}, bf16[128,2176]{1,0:T(8,128)(2,1)S(1)}, u32[]{:S(2)}, u32[]{:S(2)}) collective-permute-start(bf16[128,2176]{1,0:T(8,128)(2,1)S(1)} %collective-permute-done.9.refs_0_), channel_id=1, source_target_pairs={{0,4},{4,8},{8,12},{12,14},{14,10},{10,6},{6,2},{2,0},{1,5},{5,9},... | collective-permute-start | bytes 1671176 | tf_op jit(solution)/shard_map/ppermute | solution.py:282
  69.9 9.0 %collective-permute-done.15.refs_3_.refs_11_ = bf16[128,2048]{1,0:T(8,128)(2,1)S(1)} collective-permute-done((bf16[128,2048]{1,0:T(8,128)(2,1)S(1)}, bf16[128,2048]{1,0:T(8,128)(2,1)S(1)}, u32[]{:S(2)}, u32[]{:S(2)}) %collective-permute-start.15) | collective-permute-done | bytes 524320 | tf_op jit(solution)/shard_map/ppermute | solution.py:283
  78.9 0.3 collective-permute-start.16
  79.2 9.4 %expert_batch.8 = (bf16[2048,256]{1,0:T(8,128)(2,1)S(1)}, bf16[256,768]{1,0:T(8,128)(2,1)S(1)}, bf16[256,768]{1,0:T(8,128)(2,1)S(1)}, bf16[384,256]{1,0:T(8,128)...) custom-call(bf16[128,2176]{1,0:T(8,128)(2,1)S(1)} %collective-permut, ...), custom_call_target="tpu_custom_call" | custom-call | flops 1024 | bytes 1024 | tf_op jit(solution)/shard_map/expert_batch/pallas_call | solution.py:169
  88.7 1.8 %collective-permute-start.20 = (bf16[128,1024]{1,0:T(8,128)(2,1)S(1)}, bf16[128,1024]{1,0:T(8,128)(2,1)S(1)}, u32[]{:S(2)}, u32[]{:S(2)}) collective-permute-start(bf16[128,1024]{1,0:T(8,128)(2,1)S(1)} %get-tuple-element.119), channel_id=1, source_target_pairs={{0,4},{4,8},{8,12},{12,14},{14,10},{10,6},{6,2},{2,0},{1,5},{5,9},... | collective-permute-start | bytes 786440 | tf_op jit(solution)/shard_map/ppermute | solution.py:282
  90.4 0.3 collective-permute-start.19
  90.7 1.6 %collective-permute-done.16.refs_1_.refs_12_ = bf16[128,2048]{1,0:T(8,128)(2,1)S(1)} collective-permute-done((bf16[128,2048]{1,0:T(8,128)(2,1)S(1)}, bf16[128,2048]{1,0:T(8,128)(2,1)S(1)}, u32[]{:S(2)}, u32[]{:S(2)}) %collective-permute-start.16) | collective-permute-done | bytes 524320 | tf_op jit(solution)/shard_map/ppermute | solution.py:283
  92.3 7.4 %expert_batch.9 = (bf16[2048,128]{1,0:T(8,128)(2,1)S(1)}, bf16[128,768]{1,0:T(8,128)(2,1)S(1)}, bf16[128,768]{1,0:T(8,128)(2,1)S(1)}, bf16[384,128]{1,0:T(8,128)...) custom-call(bf16[128,2176]{1,0:T(8,128)(2,1)S(1)} %collective-permute-done.13., ...), custom_call_target="tpu_custom_call" | custom-call | flops 1024 | bytes 1024 | tf_op jit(solution)/shard_map/expert_batch/pallas_call | solution.py:169
  99.7 0.7 collective-permute-start.17
  100.4 1.4 collective-permute-start.18
  101.8 0.1 add_convert_fusion.11
  101.9 1.6 %collective-permute-start.24 = (bf16[128,1024]{1,0:T(8,128)(2,1)S(1)}, bf16[128,1024]{1,0:T(8,128)(2,1)S(1)}, u32[]{:S(2)}, u32[]{:S(2)}) collective-permute-start(bf16[128,1024]{1,0:T(8,128)(2,1)S(1)} %add_convert_fusion.10), channel_id=1, source_target_pairs={{0,4},{4,8},{8,12},{12,14},{14,10},{10,6},{6,2},{2,0},{1,5},{5,9},... | collective-permute-start | bytes 786440 | tf_op jit(solution)/shard_map/ppermute | solution.py:282
  103.5 0.4 collective-permute-start.23
  104.0 4.1 %row_grads.2 = (bf16[2048,384]{1,0:T(8,128)(2,1)S(1)}, bf16[2048,384]{1,0:T(8,128)(2,1)S(1)}) custom-call(bf16[2048,128]{1,0:T(8,128)(2,1)S(1)} %get-tuple-element.113.refs_0_, bf16[2048,256]{1,0:T(8,128)(2,1)S(1)} %get-tuple-element.114.refs_1_, bf16[2048,256]{1,0:T(8,128)(2,1)S(1)} %get-tuple-element.115.refs_2_, ...), custom_call_target="tpu_custom_call" | custom-call | flops 1024 | bytes 1024 | tf_op jit(solution)/shard_map/row_grads/pallas_call | solution.py:219
  108.1 0.1 collective-permute-start.29
  108.2 0.8 collective-permute-done.17
  108.9 0.7 collective-permute-done.18
  109.7 0.1 add_convert_fusion.9
  109.8 2.8 %collective-permute-done.24 = bf16[128,1024]{1,0:T(8,128)(2,1)S(1)} collective-permute-done((bf16[128,1024]{1,0:T(8,128)(2,1)S(1)}, bf16[128,1024]{1,0:T(8,128)(2,1)S(1)}, u32[]{:S(2)}, u32[]{:S(2)}) %collective-permute-start.24) | collective-permute-done | bytes 262176 | tf_op jit(solution)/shard_map/ppermute | solution.py:282
  112.7 0.1 add_convert_fusion.7
  112.7 1.0 collective-permute-start.25
  113.7 1.1 collective-permute-start.26
  114.8 1.0 collective-permute-start.21
  115.7 5.5 %collective-permute-done.25 = bf16[128,1024]{1,0:T(8,128)(2,1)S(1)} collective-permute-done((bf16[128,1024]{1,0:T(8,128)(2,1)S(1)}, bf16[128,1024]{1,0:T(8,128)(2,1)S(1)}, u32[]{:S(2)}, u32[]{:S(2)}) %collective-permute-start.25) | collective-permute-done | bytes 262176 | tf_op jit(solution)/shard_map/ppermute | solution.py:283
  121.2 1.1 collective-permute-start.22
  122.4 3.0 %down_grads.2 = bf16[384,2048]{1,0:T(8,128)(2,1)S(1)} custom-call(bf16[384,128]{1,0:T(8,128)(2,1)S(1)} %get-tuple-element.144.refs_0_, bf16[384,256]{1,0:T(8,128)(2,1)S(1)} %get-tuple-element.145.refs_1_, bf16[384,256]{1,0:T(8,128)(2,1)S(1)} %get-tuple-element.146.refs_2_, bf16[384,256]{1,0:T(8,128)(2,1)S(1)} %get-tuple-element.147.refs_3_, ...), custom_call_target="tpu_custom_call" | custom-call | flops 1024 | bytes 1024 | tf_op jit(solution)/shard_map/down_grads/pallas_call | solution.py:258
  125.3 0.1 collective-permute-start.33
  125.4 2.2 %collective-permute-done.22 = bf16[128,1024]{1,0:T(8,128)(2,1)S(1)} collective-permute-done((bf16[128,1024]{1,0:T(8,128)(2,1)S(1)}, bf16[128,1024]{1,0:T(8,128)(2,1)S(1)}, u32[]{:S(2)}, u32[]{:S(2)}) %collective-permute-start.22) | collective-permute-done | bytes 262176 | tf_op jit(solution)/shard_map/ppermute | solution.py:282
  127.7 0.7 collective-permute-start.27
  128.4 1.4 collective-permute-start.28
  129.8 5.0 %row_grads.3 = (bf16[2048,384]{1,0:T(8,128)(2,1)}, bf16[2048,384]{1,0:T(8,128)(2,1)}) custom-call(bf16[2048,128]{1,0:T(8,128)(2,1)S(1)} %get-tuple-element.113.refs_0_, bf16[2048,256]{1,0:T(8,128)(2,1)S(1)} %get-tuple-element.114.refs_1_, bf16[2048,256]{1,0:T(8,128)(2,1)S(1)} %get-tuple-element.115.refs_2_, ...), custom_call_target="tpu_custom_call" | custom-call | flops 1024 | bytes 1024 | tf_op jit(solution)/shard_map/row_grads/pallas_call | solution.py:219
  134.8 0.1 collective-permute-done.28
  135.0 0.1 add_convert_fusion.3
  135.1 1.5 %collective-permute-start.31 = (bf16[128,1024]{1,0:T(8,128)(2,1)S(1)}, bf16[128,1024]{1,0:T(8,128)(2,1)S(1)}, u32[]{:S(2)}, u32[]{:S(2)}) collective-permute-start(bf16[128,1024]{1,0:T(8,128)(2,1)S(1)} %add_convert_fusion.3), channel_id=1, source_target_pairs={{4,0},{8,4},{12,8},{14,12},{10,14},{6,10},{2,6},{0,2},{5,1},{9,5},... | collective-permute-start | bytes 786440 | tf_op jit(solution)/shard_map/ppermute | solution.py:283
  136.5 0.6 collective-permute-start.32
  137.1 3.8 %down_grads.3 = bf16[384,2048]{1,0:T(8,128)(2,1)} custom-call(bf16[384,128]{1,0:T(8,128)(2,1)S(1)} %get-tuple-element.174.refs_0_, bf16[384,256]{1,0:T(8,128)(2,1)S(1)} %get-tuple-element.175.refs_1_, bf16[384,256]{1,0:T(8,128)(2,1)S(1)} %get-tuple-element.176.refs_2_, bf16[384,256]{1,0:T(8,128)(2,1)S(1)} %get-tuple-element.177.refs_3_, ...), custom_call_target="tpu_custom_call" | custom-call | flops 1024 | bytes 1024 | tf_op jit(solution)/shard_map/down_grads/pallas_call | solution.py:258
  141.0 0.5 collective-permute-done.31
  141.5 1.4 collective-permute-done.32
  142.9 0.2 add_convert_fusion
  143.1 0.8 pad_maximum_fusion
  (44 shorter events, 0.4 us)
Async XLA Ops:
  2.8 3.7 %collective-permute-start = (bf16[2048,384]{1,0:T(8,128)(2,1)}, bf16[2048,384]{1,0:T(8,128)(2,1)S(1)}, u32[]{:S(2)}, u32[]{:S(2)}) collective-permute-start(bf16[2048,384]{1,0:T(8,128)(2,1)} %bitcast.9), channel_id=1, source_target_pairs={{0,1},{1,0},{2,3},{3,2},{4,5},{5,4},{6,7},{7,6},{8,9},{9,8},{10,11... | collective-permute-start | bytes 4718600 | tf_op jit(solution)/shard_map/ppermute | solution.py:284
  3.2 6.1 %collective-permute-start.1 = (bf16[2048,384]{1,0:T(8,128)(2,1)}, bf16[2048,384]{1,0:T(8,128)(2,1)S(1)}, u32[]{:S(2)}, u32[]{:S(2)}) collective-permute-start(bf16[2048,384]{1,0:T(8,128)(2,1)} %bitcast.15), channel_id=1, source_target_pairs={{0,1},{1,0},{2,3},{3,2},{4,5},{5,4},{6,7},{7,6},{8,9},{9,8},{10,11... | collective-permute-start | bytes 4718600 | tf_op jit(solution)/shard_map/ppermute | solution.py:284
  3.3 8.4 %collective-permute-start.2 = (bf16[384,2048]{1,0:T(8,128)(2,1)}, bf16[384,2048]{1,0:T(8,128)(2,1)S(1)}, u32[]{:S(2)}, u32[]{:S(2)}) collective-permute-start(bf16[384,2048]{1,0:T(8,128)(2,1)} %bitcast.21), channel_id=1, source_target_pairs={{0,1},{1,0},{2,3},{3,2},{4,5},{5,4},{6,7},{7,6},{8,9},{9,8},{10,11... | collective-permute-start | bytes 4718600 | tf_op jit(solution)/shard_map/ppermute | solution.py:284
  3.8 21.7 %collective-permute-start.3 = (bf16[128,2176]{1,0:T(8,128)(2,1)}, bf16[128,2176]{1,0:T(8,128)(2,1)S(1)}, u32[]{:S(2)}, u32[]{:S(2)}) collective-permute-start(bf16[128,2176]{1,0:T(8,128)(2,1)} %pack.1.refs_0_), channel_id=1, source_target_pairs={{0,4},{4,8},{8,12},{12,14},{14,10},{10,6},{6,2},{2,0},{1,5},{5,9},... | collective-permute-start | bytes 1671176 | tf_op jit(solution)/shard_map/ppermute | solution.py:282
  6.3 19.1 %collective-permute-start.4 = (bf16[128,2176]{1,0:T(8,128)(2,1)}, bf16[128,2176]{1,0:T(8,128)(2,1)S(1)}, u32[]{:S(2)}, u32[]{:S(2)}) collective-permute-start(bf16[128,2176]{1,0:T(8,128)(2,1)} %pack.1.refs_0_), channel_id=1, source_target_pairs={{4,0},{8,4},{12,8},{14,12},{10,14},{6,10},{2,6},{0,2},{5,1},{9,5},... | collective-permute-start | bytes 1671176 | tf_op jit(solution)/shard_map/ppermute | solution.py:283
  6.5 26.7 %collective-permute-start.8 = (bf16[128,2048]{1,0:T(8,128)(2,1)}, bf16[128,2048]{1,0:T(8,128)(2,1)S(1)}, u32[]{:S(2)}, u32[]{:S(2)}) collective-permute-start(bf16[128,2048]{1,0:T(8,128)(2,1)} %refs_5_.3), channel_id=1, source_target_pairs={{4,0},{8,4},{12,8},{14,12},{10,14},{6,10},{2,6},{0,2},{5,1},{9,5},... | collective-permute-start | bytes 1572872 | tf_op jit(solution)/shard_map/ppermute | solution.py:283
  9.4 23.9 %collective-permute-start.7 = (bf16[128,2048]{1,0:T(8,128)(2,1)}, bf16[128,2048]{1,0:T(8,128)(2,1)S(1)}, u32[]{:S(2)}, u32[]{:S(2)}) collective-permute-start(bf16[128,2048]{1,0:T(8,128)(2,1)} %refs_5_.3), channel_id=1, source_target_pairs={{0,4},{4,8},{8,12},{12,14},{14,10},{10,6},{6,2},{2,0},{1,5},{5,9},... | collective-permute-start | bytes 1572872 | tf_op jit(solution)/shard_map/ppermute | solution.py:282
  11.7 1.4 copy-start
  13.1 1.4 copy-start.2
  14.5 1.4 copy-start.4
  15.9 1.0 copy-start.6
  17.0 1.1 copy-start.8
  18.0 17.3 %copy-start.1 = (bf16[1,2048,384]{2,1,0:T(8,128)(2,1)S(1)}, bf16[1,2048,384]{2,1,0:T(8,128)(2,1)}, u32[]{:S(2)}) copy-start(bf16[1,2048,384]{2,1,0:T(8,128)(2,1)} %param.13) | copy-start | bytes 4718596
  18.0 17.3 %copy-start.3 = (bf16[1,2048,384]{2,1,0:T(8,128)(2,1)S(1)}, bf16[1,2048,384]{2,1,0:T(8,128)(2,1)}, u32[]{:S(2)}) copy-start(bf16[1,2048,384]{2,1,0:T(8,128)(2,1)} %param.14) | copy-start | bytes 4718596
  25.5 33.0 %copy-start.5 = (bf16[1,384,2048]{2,1,0:T(8,128)(2,1)S(1)}, bf16[1,384,2048]{2,1,0:T(8,128)(2,1)}, u32[]{:S(2)}) copy-start(bf16[1,384,2048]{2,1,0:T(8,128)(2,1)} %param.15) | copy-start | bytes 4718596
  25.5 19.3 %collective-permute-start.5 = (bf16[128,2176]{1,0:T(8,128)(2,1)S(1)}, bf16[128,2176]{1,0:T(8,128)(2,1)S(1)}, u32[]{:S(2)}, u32[]{:S(2)}) collective-permute-start(bf16[128,2176]{1,0:T(8,128)(2,1)S(1)} %collective-permute-done.3.refs_0_), channel_id=1, source_target_pairs={{0,4},{4,8},{8,12},{12,14},{14,10},{10,6},{6,2},{2,0},{1,5},{5,9},... | collective-permute-start | bytes 1671176 | tf_op jit(solution)/shard_map/ppermute | solution.py:282
  27.8 17.4 %collective-permute-start.6 = (bf16[128,2176]{1,0:T(8,128)(2,1)S(1)}, bf16[128,2176]{1,0:T(8,128)(2,1)S(1)}, u32[]{:S(2)}, u32[]{:S(2)}) collective-permute-start(bf16[128,2176]{1,0:T(8,128)(2,1)S(1)} %collective-permute-done.4.refs_1_), channel_id=1, source_target_pairs={{4,0},{8,4},{12,8},{14,12},{10,14},{6,10},{2,6},{0,2},{5,1},{9,5},... | collective-permute-start | bytes 1671176 | tf_op jit(solution)/shard_map/ppermute | solution.py:283
  33.2 23.2 %collective-permute-start.12 = (bf16[128,2048]{1,0:T(8,128)(2,1)S(1)}, bf16[128,2048]{1,0:T(8,128)(2,1)S(1)}, u32[]{:S(2)}, u32[]{:S(2)}) collective-permute-start(bf16[128,2048]{1,0:T(8,128)(2,1)S(1)} %collective-permute-done.8.refs_3_.refs_7_), channel_id=1, source_target_pairs={{4,0},{8,4},{12,8},{14,12},{10,14},{6,10},{2,6},{0,2},{5,1},{9,5},... | collective-permute-start | bytes 1572872 | tf_op jit(solution)/shard_map/ppermute | solution.py:283
  33.2 23.2 %collective-permute-start.11 = (bf16[128,2048]{1,0:T(8,128)(2,1)S(1)}, bf16[128,2048]{1,0:T(8,128)(2,1)S(1)}, u32[]{:S(2)}, u32[]{:S(2)}) collective-permute-start(bf16[128,2048]{1,0:T(8,128)(2,1)S(1)} %collective-permute-done.7.refs_2_.refs_6_), channel_id=1, source_target_pairs={{0,4},{4,8},{8,12},{12,14},{14,10},{10,6},{6,2},{2,0},{1,5},{5,9},... | collective-permute-start | bytes 1572872 | tf_op jit(solution)/shard_map/ppermute | solution.py:282
  45.2 23.2 %collective-permute-start.10 = (bf16[128,2176]{1,0:T(8,128)(2,1)S(1)}, bf16[128,2176]{1,0:T(8,128)(2,1)S(1)}, u32[]{:S(2)}, u32[]{:S(2)}) collective-permute-start(bf16[128,2176]{1,0:T(8,128)(2,1)S(1)} %collective-permute-done.6.refs_1_), channel_id=1, source_target_pairs={{4,0},{8,4},{12,8},{14,12},{10,14},{6,10},{2,6},{0,2},{5,1},{9,5},... | collective-permute-start | bytes 1671176 | tf_op jit(solution)/shard_map/ppermute | solution.py:283
  45.2 23.2 %collective-permute-start.9 = (bf16[128,2176]{1,0:T(8,128)(2,1)S(1)}, bf16[128,2176]{1,0:T(8,128)(2,1)S(1)}, u32[]{:S(2)}, u32[]{:S(2)}) collective-permute-start(bf16[128,2176]{1,0:T(8,128)(2,1)S(1)} %collective-permute-done.5.refs_0_), channel_id=1, source_target_pairs={{0,4},{4,8},{8,12},{12,14},{14,10},{10,6},{6,2},{2,0},{1,5},{5,9},... | collective-permute-start | bytes 1671176 | tf_op jit(solution)/shard_map/ppermute | solution.py:282
  56.4 22.5 %collective-permute-start.15 = (bf16[128,2048]{1,0:T(8,128)(2,1)S(1)}, bf16[128,2048]{1,0:T(8,128)(2,1)S(1)}, u32[]{:S(2)}, u32[]{:S(2)}) collective-permute-start(bf16[128,2048]{1,0:T(8,128)(2,1)S(1)} %collective-permute-done.12.refs_3_.refs_9_), channel_id=1, source_target_pairs={{4,0},{8,4},{12,8},{14,12},{10,14},{6,10},{2,6},{0,2},{5,1},{9,5},... | collective-permute-start | bytes 1572872 | tf_op jit(solution)/shard_map/ppermute | solution.py:283
  56.4 22.8 %collective-permute-start.14 = (bf16[128,2048]{1,0:T(8,128)(2,1)S(1)}, bf16[128,2048]{1,0:T(8,128)(2,1)S(1)}, u32[]{:S(2)}, u32[]{:S(2)}) collective-permute-start(bf16[128,2048]{1,0:T(8,128)(2,1)S(1)} %collective-permute-done.11.refs_2_.refs_8_), channel_id=1, source_target_pairs={{0,4},{4,8},{8,12},{12,14},{14,10},{10,6},{6,2},{2,0},{1,5},{5,9},... | collective-permute-start | bytes 1572872 | tf_op jit(solution)/shard_map/ppermute | solution.py:282
  68.4 22.4 %collective-permute-start.13 = (bf16[128,2176]{1,0:T(8,128)(2,1)S(1)}, bf16[128,2176]{1,0:T(8,128)(2,1)S(1)}, u32[]{:S(2)}, u32[]{:S(2)}) collective-permute-start(bf16[128,2176]{1,0:T(8,128)(2,1)S(1)} %collective-permute-done.9.refs_0_), channel_id=1, source_target_pairs={{0,4},{4,8},{8,12},{12,14},{14,10},{10,6},{6,2},{2,0},{1,5},{5,9},... | collective-permute-start | bytes 1671176 | tf_op jit(solution)/shard_map/ppermute | solution.py:282
  78.9 13.4 %collective-permute-start.16 = (bf16[128,2048]{1,0:T(8,128)(2,1)S(1)}, bf16[128,2048]{1,0:T(8,128)(2,1)S(1)}, u32[]{:S(2)}, u32[]{:S(2)}) collective-permute-start(bf16[128,2048]{1,0:T(8,128)(2,1)S(1)} %collective-permute-done.15.refs_3_.refs_11_), channel_id=1, source_target_pairs={{4,0},{8,4},{12,8},{14,12},{10,14},{6,10},{2,6},{0,2},{5,1},{9,5},... | collective-permute-start | bytes 1572872 | tf_op jit(solution)/shard_map/ppermute | solution.py:283
  88.7 13.1 %collective-permute-start.20 = (bf16[128,1024]{1,0:T(8,128)(2,1)S(1)}, bf16[128,1024]{1,0:T(8,128)(2,1)S(1)}, u32[]{:S(2)}, u32[]{:S(2)}) collective-permute-start(bf16[128,1024]{1,0:T(8,128)(2,1)S(1)} %get-tuple-element.119), channel_id=1, source_target_pairs={{0,4},{4,8},{8,12},{12,14},{14,10},{10,6},{6,2},{2,0},{1,5},{5,9},... | collective-permute-start | bytes 786440 | tf_op jit(solution)/shard_map/ppermute | solution.py:282
  90.4 11.4 %collective-permute-start.19 = (bf16[128,1024]{1,0:T(8,128)(2,1)S(1)}, bf16[128,1024]{1,0:T(8,128)(2,1)S(1)}, u32[]{:S(2)}, u32[]{:S(2)}) collective-permute-start(bf16[128,1024]{1,0:T(8,128)(2,1)S(1)} %get-tuple-element.117), channel_id=1, source_target_pairs={{4,0},{8,4},{12,8},{14,12},{10,14},{6,10},{2,6},{0,2},{5,1},{9,5},... | collective-permute-start | bytes 786440 | tf_op jit(solution)/shard_map/ppermute | solution.py:283
  99.7 9.2 %collective-permute-start.17 = (bf16[128,1024]{1,0:T(8,128)(2,1)S(1)}, bf16[128,1024]{1,0:T(8,128)(2,1)S(1)}, u32[]{:S(2)}, u32[]{:S(2)}) collective-permute-start(bf16[128,1024]{1,0:T(8,128)(2,1)S(1)} %get-tuple-element.111), channel_id=1, source_target_pairs={{4,0},{8,4},{12,8},{14,12},{10,14},{6,10},{2,6},{0,2},{5,1},{9,5},... | collective-permute-start | bytes 786440 | tf_op jit(solution)/shard_map/ppermute | solution.py:283
  100.4 9.2 %collective-permute-start.18 = (bf16[128,1024]{1,0:T(8,128)(2,1)S(1)}, bf16[128,1024]{1,0:T(8,128)(2,1)S(1)}, u32[]{:S(2)}, u32[]{:S(2)}) collective-permute-start(bf16[128,1024]{1,0:T(8,128)(2,1)S(1)} %get-tuple-element.112), channel_id=1, source_target_pairs={{0,4},{4,8},{8,12},{12,14},{14,10},{10,6},{6,2},{2,0},{1,5},{5,9},... | collective-permute-start | bytes 786440 | tf_op jit(solution)/shard_map/ppermute | solution.py:282
  101.9 10.7 %collective-permute-start.24 = (bf16[128,1024]{1,0:T(8,128)(2,1)S(1)}, bf16[128,1024]{1,0:T(8,128)(2,1)S(1)}, u32[]{:S(2)}, u32[]{:S(2)}) collective-permute-start(bf16[128,1024]{1,0:T(8,128)(2,1)S(1)} %add_convert_fusion.10), channel_id=1, source_target_pairs={{0,4},{4,8},{8,12},{12,14},{14,10},{10,6},{6,2},{2,0},{1,5},{5,9},... | collective-permute-start | bytes 786440 | tf_op jit(solution)/shard_map/ppermute | solution.py:282
  103.5 9.1 %collective-permute-start.23 = (bf16[128,1024]{1,0:T(8,128)(2,1)S(1)}, bf16[128,1024]{1,0:T(8,128)(2,1)S(1)}, u32[]{:S(2)}, u32[]{:S(2)}) collective-permute-start(bf16[128,1024]{1,0:T(8,128)(2,1)S(1)} %add_convert_fusion.11), channel_id=1, source_target_pairs={{4,0},{8,4},{12,8},{14,12},{10,14},{6,10},{2,6},{0,2},{5,1},{9,5},... | collective-permute-start | bytes 786440 | tf_op jit(solution)/shard_map/ppermute | solution.py:283
  108.1 21.7 %collective-permute-start.29 = (bf16[2048,384]{1,0:T(8,128)(2,1)S(1)}, bf16[2048,384]{1,0:T(8,128)(2,1)S(1)}, u32[]{:S(2)}, u32[]{:S(2)}) collective-permute-start(bf16[2048,384]{1,0:T(8,128)(2,1)S(1)} %get-tuple-element.128), channel_id=1, source_target_pairs={{0,1},{1,0},{2,3},{3,2},{4,5},{5,4},{6,7},{7,6},{8,9},{9,8},{10,11... | collective-permute-start | bytes 4718600 | tf_op jit(solution)/shard_map/ppermute | solution.py:284
  108.9 20.9 %collective-permute-start.30 = (bf16[2048,384]{1,0:T(8,128)(2,1)S(1)}, bf16[2048,384]{1,0:T(8,128)(2,1)S(1)}, u32[]{:S(2)}, u32[]{:S(2)}) collective-permute-start(bf16[2048,384]{1,0:T(8,128)(2,1)S(1)} %get-tuple-element.165), channel_id=1, source_target_pairs={{0,1},{1,0},{2,3},{3,2},{4,5},{5,4},{6,7},{7,6},{8,9},{9,8},{10,11... | collective-permute-start | bytes 4718600 | tf_op jit(solution)/shard_map/ppermute | solution.py:284
  109.7 12.7 %copy-start.7 = (bf16[128,2048]{1,0:T(8,128)(2,1)S(1)}, bf16[128,2048]{1,0:T(8,128)(2,1)}, u32[]{:S(2)}) copy-start(bf16[128,2048]{1,0:T(8,128)(2,1)} %refs_5_.3) | copy-start | bytes 1572868
  112.7 8.5 %collective-permute-start.25 = (bf16[128,1024]{1,0:T(8,128)(2,1)S(1)}, bf16[128,1024]{1,0:T(8,128)(2,1)S(1)}, u32[]{:S(2)}, u32[]{:S(2)}) collective-permute-start(bf16[128,1024]{1,0:T(8,128)(2,1)S(1)} %add_convert_fusion.7), channel_id=1, source_target_pairs={{4,0},{8,4},{12,8},{14,12},{10,14},{6,10},{2,6},{0,2},{5,1},{9,5},... | collective-permute-start | bytes 786440 | tf_op jit(solution)/shard_map/ppermute | solution.py:283
  113.7 11.6 %collective-permute-start.26 = (bf16[128,1024]{1,0:T(8,128)(2,1)S(1)}, bf16[128,1024]{1,0:T(8,128)(2,1)S(1)}, u32[]{:S(2)}, u32[]{:S(2)}) collective-permute-start(bf16[128,1024]{1,0:T(8,128)(2,1)S(1)} %add_convert_fusion.6), channel_id=1, source_target_pairs={{0,4},{4,8},{8,12},{12,14},{14,10},{10,6},{6,2},{2,0},{1,5},{5,9},... | collective-permute-start | bytes 786440 | tf_op jit(solution)/shard_map/ppermute | solution.py:282
  114.8 10.6 %collective-permute-start.21 = (bf16[128,1024]{1,0:T(8,128)(2,1)S(1)}, bf16[128,1024]{1,0:T(8,128)(2,1)S(1)}, u32[]{:S(2)}, u32[]{:S(2)}) collective-permute-start(bf16[128,1024]{1,0:T(8,128)(2,1)S(1)} %add_convert_fusion.9), channel_id=1, source_target_pairs={{4,0},{8,4},{12,8},{14,12},{10,14},{6,10},{2,6},{0,2},{5,1},{9,5},... | collective-permute-start | bytes 786440 | tf_op jit(solution)/shard_map/ppermute | solution.py:283
  121.2 6.4 %collective-permute-start.22 = (bf16[128,1024]{1,0:T(8,128)(2,1)S(1)}, bf16[128,1024]{1,0:T(8,128)(2,1)S(1)}, u32[]{:S(2)}, u32[]{:S(2)}) collective-permute-start(bf16[128,1024]{1,0:T(8,128)(2,1)S(1)} %add_convert_fusion.8), channel_id=1, source_target_pairs={{0,4},{4,8},{8,12},{12,14},{14,10},{10,6},{6,2},{2,0},{1,5},{5,9},... | collective-permute-start | bytes 786440 | tf_op jit(solution)/shard_map/ppermute | solution.py:282
  125.3 11.8 %collective-permute-start.33 = (bf16[384,2048]{1,0:T(8,128)(2,1)S(1)}, bf16[384,2048]{1,0:T(8,128)(2,1)S(1)}, u32[]{:S(2)}, u32[]{:S(2)}) collective-permute-start(bf16[384,2048]{1,0:T(8,128)(2,1)S(1)} %down_grads.2), channel_id=1, source_target_pairs={{0,1},{1,0},{2,3},{3,2},{4,5},{5,4},{6,7},{7,6},{8,9},{9,8},{10,11... | collective-permute-start | bytes 4718600 | tf_op jit(solution)/shard_map/ppermute | solution.py:284
  127.7 7.1 %collective-permute-start.27 = (bf16[128,1024]{1,0:T(8,128)(2,1)S(1)}, bf16[128,1024]{1,0:T(8,128)(2,1)S(1)}, u32[]{:S(2)}, u32[]{:S(2)}) collective-permute-start(bf16[128,1024]{1,0:T(8,128)(2,1)S(1)} %add_convert_fusion.5), channel_id=1, source_target_pairs={{4,0},{8,4},{12,8},{14,12},{10,14},{6,10},{2,6},{0,2},{5,1},{9,5},... | collective-permute-start | bytes 786440 | tf_op jit(solution)/shard_map/ppermute | solution.py:283
  128.4 6.6 %collective-permute-start.28 = (bf16[128,1024]{1,0:T(8,128)(2,1)S(1)}, bf16[128,1024]{1,0:T(8,128)(2,1)S(1)}, u32[]{:S(2)}, u32[]{:S(2)}) collective-permute-start(bf16[128,1024]{1,0:T(8,128)(2,1)S(1)} %add_convert_fusion.4), channel_id=1, source_target_pairs={{0,4},{4,8},{8,12},{12,14},{14,10},{10,6},{6,2},{2,0},{1,5},{5,9},... | collective-permute-start | bytes 786440 | tf_op jit(solution)/shard_map/ppermute | solution.py:282
  135.1 6.4 %collective-permute-start.31 = (bf16[128,1024]{1,0:T(8,128)(2,1)S(1)}, bf16[128,1024]{1,0:T(8,128)(2,1)S(1)}, u32[]{:S(2)}, u32[]{:S(2)}) collective-permute-start(bf16[128,1024]{1,0:T(8,128)(2,1)S(1)} %add_convert_fusion.3), channel_id=1, source_target_pairs={{4,0},{8,4},{12,8},{14,12},{10,14},{6,10},{2,6},{0,2},{5,1},{9,5},... | collective-permute-start | bytes 786440 | tf_op jit(solution)/shard_map/ppermute | solution.py:283
  136.5 6.4 %collective-permute-start.32 = (bf16[128,1024]{1,0:T(8,128)(2,1)S(1)}, bf16[128,1024]{1,0:T(8,128)(2,1)S(1)}, u32[]{:S(2)}, u32[]{:S(2)}) collective-permute-start(bf16[128,1024]{1,0:T(8,128)(2,1)S(1)} %add_convert_fusion.2), channel_id=1, source_target_pairs={{0,4},{4,8},{8,12},{12,14},{14,10},{10,6},{6,2},{2,0},{1,5},{5,9},... | collective-permute-start | bytes 786440 | tf_op jit(solution)/shard_map/ppermute | solution.py:282

commit v4 on v2

--- a/solution.py
+++ b/solution.py
@@ -286,7 +286,7 @@
     wide, half = jnp.float32, jnp.bfloat16
 
     packed = pack(tokens, routes, gates, helper, home_cap)
-    packed, own = tied((packed, (w_gate[0], w_up[0], w_down[0])))
+    own = (w_gate[0], w_up[0], w_down[0])
     weights = own + tuple(other(value) for value in own)
     turned, acts, hiddens, cots = [], [], [], []
 
@@ -322,12 +322,12 @@
 
     def far_rows():
         parts = row_grads(turned, [act[1] for act in acts])
-        sent["gate"], sent["up"] = (other(part) for part in parts)
+        sent["gate"], sent["up"] = parts
         return parts[0]
 
     def far_down():
         part = down_grads([hid[1] for hid in hiddens], cots)
-        sent["down"] = other(part)
+        sent["down"] = part
         return part
 
     def own_rows():
@@ -339,7 +339,8 @@
         out["down"] = down_grads([hid[0] for hid in hiddens], cots, (sent["down"],))
         return out["down"]
 
-    chores = [far_rows, far_down, own_rows, own_down]
+    chores = [far_rows, far_down, own_down, own_rows]
+    swapped = []
 
     def before_chore(first, second):
         first, second, turned[-1], cots[-1] = tied((first, second, turned[-1], cots[-1]))
@@ -350,17 +351,29 @@
         return first, second
 
     for s in range(reach - 1):
-        if s + 1 < reach - 1:
+        more = s + 1 < reach - 1
+        if more:
             high_down, low_up = plus(high_down, below_high[s + 1]), plus(low_up, above_low[s + 1])
             high_down, low_up = before_chore(high_down, low_up)
             high_down, low_up = down(high_down), up(low_up)
-        if s != 1 and chores:
+        if s > 0 and chores:
             low_down, high_up = after_chore(low_down, high_up)
+        if s > 0 and more:
+            low_down, high_up, high_down, low_up = tied((low_down, high_up, high_down, low_up))
         low_down, high_up = plus(low_down, below_low[s]), plus(high_up, above_high[s])
         low_down, high_up = before_chore(low_down, high_up)
+        if len(chores) == 2 and not swapped:
+            names = list(sent)
+            low_down, high_up, parts = tied((low_down, high_up, tuple(sent[name] for name in names)))
+            sent.update((name, other(part)) for name, part in zip(names, parts))
+            swapped.append(True)
         low_down, high_up = down(low_down), up(high_up)
         if s == 0 and chores:
             high_down, low_up = after_chore(high_down, low_up)
+    if not swapped:
+        while len(chores) > 2:
+            low_down, high_up = after_chore(low_down, high_up)
+        sent.update((name, other(part)) for name, part in list(sent.items()))
     while chores:
         low_down, high_up = after_chore(low_down, high_up)
 

time: 145 us -> 144 us (level)
    ppermute x14, waiting for transfers between devices: 12.1 us -> 6.4 us  [ring_local(): up = lambda value: lax.ppermute(value, 'expert', up_pairs)]
    ppermute x14, waiting for transfers between devices: 29.2 us -> 33.1 us  [ring_local(): down = lambda value: lax.ppermute(value, 'expert', down_pairs)]
    ppermute x14, starting transfers between devices: 8.92 us -> 7.31 us  [ring_local(): down = lambda value: lax.ppermute(value, 'expert', down_pairs)]
  transfers between devices with their start and end apart: 34 -> 34, of which waited for: 16 -> 15; matrix products, arithmetic and copies ran while one was open for 0% -> 0% of each run, Pallas kernels for 41% -> 42%
where the time goes in v4:
time: 144 us
  Pallas kernels  60.8 us (42%)
  waiting for transfers between devices  40.8 us (28%)
  starting transfers between devices  33.8 us (23%)
  local copies, waits for them, and re-layouts  6.34 us (4%)
  other arithmetic  1.6 us (1%)
    pallas_call x5, Pallas kernels, expert_batch(): pl.pallas_call(functools.partial(expert_kernel, len(blocks), experts), in...  42.7 us
    ppermute x14, waiting for transfers between devices, ring_local(): down = lambda value: lax.ppermute(value, 'expert', down_pairs)  33.1 us
    ppermute x14, starting transfers between devices, ring_local(): up = lambda value: lax.ppermute(value, 'expert', up_pairs)  24.8 us
    pallas_call x2, Pallas kernels, row_grads(): pl.pallas_call(functools.partial(row_kernel, len(acts), len(terms)), grid...  9.12 us
    ppermute x14, starting transfers between devices, ring_local(): down = lambda value: lax.ppermute(value, 'expert', down_pairs)  7.31 us
    pallas_call x2, Pallas kernels, down_grads(): pl.pallas_call(functools.partial(down_kernel, len(hiddens), len(cots), le...  6.78 us
    ppermute x14, waiting for transfers between devices, ring_local(): up = lambda value: lax.ppermute(value, 'expert', up_pairs)  6.4 us
    unnamed x18, local copies, waits for them, and re-layouts  6.34 us
  transfers between devices with their start and end apart: 34, of which 15 were waited for; matrix products, arithmetic and copies ran while one was open for 0% of the time, Pallas kernels for 42%

profile of v4, /device:TPU:0, one launch (start us, length us, event | category | flops | bytes accessed | tf_op | source)
XLA Modules:
  0.0 144.1 jit_solution(12220781277816878888)
XLA Ops:
  0.6 0.5 collective-permute-start
  1.1 0.1 collective-permute-start.1
  1.2 0.4 collective-permute-start.2
  1.7 2.2 %pack.1.refs_0_ = bf16[128,2176]{1,0:T(8,128)(2,1)} custom-call(s32[4,128]{1,0:T(4,128)} %bitcast.28, f32[4,128]{1,0:T(4,128)} %bitcast.29, s32[1,16]{1,0:T(1,128)} %bitcast.30, bf16[128,2048]{1,0:T(8,128)(2,1)} %tokens_ref.1), custom_call_target="tpu_custom_call" | custom-call | tf_op jit(solution)/shard_map/pack/pallas_call | solution.py:70
  3.8 2.7 %collective-permute-start.3 = (bf16[128,2176]{1,0:T(8,128)(2,1)}, bf16[128,2176]{1,0:T(8,128)(2,1)S(1)}, u32[]{:S(2)}, u32[]{:S(2)}) collective-permute-start(bf16[128,2176]{1,0:T(8,128)(2,1)} %pack.1.refs_0_), channel_id=1, source_target_pairs={{0,4},{4,8},{8,12},{12,14},{14,10},{10,6},{6,2},{2,0},{1,5},{5,9},... | collective-permute-start | bytes 1671176 | tf_op jit(solution)/shard_map/ppermute | solution.py:282
  6.5 1.9 %collective-permute-start.8 = (bf16[128,2048]{1,0:T(8,128)(2,1)}, bf16[128,2048]{1,0:T(8,128)(2,1)S(1)}, u32[]{:S(2)}, u32[]{:S(2)}) collective-permute-start(bf16[128,2048]{1,0:T(8,128)(2,1)} %refs_5_.3), channel_id=1, source_target_pairs={{4,0},{8,4},{12,8},{14,12},{10,14},{6,10},{2,6},{0,2},{5,1},{9,5},... | collective-permute-start | bytes 1572872 | tf_op jit(solution)/shard_map/ppermute | solution.py:283
  8.4 0.5 collective-permute-done.1.refs_6_.refs_8_
  8.9 2.9 %collective-permute-start.7 = (bf16[128,2048]{1,0:T(8,128)(2,1)}, bf16[128,2048]{1,0:T(8,128)(2,1)S(1)}, u32[]{:S(2)}, u32[]{:S(2)}) collective-permute-start(bf16[128,2048]{1,0:T(8,128)(2,1)} %refs_5_.3), channel_id=1, source_target_pairs={{0,4},{4,8},{8,12},{12,14},{14,10},{10,6},{6,2},{2,0},{1,5},{5,9},... | collective-permute-start | bytes 1572872 | tf_op jit(solution)/shard_map/ppermute | solution.py:282
  11.8 1.4 copy-done
  13.3 1.4 copy-done.2
  14.7 1.4 copy-done.4
  16.1 1.0 copy-done.6
  17.1 1.1 copy-done.8
  18.2 7.3 %expert_batch.5 = (bf16[2048,128]{1,0:T(8,128)(2,1)S(1)}, bf16[128,768]{1,0:T(8,128)(2,1)S(1)}, bf16[128,768]{1,0:T(8,128)(2,1)S(1)}, bf16[384,128]{1,0:T(8,128)...) custom-call(bf16[128,2176]{1,0:T(8,128)(2,1)S(1)} %copy-done.8, ...), custom_call_target="tpu_custom_call" | custom-call | flops 1024 | bytes 1024 | tf_op jit(solution)/shard_map/expert_batch/pallas_call | solution.py:169
  25.5 1.6 %collective-permute-start.5 = (bf16[128,2176]{1,0:T(8,128)(2,1)S(1)}, bf16[128,2176]{1,0:T(8,128)(2,1)S(1)}, u32[]{:S(2)}, u32[]{:S(2)}) collective-permute-start(bf16[128,2176]{1,0:T(8,128)(2,1)S(1)} %collective-permute-done.3.refs_0_), channel_id=1, source_target_pairs={{0,4},{4,8},{8,12},{12,14},{14,10},{10,6},{6,2},{2,0},{1,5},{5,9},... | collective-permute-start | bytes 1671176 | tf_op jit(solution)/shard_map/ppermute | solution.py:282
  27.2 0.4 collective-permute-start.6
  27.6 5.8 %collective-permute-done.8.refs_3_.refs_7_ = bf16[128,2048]{1,0:T(8,128)(2,1)S(1)} collective-permute-done((bf16[128,2048]{1,0:T(8,128)(2,1)}, bf16[128,2048]{1,0:T(8,128)(2,1)S(1)}, u32[]{:S(2)}, u32[]{:S(2)}) %collective-permute-start.8) | collective-permute-done | bytes 524320 | tf_op jit(solution)/shard_map/ppermute | solution.py:283
  33.4 2.0 %collective-permute-start.11 = (bf16[128,2048]{1,0:T(8,128)(2,1)S(1)}, bf16[128,2048]{1,0:T(8,128)(2,1)S(1)}, u32[]{:S(2)}, u32[]{:S(2)}) collective-permute-start(bf16[128,2048]{1,0:T(8,128)(2,1)S(1)} %collective-permute-done.7.refs_2_.refs_6_), channel_id=1, source_target_pairs={{0,4},{4,8},{8,12},{12,14},{14,10},{10,6},{6,2},{2,0},{1,5},{5,9},... | collective-permute-start | bytes 1572872 | tf_op jit(solution)/shard_map/ppermute | solution.py:282
  35.4 9.4 %expert_batch.6 = (bf16[2048,256]{1,0:T(8,128)(2,1)S(1)}, bf16[256,768]{1,0:T(8,128)(2,1)S(1)}, bf16[256,768]{1,0:T(8,128)(2,1)S(1)}, bf16[384,256]{1,0:T(8,128)...) custom-call(bf16[128,2176]{1,0:T(8,128)(2,1)S(1)} %collective-permut, ...), custom_call_target="tpu_custom_call" | custom-call | flops 1024 | bytes 1024 | tf_op jit(solution)/shard_map/expert_batch/pallas_call | solution.py:169
  44.8 0.5 collective-permute-done.6.refs_1_
  45.3 2.0 %collective-permute-start.9 = (bf16[128,2176]{1,0:T(8,128)(2,1)S(1)}, bf16[128,2176]{1,0:T(8,128)(2,1)S(1)}, u32[]{:S(2)}, u32[]{:S(2)}) collective-permute-start(bf16[128,2176]{1,0:T(8,128)(2,1)S(1)} %collective-permute-done.5.refs_0_), channel_id=1, source_target_pairs={{0,4},{4,8},{8,12},{12,14},{14,10},{10,6},{6,2},{2,0},{1,5},{5,9},... | collective-permute-start | bytes 1671176 | tf_op jit(solution)/shard_map/ppermute | solution.py:282
  47.4 9.2 %collective-permute-done.12.refs_3_.refs_9_ = bf16[128,2048]{1,0:T(8,128)(2,1)S(1)} collective-permute-done((bf16[128,2048]{1,0:T(8,128)(2,1)S(1)}, bf16[128,2048]{1,0:T(8,128)(2,1)S(1)}, u32[]{:S(2)}, u32[]{:S(2)}) %collective-permute-start.12) | collective-permute-done | bytes 524320 | tf_op jit(solution)/shard_map/ppermute | solution.py:283
  56.6 2.0 %collective-permute-start.14 = (bf16[128,2048]{1,0:T(8,128)(2,1)S(1)}, bf16[128,2048]{1,0:T(8,128)(2,1)S(1)}, u32[]{:S(2)}, u32[]{:S(2)}) collective-permute-start(bf16[128,2048]{1,0:T(8,128)(2,1)S(1)} %collective-permute-done.11.refs_2_.refs_8_), channel_id=1, source_target_pairs={{0,4},{4,8},{8,12},{12,14},{14,10},{10,6},{6,2},{2,0},{1,5},{5,9},... | collective-permute-start | bytes 1572872 | tf_op jit(solution)/shard_map/ppermute | solution.py:282
  58.6 9.4 %expert_batch.7 = (bf16[2048,256]{1,0:T(8,128)(2,1)S(1)}, bf16[256,768]{1,0:T(8,128)(2,1)S(1)}, bf16[256,768]{1,0:T(8,128)(2,1)S(1)}, bf16[384,256]{1,0:T(8,128)...) custom-call(bf16[128,2176]{1,0:T(8,128)(2,1)S(1)} %collective-permut, ...), custom_call_target="tpu_custom_call" | custom-call | flops 1024 | bytes 1024 | tf_op jit(solution)/shard_map/expert_batch/pallas_call | solution.py:169
  68.0 0.5 collective-permute-done.10.refs_1_
  68.5 1.6 %collective-permute-start.13 = (bf16[128,2176]{1,0:T(8,128)(2,1)S(1)}, bf16[128,2176]{1,0:T(8,128)(2,1)S(1)}, u32[]{:S(2)}, u32[]{:S(2)}) collective-permute-start(bf16[128,2176]{1,0:T(8,128)(2,1)S(1)} %collective-permute-done.9.refs_0_), channel_id=1, source_target_pairs={{0,4},{4,8},{8,12},{12,14},{14,10},{10,6},{6,2},{2,0},{1,5},{5,9},... | collective-permute-start | bytes 1671176 | tf_op jit(solution)/shard_map/ppermute | solution.py:282
  70.1 8.9 %collective-permute-done.15.refs_3_.refs_11_ = bf16[128,2048]{1,0:T(8,128)(2,1)S(1)} collective-permute-done((bf16[128,2048]{1,0:T(8,128)(2,1)S(1)}, bf16[128,2048]{1,0:T(8,128)(2,1)S(1)}, u32[]{:S(2)}, u32[]{:S(2)}) %collective-permute-start.15) | collective-permute-done | bytes 524320 | tf_op jit(solution)/shard_map/ppermute | solution.py:283
  79.0 0.3 collective-permute-start.16
  79.3 9.3 %expert_batch.8 = (bf16[2048,256]{1,0:T(8,128)(2,1)S(1)}, bf16[256,768]{1,0:T(8,128)(2,1)S(1)}, bf16[256,768]{1,0:T(8,128)(2,1)S(1)}, bf16[384,256]{1,0:T(8,128)...) custom-call(bf16[128,2176]{1,0:T(8,128)(2,1)S(1)} %collective-permut, ...), custom_call_target="tpu_custom_call" | custom-call | flops 1024 | bytes 1024 | tf_op jit(solution)/shard_map/expert_batch/pallas_call | solution.py:169
  88.6 1.8 %collective-permute-start.20 = (bf16[128,1024]{1,0:T(8,128)(2,1)S(1)}, bf16[128,1024]{1,0:T(8,128)(2,1)S(1)}, u32[]{:S(2)}, u32[]{:S(2)}) collective-permute-start(bf16[128,1024]{1,0:T(8,128)(2,1)S(1)} %get-tuple-element.114), channel_id=1, source_target_pairs={{0,4},{4,8},{8,12},{12,14},{14,10},{10,6},{6,2},{2,0},{1,5},{5,9},... | collective-permute-start | bytes 786440 | tf_op jit(solution)/shard_map/ppermute | solution.py:282
  90.4 0.3 collective-permute-start.19
  90.7 1.7 %collective-permute-done.16.refs_1_.refs_12_ = bf16[128,2048]{1,0:T(8,128)(2,1)S(1)} collective-permute-done((bf16[128,2048]{1,0:T(8,128)(2,1)S(1)}, bf16[128,2048]{1,0:T(8,128)(2,1)S(1)}, u32[]{:S(2)}, u32[]{:S(2)}) %collective-permute-start.16) | collective-permute-done | bytes 524320 | tf_op jit(solution)/shard_map/ppermute | solution.py:283
  92.4 7.3 %expert_batch.9 = (bf16[2048,128]{1,0:T(8,128)(2,1)S(1)}, bf16[128,768]{1,0:T(8,128)(2,1)S(1)}, bf16[128,768]{1,0:T(8,128)(2,1)S(1)}, bf16[384,128]{1,0:T(8,128)...) custom-call(bf16[128,2176]{1,0:T(8,128)(2,1)S(1)} %collective-permute-done.13., ...), custom_call_target="tpu_custom_call" | custom-call | flops 1024 | bytes 1024 | tf_op jit(solution)/shard_map/expert_batch/pallas_call | solution.py:169
  99.7 1.6 %collective-permute-start.18 = (bf16[128,1024]{1,0:T(8,128)(2,1)S(1)}, bf16[128,1024]{1,0:T(8,128)(2,1)S(1)}, u32[]{:S(2)}, u32[]{:S(2)}) collective-permute-start(bf16[128,1024]{1,0:T(8,128)(2,1)S(1)} %get-tuple-element.110), channel_id=1, source_target_pairs={{0,4},{4,8},{8,12},{12,14},{14,10},{10,6},{6,2},{2,0},{1,5},{5,9},... | collective-permute-start | bytes 786440 | tf_op jit(solution)/shard_map/ppermute | solution.py:282
  101.4 0.5 collective-permute-start.17
  102.0 0.7 collective-permute-start.23
  102.6 1.4 collective-permute-start.24
  104.0 4.9 %collective-permute-done.18 = bf16[128,1024]{1,0:T(8,128)(2,1)S(1)} collective-permute-done((bf16[128,1024]{1,0:T(8,128)(2,1)S(1)}, bf16[128,1024]{1,0:T(8,128)(2,1)S(1)}, u32[]{:S(2)}, u32[]{:S(2)}) %collective-permute-start.18) | collective-permute-done | bytes 262176 | tf_op jit(solution)/shard_map/ppermute | solution.py:282
  109.0 1.4 collective-permute-done.17
  110.4 4.1 %row_grads.2 = (bf16[2048,384]{1,0:T(8,128)(2,1)S(1)}, bf16[2048,384]{1,0:T(8,128)(2,1)S(1)}) custom-call(bf16[2048,128]{1,0:T(8,128)(2,1)S(1)} %get-tuple-element.128.refs_0_, bf16[2048,256]{1,0:T(8,128)(2,1)S(1)} %get-tuple-element.129.refs_1_, bf16[2048,256]{1,0:T(8,128)(2,1)S(1)} %get-tuple-element.130.refs_2_, ...), custom_call_target="tpu_custom_call" | custom-call | flops 1024 | bytes 1024 | tf_op jit(solution)/shard_map/row_grads/pallas_call | solution.py:219
  114.5 0.1 add_convert_fusion.6
  114.6 0.1 add_convert_fusion.7
  114.6 0.5 collective-permute-start.21
  115.1 1.6 %collective-permute-start.22 = (bf16[128,1024]{1,0:T(8,128)(2,1)S(1)}, bf16[128,1024]{1,0:T(8,128)(2,1)S(1)}, u32[]{:S(2)}, u32[]{:S(2)}) collective-permute-start(bf16[128,1024]{1,0:T(8,128)(2,1)S(1)} %add_convert_fusion.10), channel_id=1, source_target_pairs={{0,4},{4,8},{8,12},{12,14},{14,10},{10,6},{6,2},{2,0},{1,5},{5,9},... | collective-permute-start | bytes 786440 | tf_op jit(solution)/shard_map/ppermute | solution.py:282
  116.7 0.5 collective-permute-start.25
  117.2 1.6 %collective-permute-start.26 = (bf16[128,1024]{1,0:T(8,128)(2,1)S(1)}, bf16[128,1024]{1,0:T(8,128)(2,1)S(1)}, u32[]{:S(2)}, u32[]{:S(2)}) collective-permute-start(bf16[128,1024]{1,0:T(8,128)(2,1)S(1)} %add_convert_fusion.6), channel_id=1, source_target_pairs={{0,4},{4,8},{8,12},{12,14},{14,10},{10,6},{6,2},{2,0},{1,5},{5,9},... | collective-permute-start | bytes 786440 | tf_op jit(solution)/shard_map/ppermute | solution.py:282
  118.7 3.0 %down_grads.2 = bf16[384,2048]{1,0:T(8,128)(2,1)S(1)} custom-call(bf16[384,128]{1,0:T(8,128)(2,1)S(1)} %get-tuple-element.121.refs_0_, bf16[384,256]{1,0:T(8,128)(2,1)S(1)} %get-tuple-element.122.refs_1_, bf16[384,256]{1,0:T(8,128)(2,1)S(1)} %get-tuple-element.123.refs_2_, bf16[384,256]{1,0:T(8,128)(2,1)S(1)} %get-tuple-element.124.refs_3_, ...), custom_call_target="tpu_custom_call" | custom-call | flops 1024 | bytes 1024 | tf_op jit(solution)/shard_map/down_grads/pallas_call | solution.py:258
  121.7 2.6 %collective-permute-done.25 = bf16[128,1024]{1,0:T(8,128)(2,1)S(1)} collective-permute-done((bf16[128,1024]{1,0:T(8,128)(2,1)S(1)}, bf16[128,1024]{1,0:T(8,128)(2,1)S(1)}, u32[]{:S(2)}, u32[]{:S(2)}) %collective-permute-start.25) | collective-permute-done | bytes 262176 | tf_op jit(solution)/shard_map/ppermute | solution.py:283
  124.5 0.1 collective-permute-start.29
  124.6 0.5 collective-permute-start.32
  125.0 0.1 collective-permute-start.33
  125.1 1.2 collective-permute-start.27
  126.3 0.8 collective-permute-start.28
  127.2 0.8 collective-permute-done.29.refs_13_
  128.0 3.8 %down_grads.3 = bf16[384,2048]{1,0:T(8,128)(2,1)} custom-call(bf16[384,128]{1,0:T(8,128)(2,1)S(1)} %get-tuple-element.159.refs_0_, bf16[384,256]{1,0:T(8,128)(2,1)S(1)} %get-tuple-element.160.refs_1_, bf16[384,256]{1,0:T(8,128)(2,1)S(1)} %get-tuple-element.161.refs_2_, bf16[384,256]{1,0:T(8,128)(2,1)S(1)} %get-tuple-element.162.refs_3_, ...), custom_call_target="tpu_custom_call" | custom-call | flops 1024 | bytes 1024 | tf_op jit(solution)/shard_map/down_grads/pallas_call | solution.py:258
  131.8 2.0 %collective-permute-done.27 = bf16[128,1024]{1,0:T(8,128)(2,1)S(1)} collective-permute-done((bf16[128,1024]{1,0:T(8,128)(2,1)S(1)}, bf16[128,1024]{1,0:T(8,128)(2,1)S(1)}, u32[]{:S(2)}, u32[]{:S(2)}) %collective-permute-start.27) | collective-permute-done | bytes 262176 | tf_op jit(solution)/shard_map/ppermute | solution.py:283
  133.8 0.9 collective-permute-done.28
  134.8 0.9 collective-permute-start.30
  135.8 1.1 collective-permute-start.31
  136.9 5.0 %row_grads.3 = (bf16[2048,384]{1,0:T(8,128)(2,1)}, bf16[2048,384]{1,0:T(8,128)(2,1)}) custom-call(bf16[2048,128]{1,0:T(8,128)(2,1)S(1)} %get-tuple-element.128.refs_0_, bf16[2048,256]{1,0:T(8,128)(2,1)S(1)} %get-tuple-element.129.refs_1_, bf16[2048,256]{1,0:T(8,128)(2,1)S(1)} %get-tuple-element.130.refs_2_, ...), custom_call_target="tpu_custom_call" | custom-call | flops 1024 | bytes 1024 | tf_op jit(solution)/shard_map/row_grads/pallas_call | solution.py:219
  141.9 0.5 collective-permute-done.30
  142.4 0.6 collective-permute-done.31
  143.0 0.2 add_convert_fusion
  143.3 0.8 pad_maximum_fusion
  (44 shorter events, 0.5 us)
Async XLA Ops:
  0.6 5.8 %collective-permute-start = (bf16[2048,384]{1,0:T(8,128)(2,1)}, bf16[2048,384]{1,0:T(8,128)(2,1)S(1)}, u32[]{:S(2)}, u32[]{:S(2)}) collective-permute-start(bf16[2048,384]{1,0:T(8,128)(2,1)} %bitcast.9), channel_id=1, source_target_pairs={{0,1},{1,0},{2,3},{3,2},{4,5},{5,4},{6,7},{7,6},{8,9},{9,8},{10,11... | collective-permute-start | bytes 4718600 | tf_op jit(solution)/shard_map/ppermute | solution.py:284
  1.1 7.7 %collective-permute-start.1 = (bf16[2048,384]{1,0:T(8,128)(2,1)}, bf16[2048,384]{1,0:T(8,128)(2,1)S(1)}, u32[]{:S(2)}, u32[]{:S(2)}) collective-permute-start(bf16[2048,384]{1,0:T(8,128)(2,1)} %bitcast.15), channel_id=1, source_target_pairs={{0,1},{1,0},{2,3},{3,2},{4,5},{5,4},{6,7},{7,6},{8,9},{9,8},{10,11... | collective-permute-start | bytes 4718600 | tf_op jit(solution)/shard_map/ppermute | solution.py:284
  1.2 10.6 %collective-permute-start.2 = (bf16[384,2048]{1,0:T(8,128)(2,1)}, bf16[384,2048]{1,0:T(8,128)(2,1)}, u32[]{:S(2)}, u32[]{:S(2)}) collective-permute-start(bf16[384,2048]{1,0:T(8,128)(2,1)} %bitcast.21), channel_id=1, source_target_pairs={{0,1},{1,0},{2,3},{3,2},{4,5},{5,4},{6,7},{7,6},{8,9},{9,8},{10,11... | collective-permute-start | bytes 4718600 | tf_op jit(solution)/shard_map/ppermute | solution.py:284
  3.8 21.7 %collective-permute-start.3 = (bf16[128,2176]{1,0:T(8,128)(2,1)}, bf16[128,2176]{1,0:T(8,128)(2,1)S(1)}, u32[]{:S(2)}, u32[]{:S(2)}) collective-permute-start(bf16[128,2176]{1,0:T(8,128)(2,1)} %pack.1.refs_0_), channel_id=1, source_target_pairs={{0,4},{4,8},{8,12},{12,14},{14,10},{10,6},{6,2},{2,0},{1,5},{5,9},... | collective-permute-start | bytes 1671176 | tf_op jit(solution)/shard_map/ppermute | solution.py:282
  6.5 19.0 %collective-permute-start.4 = (bf16[128,2176]{1,0:T(8,128)(2,1)}, bf16[128,2176]{1,0:T(8,128)(2,1)S(1)}, u32[]{:S(2)}, u32[]{:S(2)}) collective-permute-start(bf16[128,2176]{1,0:T(8,128)(2,1)} %pack.1.refs_0_), channel_id=1, source_target_pairs={{4,0},{8,4},{12,8},{14,12},{10,14},{6,10},{2,6},{0,2},{5,1},{9,5},... | collective-permute-start | bytes 1671176 | tf_op jit(solution)/shard_map/ppermute | solution.py:283
  6.5 26.9 %collective-permute-start.8 = (bf16[128,2048]{1,0:T(8,128)(2,1)}, bf16[128,2048]{1,0:T(8,128)(2,1)S(1)}, u32[]{:S(2)}, u32[]{:S(2)}) collective-permute-start(bf16[128,2048]{1,0:T(8,128)(2,1)} %refs_5_.3), channel_id=1, source_target_pairs={{4,0},{8,4},{12,8},{14,12},{10,14},{6,10},{2,6},{0,2},{5,1},{9,5},... | collective-permute-start | bytes 1572872 | tf_op jit(solution)/shard_map/ppermute | solution.py:283
  8.9 24.5 %collective-permute-start.7 = (bf16[128,2048]{1,0:T(8,128)(2,1)}, bf16[128,2048]{1,0:T(8,128)(2,1)S(1)}, u32[]{:S(2)}, u32[]{:S(2)}) collective-permute-start(bf16[128,2048]{1,0:T(8,128)(2,1)} %refs_5_.3), channel_id=1, source_target_pairs={{0,4},{4,8},{8,12},{12,14},{14,10},{10,6},{6,2},{2,0},{1,5},{5,9},... | collective-permute-start | bytes 1572872 | tf_op jit(solution)/shard_map/ppermute | solution.py:282
  11.8 1.4 copy-start
  13.3 1.4 copy-start.2
  14.7 1.4 copy-start.4
  16.1 1.0 copy-start.6
  17.1 1.1 copy-start.8
  18.2 17.3 %copy-start.1 = (bf16[1,2048,384]{2,1,0:T(8,128)(2,1)S(1)}, bf16[1,2048,384]{2,1,0:T(8,128)(2,1)}, u32[]{:S(2)}) copy-start(bf16[1,2048,384]{2,1,0:T(8,128)(2,1)} %param.13) | copy-start | bytes 4718596
  18.2 17.3 %copy-start.3 = (bf16[1,2048,384]{2,1,0:T(8,128)(2,1)S(1)}, bf16[1,2048,384]{2,1,0:T(8,128)(2,1)}, u32[]{:S(2)}) copy-start(bf16[1,2048,384]{2,1,0:T(8,128)(2,1)} %param.14) | copy-start | bytes 4718596
  25.5 33.1 %copy-start.5 = (bf16[1,384,2048]{2,1,0:T(8,128)(2,1)S(1)}, bf16[1,384,2048]{2,1,0:T(8,128)(2,1)}, u32[]{:S(2)}) copy-start(bf16[1,384,2048]{2,1,0:T(8,128)(2,1)} %param.15) | copy-start | bytes 4718596
  25.5 19.3 %collective-permute-start.5 = (bf16[128,2176]{1,0:T(8,128)(2,1)S(1)}, bf16[128,2176]{1,0:T(8,128)(2,1)S(1)}, u32[]{:S(2)}, u32[]{:S(2)}) collective-permute-start(bf16[128,2176]{1,0:T(8,128)(2,1)S(1)} %collective-permute-done.3.refs_0_), channel_id=1, source_target_pairs={{0,4},{4,8},{8,12},{12,14},{14,10},{10,6},{6,2},{2,0},{1,5},{5,9},... | collective-permute-start | bytes 1671176 | tf_op jit(solution)/shard_map/ppermute | solution.py:282
  27.2 18.2 %collective-permute-start.6 = (bf16[128,2176]{1,0:T(8,128)(2,1)S(1)}, bf16[128,2176]{1,0:T(8,128)(2,1)S(1)}, u32[]{:S(2)}, u32[]{:S(2)}) collective-permute-start(bf16[128,2176]{1,0:T(8,128)(2,1)S(1)} %collective-permute-done.4.refs_1_), channel_id=1, source_target_pairs={{4,0},{8,4},{12,8},{14,12},{10,14},{6,10},{2,6},{0,2},{5,1},{9,5},... | collective-permute-start | bytes 1671176 | tf_op jit(solution)/shard_map/ppermute | solution.py:283
  33.4 23.2 %collective-permute-start.12 = (bf16[128,2048]{1,0:T(8,128)(2,1)S(1)}, bf16[128,2048]{1,0:T(8,128)(2,1)S(1)}, u32[]{:S(2)}, u32[]{:S(2)}) collective-permute-start(bf16[128,2048]{1,0:T(8,128)(2,1)S(1)} %collective-permute-done.8.refs_3_.refs_7_), channel_id=1, source_target_pairs={{4,0},{8,4},{12,8},{14,12},{10,14},{6,10},{2,6},{0,2},{5,1},{9,5},... | collective-permute-start | bytes 1572872 | tf_op jit(solution)/shard_map/ppermute | solution.py:283
  33.4 23.2 %collective-permute-start.11 = (bf16[128,2048]{1,0:T(8,128)(2,1)S(1)}, bf16[128,2048]{1,0:T(8,128)(2,1)S(1)}, u32[]{:S(2)}, u32[]{:S(2)}) collective-permute-start(bf16[128,2048]{1,0:T(8,128)(2,1)S(1)} %collective-permute-done.7.refs_2_.refs_6_), channel_id=1, source_target_pairs={{0,4},{4,8},{8,12},{12,14},{14,10},{10,6},{6,2},{2,0},{1,5},{5,9},... | collective-permute-start | bytes 1572872 | tf_op jit(solution)/shard_map/ppermute | solution.py:282
  45.3 23.2 %collective-permute-start.10 = (bf16[128,2176]{1,0:T(8,128)(2,1)S(1)}, bf16[128,2176]{1,0:T(8,128)(2,1)S(1)}, u32[]{:S(2)}, u32[]{:S(2)}) collective-permute-start(bf16[128,2176]{1,0:T(8,128)(2,1)S(1)} %collective-permute-done.6.refs_1_), channel_id=1, source_target_pairs={{4,0},{8,4},{12,8},{14,12},{10,14},{6,10},{2,6},{0,2},{5,1},{9,5},... | collective-permute-start | bytes 1671176 | tf_op jit(solution)/shard_map/ppermute | solution.py:283
  45.3 23.2 %collective-permute-start.9 = (bf16[128,2176]{1,0:T(8,128)(2,1)S(1)}, bf16[128,2176]{1,0:T(8,128)(2,1)S(1)}, u32[]{:S(2)}, u32[]{:S(2)}) collective-permute-start(bf16[128,2176]{1,0:T(8,128)(2,1)S(1)} %collective-permute-done.5.refs_0_), channel_id=1, source_target_pairs={{0,4},{4,8},{8,12},{12,14},{14,10},{10,6},{6,2},{2,0},{1,5},{5,9},... | collective-permute-start | bytes 1671176 | tf_op jit(solution)/shard_map/ppermute | solution.py:282
  56.6 22.4 %collective-permute-start.15 = (bf16[128,2048]{1,0:T(8,128)(2,1)S(1)}, bf16[128,2048]{1,0:T(8,128)(2,1)S(1)}, u32[]{:S(2)}, u32[]{:S(2)}) collective-permute-start(bf16[128,2048]{1,0:T(8,128)(2,1)S(1)} %collective-permute-done.12.refs_3_.refs_9_), channel_id=1, source_target_pairs={{4,0},{8,4},{12,8},{14,12},{10,14},{6,10},{2,6},{0,2},{5,1},{9,5},... | collective-permute-start | bytes 1572872 | tf_op jit(solution)/shard_map/ppermute | solution.py:283
  56.6 22.7 %collective-permute-start.14 = (bf16[128,2048]{1,0:T(8,128)(2,1)S(1)}, bf16[128,2048]{1,0:T(8,128)(2,1)S(1)}, u32[]{:S(2)}, u32[]{:S(2)}) collective-permute-start(bf16[128,2048]{1,0:T(8,128)(2,1)S(1)} %collective-permute-done.11.refs_2_.refs_8_), channel_id=1, source_target_pairs={{0,4},{4,8},{8,12},{12,14},{14,10},{10,6},{6,2},{2,0},{1,5},{5,9},... | collective-permute-start | bytes 1572872 | tf_op jit(solution)/shard_map/ppermute | solution.py:282
  68.5 22.2 %collective-permute-start.13 = (bf16[128,2176]{1,0:T(8,128)(2,1)S(1)}, bf16[128,2176]{1,0:T(8,128)(2,1)S(1)}, u32[]{:S(2)}, u32[]{:S(2)}) collective-permute-start(bf16[128,2176]{1,0:T(8,128)(2,1)S(1)} %collective-permute-done.9.refs_0_), channel_id=1, source_target_pairs={{0,4},{4,8},{8,12},{12,14},{14,10},{10,6},{6,2},{2,0},{1,5},{5,9},... | collective-permute-start | bytes 1671176 | tf_op jit(solution)/shard_map/ppermute | solution.py:282
  79.0 13.5 %collective-permute-start.16 = (bf16[128,2048]{1,0:T(8,128)(2,1)S(1)}, bf16[128,2048]{1,0:T(8,128)(2,1)S(1)}, u32[]{:S(2)}, u32[]{:S(2)}) collective-permute-start(bf16[128,2048]{1,0:T(8,128)(2,1)S(1)} %collective-permute-done.15.refs_3_.refs_11_), channel_id=1, source_target_pairs={{4,0},{8,4},{12,8},{14,12},{10,14},{6,10},{2,6},{0,2},{5,1},{9,5},... | collective-permute-start | bytes 1572872 | tf_op jit(solution)/shard_map/ppermute | solution.py:283
  88.6 12.7 %collective-permute-start.20 = (bf16[128,1024]{1,0:T(8,128)(2,1)S(1)}, bf16[128,1024]{1,0:T(8,128)(2,1)S(1)}, u32[]{:S(2)}, u32[]{:S(2)}) collective-permute-start(bf16[128,1024]{1,0:T(8,128)(2,1)S(1)} %get-tuple-element.114), channel_id=1, source_target_pairs={{0,4},{4,8},{8,12},{12,14},{14,10},{10,6},{6,2},{2,0},{1,5},{5,9},... | collective-permute-start | bytes 786440 | tf_op jit(solution)/shard_map/ppermute | solution.py:282
  90.4 11.5 %collective-permute-start.19 = (bf16[128,1024]{1,0:T(8,128)(2,1)S(1)}, bf16[128,1024]{1,0:T(8,128)(2,1)S(1)}, u32[]{:S(2)}, u32[]{:S(2)}) collective-permute-start(bf16[128,1024]{1,0:T(8,128)(2,1)S(1)} %get-tuple-element.112), channel_id=1, source_target_pairs={{4,0},{8,4},{12,8},{14,12},{10,14},{6,10},{2,6},{0,2},{5,1},{9,5},... | collective-permute-start | bytes 786440 | tf_op jit(solution)/shard_map/ppermute | solution.py:283
  99.7 9.2 %collective-permute-start.18 = (bf16[128,1024]{1,0:T(8,128)(2,1)S(1)}, bf16[128,1024]{1,0:T(8,128)(2,1)S(1)}, u32[]{:S(2)}, u32[]{:S(2)}) collective-permute-start(bf16[128,1024]{1,0:T(8,128)(2,1)S(1)} %get-tuple-element.110), channel_id=1, source_target_pairs={{0,4},{4,8},{8,12},{12,14},{14,10},{10,6},{6,2},{2,0},{1,5},{5,9},... | collective-permute-start | bytes 786440 | tf_op jit(solution)/shard_map/ppermute | solution.py:282
  101.4 8.9 %collective-permute-start.17 = (bf16[128,1024]{1,0:T(8,128)(2,1)S(1)}, bf16[128,1024]{1,0:T(8,128)(2,1)S(1)}, u32[]{:S(2)}, u32[]{:S(2)}) collective-permute-start(bf16[128,1024]{1,0:T(8,128)(2,1)S(1)} %get-tuple-element.108), channel_id=1, source_target_pairs={{4,0},{8,4},{12,8},{14,12},{10,14},{6,10},{2,6},{0,2},{5,1},{9,5},... | collective-permute-start | bytes 786440 | tf_op jit(solution)/shard_map/ppermute | solution.py:283
  102.0 12.5 %collective-permute-start.23 = (bf16[128,1024]{1,0:T(8,128)(2,1)S(1)}, bf16[128,1024]{1,0:T(8,128)(2,1)S(1)}, u32[]{:S(2)}, u32[]{:S(2)}) collective-permute-start(bf16[128,1024]{1,0:T(8,128)(2,1)S(1)} %add_convert_fusion.9), channel_id=1, source_target_pairs={{4,0},{8,4},{12,8},{14,12},{10,14},{6,10},{2,6},{0,2},{5,1},{9,5},... | collective-permute-start | bytes 786440 | tf_op jit(solution)/shard_map/ppermute | solution.py:283
  102.6 11.8 %collective-permute-start.24 = (bf16[128,1024]{1,0:T(8,128)(2,1)S(1)}, bf16[128,1024]{1,0:T(8,128)(2,1)S(1)}, u32[]{:S(2)}, u32[]{:S(2)}) collective-permute-start(bf16[128,1024]{1,0:T(8,128)(2,1)S(1)} %add_convert_fusion.8), channel_id=1, source_target_pairs={{0,4},{4,8},{8,12},{12,14},{14,10},{10,6},{6,2},{2,0},{1,5},{5,9},... | collective-permute-start | bytes 786440 | tf_op jit(solution)/shard_map/ppermute | solution.py:282
  114.5 4.3 %copy-start.7 = (bf16[128,2048]{1,0:T(8,128)(2,1)S(1)}, bf16[128,2048]{1,0:T(8,128)(2,1)}, u32[]{:S(2)}) copy-start(bf16[128,2048]{1,0:T(8,128)(2,1)} %refs_5_.3) | copy-start | bytes 1572868
  114.6 7.1 %collective-permute-start.21 = (bf16[128,1024]{1,0:T(8,128)(2,1)S(1)}, bf16[128,1024]{1,0:T(8,128)(2,1)S(1)}, u32[]{:S(2)}, u32[]{:S(2)}) collective-permute-start(bf16[128,1024]{1,0:T(8,128)(2,1)S(1)} %add_convert_fusion.11), channel_id=1, source_target_pairs={{4,0},{8,4},{12,8},{14,12},{10,14},{6,10},{2,6},{0,2},{5,1},{9,5},... | collective-permute-start | bytes 786440 | tf_op jit(solution)/shard_map/ppermute | solution.py:283
  115.1 6.6 %collective-permute-start.22 = (bf16[128,1024]{1,0:T(8,128)(2,1)S(1)}, bf16[128,1024]{1,0:T(8,128)(2,1)S(1)}, u32[]{:S(2)}, u32[]{:S(2)}) collective-permute-start(bf16[128,1024]{1,0:T(8,128)(2,1)S(1)} %add_convert_fusion.10), channel_id=1, source_target_pairs={{0,4},{4,8},{8,12},{12,14},{14,10},{10,6},{6,2},{2,0},{1,5},{5,9},... | collective-permute-start | bytes 786440 | tf_op jit(solution)/shard_map/ppermute | solution.py:282
  116.7 7.6 %collective-permute-start.25 = (bf16[128,1024]{1,0:T(8,128)(2,1)S(1)}, bf16[128,1024]{1,0:T(8,128)(2,1)S(1)}, u32[]{:S(2)}, u32[]{:S(2)}) collective-permute-start(bf16[128,1024]{1,0:T(8,128)(2,1)S(1)} %add_convert_fusion.7), channel_id=1, source_target_pairs={{4,0},{8,4},{12,8},{14,12},{10,14},{6,10},{2,6},{0,2},{5,1},{9,5},... | collective-permute-start | bytes 786440 | tf_op jit(solution)/shard_map/ppermute | solution.py:283
  117.2 7.2 %collective-permute-start.26 = (bf16[128,1024]{1,0:T(8,128)(2,1)S(1)}, bf16[128,1024]{1,0:T(8,128)(2,1)S(1)}, u32[]{:S(2)}, u32[]{:S(2)}) collective-permute-start(bf16[128,1024]{1,0:T(8,128)(2,1)S(1)} %add_convert_fusion.6), channel_id=1, source_target_pairs={{0,4},{4,8},{8,12},{12,14},{14,10},{10,6},{6,2},{2,0},{1,5},{5,9},... | collective-permute-start | bytes 786440 | tf_op jit(solution)/shard_map/ppermute | solution.py:282
  124.5 3.5 %collective-permute-start.29 = (bf16[384,2048]{1,0:T(8,128)(2,1)S(1)}, bf16[384,2048]{1,0:T(8,128)(2,1)S(1)}, u32[]{:S(2)}, u32[]{:S(2)}) collective-permute-start(bf16[384,2048]{1,0:T(8,128)(2,1)S(1)} %down_grads.2), channel_id=1, source_target_pairs={{0,1},{1,0},{2,3},{3,2},{4,5},{5,4},{6,7},{7,6},{8,9},{9,8},{10,11... | collective-permute-start | bytes 4718600 | tf_op jit(solution)/shard_map/ppermute | solution.py:284
  124.6 12.3 %collective-permute-start.32 = (bf16[2048,384]{1,0:T(8,128)(2,1)S(1)}, bf16[2048,384]{1,0:T(8,128)(2,1)S(1)}, u32[]{:S(2)}, u32[]{:S(2)}) collective-permute-start(bf16[2048,384]{1,0:T(8,128)(2,1)S(1)} %get-tuple-element.179), channel_id=1, source_target_pairs={{0,1},{1,0},{2,3},{3,2},{4,5},{5,4},{6,7},{7,6},{8,9},{9,8},{10,11... | collective-permute-start | bytes 4718600 | tf_op jit(solution)/shard_map/ppermute | solution.py:284
  125.0 11.8 %collective-permute-start.33 = (bf16[2048,384]{1,0:T(8,128)(2,1)S(1)}, bf16[2048,384]{1,0:T(8,128)(2,1)S(1)}, u32[]{:S(2)}, u32[]{:S(2)}) collective-permute-start(bf16[2048,384]{1,0:T(8,128)(2,1)S(1)} %get-tuple-element.180), channel_id=1, source_target_pairs={{0,1},{1,0},{2,3},{3,2},{4,5},{5,4},{6,7},{7,6},{8,9},{9,8},{10,11... | collective-permute-start | bytes 4718600 | tf_op jit(solution)/shard_map/ppermute | solution.py:284
  125.1 8.7 %collective-permute-start.27 = (bf16[128,1024]{1,0:T(8,128)(2,1)S(1)}, bf16[128,1024]{1,0:T(8,128)(2,1)S(1)}, u32[]{:S(2)}, u32[]{:S(2)}) collective-permute-start(bf16[128,1024]{1,0:T(8,128)(2,1)S(1)} %add_convert_fusion.5), channel_id=1, source_target_pairs={{4,0},{8,4},{12,8},{14,12},{10,14},{6,10},{2,6},{0,2},{5,1},{9,5},... | collective-permute-start | bytes 786440 | tf_op jit(solution)/shard_map/ppermute | solution.py:283
  126.3 8.4 %collective-permute-start.28 = (bf16[128,1024]{1,0:T(8,128)(2,1)S(1)}, bf16[128,1024]{1,0:T(8,128)(2,1)S(1)}, u32[]{:S(2)}, u32[]{:S(2)}) collective-permute-start(bf16[128,1024]{1,0:T(8,128)(2,1)S(1)} %add_convert_fusion.4), channel_id=1, source_target_pairs={{0,4},{4,8},{8,12},{12,14},{14,10},{10,6},{6,2},{2,0},{1,5},{5,9},... | collective-permute-start | bytes 786440 | tf_op jit(solution)/shard_map/ppermute | solution.py:282
  134.8 7.6 %collective-permute-start.30 = (bf16[128,1024]{1,0:T(8,128)(2,1)S(1)}, bf16[128,1024]{1,0:T(8,128)(2,1)S(1)}, u32[]{:S(2)}, u32[]{:S(2)}) collective-permute-start(bf16[128,1024]{1,0:T(8,128)(2,1)S(1)} %add_convert_fusion.3), channel_id=1, source_target_pairs={{4,0},{8,4},{12,8},{14,12},{10,14},{6,10},{2,6},{0,2},{5,1},{9,5},... | collective-permute-start | bytes 786440 | tf_op jit(solution)/shard_map/ppermute | solution.py:283
  135.8 7.3 %collective-permute-start.31 = (bf16[128,1024]{1,0:T(8,128)(2,1)S(1)}, bf16[128,1024]{1,0:T(8,128)(2,1)S(1)}, u32[]{:S(2)}, u32[]{:S(2)}) collective-permute-start(bf16[128,1024]{1,0:T(8,128)(2,1)S(1)} %add_convert_fusion.2), channel_id=1, source_target_pairs={{0,4},{4,8},{8,12},{12,14},{14,10},{10,6},{6,2},{2,0},{1,5},{5,9},... | collective-permute-start | bytes 786440 | tf_op jit(solution)/shard_map/ppermute | solution.py:282
